TPU v7x, 32 devices: a whole 2x2x4 slice. The times are simulated.
32 devices in a mesh: var: 4 (over z), dp: 2 (over core), segment: 4 (over y, x).
Axes of the slice: x: 2, y: 2, z: 4, core: 2. Of those that a mesh axis runs over, the one named last changes fastest.
Arguments:
- queries: bfloat16 [2, 4, 4, 256, 1024], P('dp', 'segment', 'var'), parts along dimension 0, may hold values from -22 to 22
- keys: bfloat16 [2, 4, 4, 256, 1024], P('dp', 'segment', 'var'), parts along dimension 0, may hold values from -22 to 22
- values: bfloat16 [2, 4, 4, 256, 1024], P('dp', 'segment', 'var'), parts along dimension 0, may hold values from -6 to 6
- out_grad: bfloat16 [2, 4, 4, 256, 1024], P('dp', 'segment', 'var'), parts along dimension 0, may hold values from -96 to 96
- proj_weight: bfloat16 [4, 2048, 3072], P('segment', 'var'), may hold values from -0.125 to 0.125
- links: int32 [4, 3], replicated, may hold values from -1 to 3, as said below
Outputs:
- passed: bfloat16 [2, 4, 4, 256, 2048], P('dp', 'segment', 'var'), parts along dimension 0
There are 2 independent parts, one for each index of `dp`. A program takes and returns all parts, laid end to end along the dimension named above; an argument that names none is the same for every part. Nothing has to cross between parts.
Inputs may be any that keep to these rules, and one draw needn't show every extreme that they name: `links`: row v lists v itself and some of the 2 variables at cyclic distance 1 to 1 from v (indices modulo 4), each at most once, listed first in order of signed offset, the remaining entries -1; some variable lists all 3.
All inputs are finite; a program needn't handle non-finite values.
Results may differ from a plain program's by a relative error of at most 0.007.
Values may be sent and summed in bfloat16 or wider, within the bound.
No kernel may reach another device: no remote copies, remote signals or barrier semaphores. Data moves between devices by JAX's collectives and lax.ppermute only.
A program may use at most 256 MiB of HBM per device.

v0:
```python
import math

import jax
import jax.numpy as jnp
from jax import lax
from jax.sharding import PartitionSpec as P

HEADS = 16
CAUSAL_BLOCK = 128


neg_big = -1e30


def passed_along(block, axis, distance):
    devices = range(lax.axis_size(axis))
    route = [((i - distance) % len(devices), i) for i in devices]
    return lax.ppermute(block, axis, route)


def block_terms(own_query, own_grad, key_block, value_block, allowed, score_scale):
    scores = (
        jnp.einsum("phe,qhe->hpq", own_query, key_block, preferred_element_type=jnp.float32)
        * score_scale
    )
    scores = jnp.where(allowed[None], scores, neg_big)
    grad_attn = jnp.einsum(
        "phe,qhe->hpq", own_grad, value_block, preferred_element_type=jnp.float32
    )
    return (scores, grad_attn)


def shards(queries, keys, values, out_grad, proj_weight, links):
    patches = queries.shape[3]
    feature_width = queries.shape[4]
    head_size = feature_width // HEADS
    score_scale = 1.0 / math.sqrt(head_size)
    token_shape = (patches, HEADS, head_size)
    own_query = queries.reshape(token_shape)
    own_grad = out_grad.reshape(token_shape)
    own_pair = jnp.stack(
        [keys.reshape(patches, feature_width), values.reshape(patches, feature_width)]
    )
    var_count = lax.axis_size("var")
    reach = min(4, (var_count - 1) // 2)
    own_index = lax.axis_index("var")
    own_links = lax.dynamic_index_in_dim(links, own_index, 0, keepdims=False)
    block_index = jnp.arange(patches, dtype=jnp.int32) // CAUSAL_BLOCK
    causal = block_index[:, None] >= block_index[None, :]
    fetched = [(0, own_pair)]
    for distance in range(1, reach + 1):
        from_below = passed_along(own_pair, "var", distance)
        from_above = passed_along(own_pair, "var", -distance)
        fetched.append((-distance, from_below))
        fetched.append((distance, from_above))
    blocks = []
    for offset, pair_block in fetched:
        linked = jnp.any(own_links == (own_index + offset) % var_count)
        blocks.append(
            (
                offset,
                pair_block[0].reshape(token_shape),
                pair_block[1].reshape(token_shape),
                causal & linked,
            )
        )
    row_max = jnp.full((HEADS, patches), neg_big, jnp.float32)
    row_sum = jnp.zeros((HEADS, patches), jnp.float32)
    weighted = jnp.zeros((HEADS, patches), jnp.float32)
    for offset, key_block, value_block, allowed in blocks:
        scores, grad_attn = block_terms(
            own_query, own_grad, key_block, value_block, allowed, score_scale
        )
        new_max = jnp.maximum(row_max, scores.max(axis=2))
        shrink = jnp.exp(row_max - new_max)
        attention = jnp.exp(scores - new_max[:, :, None])
        row_sum = row_sum * shrink + attention.sum(axis=2)
        weighted = weighted * shrink + (attention * grad_attn).sum(axis=2)
        row_max = new_max
    log_total = row_max + jnp.log(row_sum)
    row_delta = weighted / row_sum
    grad_query = jnp.zeros(token_shape, jnp.float32)
    summed = jnp.zeros((2, patches, feature_width), jnp.float32)
    for offset, key_block, value_block, allowed in blocks:
        scores, grad_attn = block_terms(
            own_query, own_grad, key_block, value_block, allowed, score_scale
        )
        attention = jnp.exp(scores - log_total[:, :, None])
        attention_low = attention.astype(jnp.bfloat16)
        score_grad = (score_scale * attention * (grad_attn - row_delta[:, :, None])).astype(
            jnp.bfloat16
        )
        grad_query = grad_query + jnp.einsum(
            "hpq,qhe->phe", score_grad, key_block, preferred_element_type=jnp.float32
        )
        key_part = jnp.einsum(
            "hpq,phe->qhe", score_grad, own_query, preferred_element_type=jnp.float32
        ).astype(jnp.bfloat16)
        value_part = jnp.einsum(
            "hpq,phe->qhe", attention_low, own_grad, preferred_element_type=jnp.float32
        ).astype(jnp.bfloat16)
        part_pair = jnp.stack(
            [key_part.reshape(patches, feature_width), value_part.reshape(patches, feature_width)]
        )
        if offset == 0:
            arrived = part_pair
        elif offset > 0:
            arrived = passed_along(part_pair, "var", offset)
        else:
            arrived = passed_along(part_pair, "var", offset)
        summed = summed + arrived.astype(jnp.float32)
    grad_kv = summed.astype(jnp.bfloat16)
    grad_qkv = jnp.concatenate(
        [grad_query.astype(jnp.bfloat16).reshape(patches, feature_width), grad_kv[0], grad_kv[1]],
        axis=1,
    )
    input_grad = jnp.einsum(
        "pc,rc->pr",
        grad_qkv,
        lax.all_gather(proj_weight, "var", axis=1, tiled=True)[0],
        preferred_element_type=jnp.float32,
    )
    passed = passed_along(input_grad.astype(jnp.bfloat16), "segment", -1)
    return passed.reshape(1, 1, 1, patches, input_grad.shape[1])


def solution(mesh):
    return jax.shard_map(
        shards,
        mesh=mesh,
        in_specs=(
            P("dp", "segment", "var", None, None),
            P("dp", "segment", "var", None, None),
            P("dp", "segment", "var", None, None),
            P("dp", "segment", "var", None, None),
            P("segment", "var", None),
            P(),
        ),
        out_specs=P("dp", "segment", "var", None, None),
        check_vma=False,
    )
```

profile of v0, /device:TPU:0, one launch (start us, length us, event | category | flops | bytes accessed | tf_op | source)
XLA Modules:
  0.0 348.4 jit_solution(11081777774045563238)
XLA Ops:
  6.5 0.0 all-gather.2.cloned.1.call-start
  6.6 0.7 all-gather.2.cloned.1.call-update
  7.3 2.3 pad_maximum_fusion
  9.5 5.0 %collective-permute-start.1 = (bf16[2,256,1024]{2,1,0:T(8,128)(2,1)}, bf16[2,256,1024]{2,1,0:T(8,128)(2,1)}, u32[]{:S(2)}, u32[]{:S(2)}) collective-permute-start(bf16[2,256,1024]{2,1,0:T(8,128)(2,1)} %pad_maximum_fusion), channel_id=1, source_target_pairs={{8,0},{16,8},{24,16},{0,24},{9,1},{17,9},{25,17},{1,25},{10,2},{18... | collective-permute-start | bytes 3145736 | tf_op jit(solution)/shard_map/ppermute | solution.py:18
  14.6 0.2 copy.38
  14.8 0.2 copy.44
  15.0 0.2 copy.37
  15.2 0.2 copy.43
  15.5 1.4 compare_reduce_fusion
  16.9 2.1 compare_and_fusion.2
  19.0 3.1 fusion.17
  22.0 43.7 %collective-permute-done.1 = bf16[2,256,1024]{2,1,0:T(8,128)(2,1)} collective-permute-done((bf16[2,256,1024]{2,1,0:T(8,128)(2,1)}, bf16[2,256,1024]{2,1,0:T(8,128)(2,1)}, u32[]{:S(2)}, u32[]{:S(2)}) %collective-permute-start.1) | collective-permute-done | bytes 1048608 | tf_op jit(solution)/shard_map/ppermute | solution.py:18
  65.7 2.1 fusion.66
  67.8 0.2 copy.41
  68.0 29.7 %collective-permute-done = bf16[2,256,1024]{2,1,0:T(8,128)(2,1)} collective-permute-done((bf16[2,256,1024]{2,1,0:T(8,128)(2,1)}, bf16[2,256,1024]{2,1,0:T(8,128)(2,1)}, u32[]{:S(2)}, u32[]{:S(2)}) %collective-permute-start) | collective-permute-done | bytes 1048608 | tf_op jit(solution)/shard_map/ppermute | solution.py:18
  97.7 2.3 fusion.65
  100.0 1.2 copy.39
  101.3 2.0 copy.45
  103.3 2.0 copy.46
  105.3 0.8 fusion.19
  106.2 0.8 fusion.18
  107.1 0.5 copy-done
  107.6 3.4 multiply_reduce_fusion
  111.0 3.5 fusion.5
  114.5 3.4 fusion.2
  117.9 7.0 %multiply_convert_fusion = (bf16[16,256,256]{1,2,0:T(8,128)(2,1)S(1)}, bf16[16,256,256]{1,2,0:T(8,128)(2,1)S(1)}, bf16[16,256,256]{1,2,0:T(8,128)(2,1)S(1)}) fusion(f32[16,256,256]{1,2,0:T(8,128)} %get-tuple-element.39, f32[16,256,256]{1,2,0:T(8,128)S(1)} %copy-done, f32[16,256]{1,0:T(8,128)S(1)} %get-tuple-element.22, f32[16,256]{1,0:T(8,128)S(1)} %get-tuple-element.23, ...), kind=kLoop, calls=%fused_computation.16 | loop fusion | flops 22020096 | bytes 31686656 | tf_op jit(solution)/shard_map/convert_element_type | solution.py:90
  124.9 0.8 convolution_convert_fusion.1
  125.7 1.1 fusion.49
  126.8 0.1 pad_maximum_fusion.1
  126.9 6.6 %collective-permute-start.2 = (bf16[2,256,1024]{1,2,0:T(8,128)(2,1)S(1)}, bf16[2,256,1024]{1,2,0:T(8,128)(2,1)S(1)}, u32[]{:S(2)}, u32[]{:S(2)}) collective-permute-start(bf16[2,256,1024]{1,2,0:T(8,128)(2,1)S(1)} %pad_maximum_fusion.1), channel_id=1, source_target_pairs={{8,0},{16,8},{24,16},{0,24},{9,1},{17,9},{25,17},{1,25},{10,2},{18... | collective-permute-start | bytes 3145736 | tf_op jit(solution)/shard_map/ppermute | solution.py:18
  133.5 0.8 convolution_convert_fusion
  134.3 1.1 fusion.52
  135.3 0.1 pad_maximum_fusion.2
  135.4 2.6 collective-permute-start.3
  138.1 0.5 convolution_bitcast_fusion.1
  138.5 0.5 convolution_bitcast_fusion
  139.0 0.8 convolution_convert_fusion.2
  139.8 0.5 fusion.45
  140.3 1.1 fusion.46
  141.3 84.0 %collective-permute-done.2 = bf16[2,256,1024]{1,2,0:T(8,128)(2,1)S(1)} collective-permute-done((bf16[2,256,1024]{1,2,0:T(8,128)(2,1)S(1)}, bf16[2,256,1024]{1,2,0:T(8,128)(2,1)S(1)}, u32[]{:S(2)}, u32[]{:S(2)}) %collective-permute-start.2) | collective-permute-done | bytes 1048608 | tf_op jit(solution)/shard_map/ppermute | solution.py:18
  225.3 1.7 collective-permute-done.3
  227.0 0.4 add_convert_fusion
  227.5 0.1 slice_bitcast_fusion.1
  227.5 79.9 %all-gather.2.cloned.1.call-done = bf16[1,2048,3072]{2,1,0:T(8,128)(2,1)} async-done(((bf16[1,512,3072]{2,1,0:T(8,128)(2,1)}), bf16[1,2048,3072]{2,1,0:T(8,128)(2,1)}) %all-gather.2.cloned.1.call-update) | async-done | bytes 12582928 | tf_op jit(solution)/shard_map/all_gather | solution.py:120
  307.4 8.0 %fusion.14 = bf16[256,2048]{1,0:T(8,128)(2,1)S(1)} fusion(bf16[1,2048,3072]{2,1,0:T(8,128)(2,1)} %all-gather.2.cloned.1.call-done, bf16[256,1024]{0,1:T(8,128)(2,1)S(1)} %get-tuple-element.17, bf16[256,1024]{0,1:T(8,128)(2,1)S(1)} %get-tuple-element.16, bf16[256,1024]{0,1:T(8,128)(2,1)S(1)} %bitcast.153), kind=kOutput, calls=%fused_computation.29 | convolution fusion | flops 3226468352 | bytes 15204352 | tf_op jit(solution)/shard_map/pc,rc->pr/dot_general | solution.py:117
  315.5 2.5 collective-permute-start.4
  318.0 22.6 %collective-permute-done.4 = bf16[256,2048]{1,0:T(8,128)(2,1)S(1)} collective-permute-done((bf16[256,2048]{1,0:T(8,128)(2,1)S(1)}, bf16[256,2048]{1,0:T(8,128)(2,1)S(1)}, u32[]{:S(2)}, u32[]{:S(2)}) %collective-permute-start.4) | collective-permute-done | bytes 1048608 | tf_op jit(solution)/shard_map/ppermute | solution.py:18
  340.6 1.0 copy.66
  (17 shorter events, 0.1 us)
Async XLA Ops:
  6.5 8.1 %copy-start.3 = (bf16[1,1,1,256,1024]{4,3,2,1,0:T(8,128)(2,1)S(1)}, bf16[1,1,1,256,1024]{4,3,2,1,0:T(8,128)(2,1)}, u32[]{:S(2)}) copy-start(bf16[1,1,1,256,1024]{4,3,2,1,0:T(8,128)(2,1)} %param.7) | copy-start | bytes 1572868
  6.5 8.3 %copy-start.4 = (bf16[1,1,1,256,1024]{4,3,2,1,0:T(8,128)(2,1)S(1)}, bf16[1,1,1,256,1024]{4,3,2,1,0:T(8,128)(2,1)}, u32[]{:S(2)}) copy-start(bf16[1,1,1,256,1024]{4,3,2,1,0:T(8,128)(2,1)} %param.8) | copy-start | bytes 1572868
  6.5 8.5 %copy-start.5 = (bf16[1,1,1,256,1024]{4,3,2,1,0:T(8,128)(2,1)S(1)}, bf16[1,1,1,256,1024]{4,3,2,1,0:T(8,128)(2,1)}, u32[]{:S(2)}) copy-start(bf16[1,1,1,256,1024]{4,3,2,1,0:T(8,128)(2,1)} %param.6) | copy-start | bytes 1572868
  6.5 8.7 %copy-start.6 = (bf16[1,1,1,256,1024]{4,3,2,1,0:T(8,128)(2,1)S(1)}, bf16[1,1,1,256,1024]{4,3,2,1,0:T(8,128)(2,1)}, u32[]{:S(2)}) copy-start(bf16[1,1,1,256,1024]{4,3,2,1,0:T(8,128)(2,1)} %param.9) | copy-start | bytes 1572868
  6.5 300.9 %all-gather.2.cloned.1.call-start = ((), (), s32[]{:S(2)}) async-start(), calls=%async_computation | async-start | bytes 15728640 | tf_op jit(solution)/shard_map/all_gather | solution.py:120
  9.5 56.2 %collective-permute-start.1 = (bf16[2,256,1024]{2,1,0:T(8,128)(2,1)}, bf16[2,256,1024]{2,1,0:T(8,128)(2,1)}, u32[]{:S(2)}, u32[]{:S(2)}) collective-permute-start(bf16[2,256,1024]{2,1,0:T(8,128)(2,1)} %pad_maximum_fusion), channel_id=1, source_target_pairs={{8,0},{16,8},{24,16},{0,24},{9,1},{17,9},{25,17},{1,25},{10,2},{18... | collective-permute-start | bytes 3145736 | tf_op jit(solution)/shard_map/ppermute | solution.py:18
  14.6 83.2 %collective-permute-start = (bf16[2,256,1024]{2,1,0:T(8,128)(2,1)}, bf16[2,256,1024]{2,1,0:T(8,128)(2,1)}, u32[]{:S(2)}, u32[]{:S(2)}) collective-permute-start(bf16[2,256,1024]{2,1,0:T(8,128)(2,1)} %pad_maximum_fusion), channel_id=1, source_target_pairs={{24,0},{0,8},{8,16},{16,24},{25,1},{1,9},{9,17},{17,25},{26,2},{2,... | collective-permute-start | bytes 3145736 | tf_op jit(solution)/shard_map/ppermute | solution.py:18
  105.3 2.2 copy-start
  107.6 3.5 copy-start.2
  111.0 3.5 copy-start.1
  126.9 98.5 %collective-permute-start.2 = (bf16[2,256,1024]{1,2,0:T(8,128)(2,1)S(1)}, bf16[2,256,1024]{1,2,0:T(8,128)(2,1)S(1)}, u32[]{:S(2)}, u32[]{:S(2)}) collective-permute-start(bf16[2,256,1024]{1,2,0:T(8,128)(2,1)S(1)} %pad_maximum_fusion.1), channel_id=1, source_target_pairs={{8,0},{16,8},{24,16},{0,24},{9,1},{17,9},{25,17},{1,25},{10,2},{18... | collective-permute-start | bytes 3145736 | tf_op jit(solution)/shard_map/ppermute | solution.py:18
  135.4 91.6 %collective-permute-start.3 = (bf16[2,256,1024]{1,2,0:T(8,128)(2,1)S(1)}, bf16[2,256,1024]{1,2,0:T(8,128)(2,1)S(1)}, u32[]{:S(2)}, u32[]{:S(2)}) collective-permute-start(bf16[2,256,1024]{1,2,0:T(8,128)(2,1)S(1)} %pad_maximum_fusion.2), channel_id=1, source_target_pairs={{24,0},{0,8},{8,16},{16,24},{25,1},{1,9},{9,17},{17,25},{26,2},{2,... | collective-permute-start | bytes 3145736 | tf_op jit(solution)/shard_map/ppermute | solution.py:18
  315.5 25.1 %collective-permute-start.4 = (bf16[256,2048]{1,0:T(8,128)(2,1)S(1)}, bf16[256,2048]{1,0:T(8,128)(2,1)S(1)}, u32[]{:S(2)}, u32[]{:S(2)}) collective-permute-start(bf16[256,2048]{1,0:T(8,128)(2,1)S(1)} %fusion.14), channel_id=1, source_target_pairs={{1,0},{2,1},{3,2},{0,3},{5,4},{6,5},{7,6},{4,7},{9,8},{10,9},{11,1... | collective-permute-start | bytes 3145736 | tf_op jit(solution)/shard_map/ppermute | solution.py:18
Sparse Core Ops, SparseCore 0:
  8.9 298.4 all-gather.1
where the time goes:
time: 349 us; the launch traced here: 348 us
  waiting for transfers between devices  262 us (75%)
  matrix products  30 us (9%)
  starting transfers between devices  16.8 us (5%)
  between operations  13.6 us (4%)
  other arithmetic  13.4 us (4%)
  local copies, waits for them, and re-layouts  12.2 us (3%)
    ppermute x5, waiting for transfers between devices, passed_along(): return lax.ppermute(block, axis, route)  182 us
    all_gather x1, waiting for transfers between devices, shards(): lax.all_gather(proj_weight, 'var', axis=1, tiled=True)[0]  79.9 us
    ppermute x5, starting transfers between devices, passed_along(): return lax.ppermute(block, axis, route)  16.8 us
    dot_general x3, matrix products, block_terms(): jnp.einsum('phe,qhe->hpq', own_grad, value_block, preferred_element_type=...  10.3 us
    slice x4, local copies, waits for them, and re-layouts, shards(): pair_block[1].reshape(token_shape)  8.4 us
    dot_general x1, matrix products, shards(): jnp.einsum('pc,rc->pr', grad_qkv, lax.all_gather(proj_weight, 'var', axis...  8.05 us
    convert_element_type x1, other arithmetic, shards(): (score_scale * attention * (grad_attn - row_delta[:, :, None])).astype(jn...  7.01 us
  transfers between devices with their start and end apart: 6, of which 6 were waited for; matrix products, arithmetic and copies ran while one was open for 13% of the time, Pallas kernels for 0%

commit v1 on v0

v1 whole, which is shorter than its diff:
```python
import functools
import math

import jax
import jax.numpy as jnp
from jax import lax
from jax.experimental import pallas as pl
from jax.experimental.pallas import tpu as pltpu
from jax.sharding import PartitionSpec as P

HEADS = 16
CAUSAL_BLOCK = 128
GROUP = 4

neg_big = -1e30
f32 = jnp.float32
bf16 = jnp.bfloat16


def passed_along(block, axis, distance):
    devices = range(lax.axis_size(axis))
    route = [((i - distance) % len(devices), i) for i in devices]
    return lax.ppermute(block, axis, route)


def after(block, *earlier):
    return lax.optimization_barrier((block,) + earlier)[0]


def dot_nt(a, b):
    return lax.dot_general(a, b, (((1,), (1,)), ((), ())), preferred_element_type=f32)


def dot_nn(a, b):
    return lax.dot_general(a, b, (((1,), (0,)), ((), ())), preferred_element_type=f32)


def own_half(block, half, head_size):
    lane = lax.broadcasted_iota(jnp.int32, block.shape, 1)
    keep = (lane < head_size) if half == 0 else (lane >= head_size)
    return jnp.where(keep, block, jnp.zeros_like(block))


def block_products(key_half, value_half, query, grad, blocks):
    out = []
    for j in range(blocks):
        rows = slice(j * CAUSAL_BLOCK, (j + 1) * CAUSAL_BLOCK)
        start = j * CAUSAL_BLOCK
        out.append(
            (dot_nt(key_half[rows], query[start:]), dot_nt(value_half[rows], grad[start:]))
        )
    return out


def stats_kernel(sources, head_size, scale, linked_ref, k_ref, v_ref, *refs):
    ins, outs = refs[: 2 * sources], refs[2 * sources :]
    patches = k_ref.shape[0]
    blocks = patches // CAUSAL_BLOCK
    factor = scale * math.log2(math.e)
    for s in range(sources):
        linked = linked_ref[s] != 0
        lams, deltas = [], []
        for h in range(GROUP):
            cols = slice((h // 2) * 2 * head_size, (h // 2 + 1) * 2 * head_size)
            key_half = own_half(k_ref[:, cols], h % 2, head_size)
            value_half = own_half(v_ref[:, cols], h % 2, head_size)
            parts = block_products(
                key_half, value_half, ins[2 * s][:, cols], ins[2 * s + 1][:, cols], blocks
            )
            lam_row, delta_row = [], []
            for i in range(blocks):
                pieces = []
                for j in range(i + 1):
                    at = slice((i - j) * CAUSAL_BLOCK, (i - j + 1) * CAUSAL_BLOCK)
                    pieces.append((parts[j][0][:, at], parts[j][1][:, at]))
                top = functools.reduce(
                    jnp.maximum, [jnp.max(p[0], axis=0, keepdims=True) for p in pieces]
                )
                total = 0.0
                weighted = 0.0
                for score, grad_attn in pieces:
                    e = jnp.exp2((score - top) * factor)
                    total = total + jnp.sum(e, axis=0, keepdims=True)
                    weighted = weighted + jnp.sum(e * grad_attn, axis=0, keepdims=True)
                lam_row.append(top + jnp.log(total) * (1.0 / scale))
                delta_row.append(weighted / total)
            lams.append(jnp.concatenate(lam_row, axis=1))
            deltas.append(jnp.concatenate(delta_row, axis=1))
        lam = jnp.where(linked, jnp.concatenate(lams, axis=0), neg_big)
        delta = jnp.where(linked, jnp.concatenate(deltas, axis=0), 0.0)
        outs[s][0] = jnp.concatenate([lam, delta], axis=0)


def grads_kernel(sources, window, head_size, scale, linked_ref, k_ref, v_ref, *refs):
    ins = refs[: 2 * sources]
    stats = refs[2 * sources : 2 * sources + sources * window]
    outs = refs[2 * sources + sources * window :]
    own_out, part_outs, kv_out = outs[0], outs[1:sources], outs[sources]
    patches = k_ref.shape[0]
    blocks = patches // CAUSAL_BLOCK
    factor = scale * math.log2(math.e)
    key_t = jnp.transpose(k_ref[...].astype(f32)).astype(bf16)
    totals = []
    for s in range(sources):
        lams = [r[0, :GROUP] for r in stats[s * window : (s + 1) * window]]
        deltas = [r[0, GROUP:] for r in stats[s * window : (s + 1) * window]]
        top = functools.reduce(jnp.maximum, lams)
        weights = [jnp.exp2((lam - top) * factor) for lam in lams]
        total = functools.reduce(jnp.add, weights)
        delta = functools.reduce(jnp.add, [w * d for w, d in zip(weights, deltas)]) / total
        lam = top + jnp.log(total) * (1.0 / scale)
        lam = jnp.where(linked_ref[s] != 0, lam, -neg_big)
        totals.append((lam, delta))
    for pair in range(GROUP // 2):
        cols = slice(pair * 2 * head_size, (pair + 1) * 2 * head_size)
        halves = [
            (
                own_half(k_ref[:, cols], half, head_size),
                own_half(v_ref[:, cols], half, head_size),
            )
            for half in range(2)
        ]
        key_sum = jnp.zeros((patches, 2 * head_size), f32)
        value_sum = jnp.zeros((patches, 2 * head_size), f32)
        for s in range(sources):
            query, grad = ins[2 * s][:, cols], ins[2 * s + 1][:, cols]
            query_t = []
            for half in range(2):
                h = 2 * pair + half
                lam = totals[s][0][h : h + 1]
                delta = totals[s][1][h : h + 1]
                parts = block_products(*halves[half], query, grad, blocks)
                attn_rows, score_rows = [], []
                for j in range(blocks):
                    start = j * CAUSAL_BLOCK
                    attn = jnp.exp2((parts[j][0] - lam[:, start:]) * factor)
                    score_grad = (attn * (parts[j][1] - delta[:, start:])).astype(bf16)
                    attn = attn.astype(bf16)
                    if start:
                        pad = jnp.zeros((CAUSAL_BLOCK, start), bf16)
                        attn = jnp.concatenate([pad, attn], axis=1)
                        score_grad = jnp.concatenate([pad, score_grad], axis=1)
                    attn_rows.append(attn)
                    score_rows.append(score_grad)
                attn = jnp.concatenate(attn_rows, axis=0)
                score_grad = jnp.concatenate(score_rows, axis=0)
                key_sum = key_sum + dot_nn(score_grad, own_half(query, half, head_size))
                value_sum = value_sum + dot_nn(attn, own_half(grad, half, head_size))
                query_t.append(dot_nn(key_t[h * head_size : (h + 1) * head_size], score_grad))
            part = jnp.transpose(jnp.concatenate(query_t, axis=0)) * scale
            if s == 0:
                own_out[:, cols] = part
            else:
                part_outs[s - 1][:, cols] = part.astype(bf16)
        kv_out[0, :, cols] = (key_sum * scale).astype(bf16)
        kv_out[1, :, cols] = value_sum.astype(bf16)


def specs(patches, width):
    token = pl.BlockSpec((patches, width), lambda g: (0, g))
    stat = pl.BlockSpec((1, 2 * GROUP, patches), lambda g: (g, 0, 0))
    flag = pl.BlockSpec(memory_space=pltpu.SMEM)
    return token, stat, flag


def block_stats(linked, keys, values, pairs, head_size, scale):
    patches, features = keys.shape
    token, stat, flag = specs(patches, GROUP * head_size)
    groups = HEADS // GROUP
    n = len(pairs)
    return pl.pallas_call(
        functools.partial(stats_kernel, n, head_size, scale),
        grid=(groups,),
        in_specs=[flag] + [token] * (2 + 2 * n),
        out_specs=[stat] * n,
        out_shape=[jax.ShapeDtypeStruct((groups, 2 * GROUP, patches), f32)] * n,
        compiler_params=pltpu.CompilerParams(vmem_limit_bytes=48 * 2**20),
        cost_estimate=pl.CostEstimate(
            flops=8 * n * patches * patches * features,
            bytes_accessed=4 * (n + 1) * patches * features,
            transcendentals=n * HEADS * patches * patches,
        ),
        name="row_stats",
    )(linked, keys, values, *[x for pair in pairs for x in pair])


def block_grads(linked, keys, values, pairs, stats, head_size, scale):
    patches, features = keys.shape
    token, stat, flag = specs(patches, GROUP * head_size)
    groups = HEADS // GROUP
    n = len(pairs)
    window = len(stats[0])
    both = pl.BlockSpec((2, patches, GROUP * head_size), lambda g: (0, 0, g))
    shape = jax.ShapeDtypeStruct
    return pl.pallas_call(
        functools.partial(grads_kernel, n, window, head_size, scale),
        grid=(groups,),
        in_specs=[flag] + [token] * (2 + 2 * n) + [stat] * (n * window),
        out_specs=[token] * n + [both],
        out_shape=[shape((patches, features), f32)]
        + [shape((patches, features), bf16)] * (n - 1)
        + [shape((2, patches, features), bf16)],
        compiler_params=pltpu.CompilerParams(vmem_limit_bytes=48 * 2**20),
        cost_estimate=pl.CostEstimate(
            flops=20 * n * patches * patches * features,
            bytes_accessed=8 * (n + 1) * patches * features,
            transcendentals=n * HEADS * patches * patches,
        ),
        name="block_grads",
    )(
        linked,
        keys,
        values,
        *[x for pair in pairs for x in pair],
        *[x for group in stats for x in group],
    )


def place_kernel(at_ref, *refs):
    out_ref = refs[-1]
    for i, ref in enumerate(refs[:-1]):
        width = ref.shape[1]
        col = pl.multiple_of(at_ref[i] * width, width)
        out_ref[pl.ds(0, ref.shape[0]), pl.ds(col, width)] = ref[...]


def times(tokens, rows):
    return dot_nt(tokens, rows).astype(bf16)


def swapped(block):
    return lax.ppermute(block, "dp", [(0, 1), (1, 0)])


def handed_on(result, patches, segments, outer=None):
    axes = ("dp", "segment") if outer is None else ("var", "dp", "segment")
    out = []
    for cross in range(2):
        route = []
        for src, dst in outer or [(0, 0)]:
            for d in range(2):
                for s in range(segments):
                    route.append(
                        (
                            (src * 2 + d) * segments + s,
                            (dst * 2 + (d + cross) % 2) * segments + (s - 1) % segments,
                        )
                    )
        out.append(
            lax.ppermute(result[cross * patches : (cross + 1) * patches], axes, route)
        )
    return out


def attention_grads(queries, keys, values, out_grad, links, reach, first, second, third):
    patches, feature_width = queries.shape
    head_size = feature_width // HEADS
    scale = 1.0 / math.sqrt(head_size)
    n = lax.axis_size("var")
    own = lax.axis_index("var")
    offsets = [0] + [o for d in range(1, reach + 1) for o in (d, -d)]
    pairs = [(queries, out_grad)]
    for o in offsets[1:]:
        pairs.append((passed_along(queries, "var", -o), passed_along(out_grad, "var", -o)))
    sources = (own + jnp.array(offsets, jnp.int32)) % n
    linked = jnp.any(links[sources] == own, axis=1).astype(jnp.int32)
    own_stats = block_stats(linked[:1], keys, values, pairs[:1], head_size, scale)
    first(own_stats[0])
    other_stats = block_stats(linked[1:], keys, values, pairs[1:], head_size, scale)
    stats = dict(zip(offsets, list(own_stats) + list(other_stats)))
    needed = {}
    for d in offsets:
        for e in offsets:
            entries = needed.setdefault((d + e) % n, [])
            if -e not in entries:
                entries.append(-e)
    arrived = {}
    for t, entries in needed.items():
        if t == 0:
            arrived[t] = {o: stats[o] for o in entries}
            continue
        entries.sort()
        message = jnp.stack([stats[o] for o in entries])
        message = passed_along(message, "var", -t)
        arrived[t] = {o: message[i] for i, o in enumerate(entries)}
    second(other_stats[0])
    windows = [[arrived[(d + e) % n][-e] for e in offsets] for d in offsets]
    grads = block_grads(linked, keys, values, pairs, windows, head_size, scale)
    third(grads[-1])
    query_grad = grads[0]
    for o, part in zip(offsets[1:], grads[1:-1]):
        query_grad = query_grad + passed_along(part, "var", o).astype(f32)
    return query_grad.astype(bf16), grads[-1]


def shards(queries, keys, values, out_grad, proj_weight, links):
    patches, feature_width = queries.shape[3:]
    n = lax.axis_size("var")
    segments = lax.axis_size("segment")
    reach = min(4, (n - 1) // 2)
    flat = [x.reshape(patches, feature_width) for x in (queries, keys, values, out_grad)]
    weight = proj_weight[0]
    if n != 4:
        nothing = lambda value: None
        query_grad, pair = attention_grads(*flat, links, reach, nothing, nothing, nothing)
        grad_qkv = jnp.concatenate([query_grad, pair[0], pair[1]], axis=1)
        whole = lax.all_gather(weight, "var", axis=0, tiled=True)
        passed = passed_along(times(grad_qkv, whole), "segment", -1)
        return passed.reshape(1, 1, 1, patches, whole.shape[0])

    own = lax.axis_index("var")
    core = lax.axis_index("dp")
    half = weight.shape[0] // 2
    cuts = [(0, half // 4), (half // 4, half * 5 // 8), (half * 5 // 8, half)]
    below, above = [], []

    def near(i):
        def start(value):
            lo, hi = cuts[i]
            piece = lax.dynamic_slice_in_dim(weight, core * half + lo, hi - lo, 0)
            piece = after(piece, value)
            below.append(lax.ppermute(piece, "var", [(0, 1), (1, 2), (2, 3)]))
            above.append(lax.ppermute(piece, "var", [(1, 0), (2, 1), (3, 2)]))

        return start

    query_grad, pair = attention_grads(*flat, links, reach, near(0), near(1), near(2))
    far = []
    for up, down in zip(below, above):
        up = lax.ppermute(after(up, pair), "var", [(1, 2), (2, 3)])
        down = lax.ppermute(after(down, pair), "var", [(1, 0), (2, 1)])
        far.append(jnp.where(own < 2, down, up))
    inward = [(0, 1), (3, 2)]
    outer_pair = lax.ppermute(pair, "var", inward)
    outer_query = lax.ppermute(query_grad, "var", inward)

    def tokens(query_part, pair_part):
        other_pair, other_query = swapped(pair_part), swapped(query_part)
        return jnp.concatenate(
            [
                jnp.concatenate([query_part, pair_part[0], pair_part[1]], axis=1),
                jnp.concatenate([other_query, other_pair[0], other_pair[1]], axis=1),
            ],
            axis=0,
        )

    own_tokens = tokens(query_grad, pair)
    outer_tokens = tokens(outer_query, outer_pair)
    own_rows = lax.dynamic_slice_in_dim(weight, core * half, half, 0)
    near_rows = jnp.concatenate([own_rows] + above + below, axis=0)
    handed = handed_on(times(own_tokens, near_rows), patches, segments)
    far_rows = jnp.concatenate(far, axis=0)
    handed_far = handed_on(times(own_tokens, far_rows), patches, segments)
    handed_end = handed_on(
        times(outer_tokens, far_rows), patches, segments, outer=[(1, 0), (2, 3)]
    )
    pieces, places = [], []
    for cross in range(2):
        side = (core + cross) % 2
        by_step = [handed[cross][:, i * half : (i + 1) * half] for i in range(3)]
        end = handed_end[cross]
        by_step = [
            by_step[0],
            jnp.where(own == 3, end, by_step[1]),
            handed_far[cross],
            jnp.where(own == 0, end, by_step[2]),
        ]
        for step, piece in enumerate(by_step):
            pieces.append(piece)
            places.append((own + step) % 4 * 2 + side)
    passed = pl.pallas_call(
        place_kernel,
        in_specs=[pl.BlockSpec(memory_space=pltpu.SMEM)]
        + [pl.BlockSpec(memory_space=pltpu.VMEM)] * 8,
        out_specs=pl.BlockSpec(memory_space=pltpu.VMEM),
        out_shape=jax.ShapeDtypeStruct((patches, 8 * half), bf16),
        name="placed",
    )(jnp.stack(places).astype(jnp.int32), *pieces)
    return passed.reshape(1, 1, 1, patches, 8 * half)


def solution(mesh):
    return jax.shard_map(
        shards,
        mesh=mesh,
        in_specs=(
            P("dp", "segment", "var", None, None),
            P("dp", "segment", "var", None, None),
            P("dp", "segment", "var", None, None),
            P("dp", "segment", "var", None, None),
            P("segment", "var", None),
            P(),
        ),
        out_specs=P("dp", "segment", "var", None, None),
        check_vma=False,
    )
```

time: 349 us -> 203 us (0.58)
  waiting for transfers between devices: 262 us -> 95.4 us
  starting transfers between devices: 16.8 us -> 56.9 us
  matrix products: 30 us -> 4.7 us
  Pallas kernels: 0 us -> 24.5 us
  between operations: 13.6 us -> 0.49 us
  other arithmetic: 13.4 us -> 2.79 us
  local copies, waits for them, and re-layouts: 12.2 us -> 16.8 us
    ppermute x5 -> x9, waiting for transfers between devices: 182 us -> 62.3 us  [passed_along(): return lax.ppermute(block, axis, route)]
    all_gather x1 -> x0, waiting for transfers between devices: 79.9 us -> none  [shards(): lax.all_gather(proj_weight, 'var', axis=1, tiled=True)[0]]
    ppermute x0 -> x24, starting transfers between devices: none -> 39.1 us  [the longest x3 16.3 us: start(): below.append(lax.ppermute(piece, 'var', [(0, 1), (1, 2), (2, 3)]))]
    ppermute x0 -> x24, waiting for transfers between devices: none -> 33 us  [the longest x1 14.2 us: shards(): outer_pair = lax.ppermute(pair, 'var', inward)]
    dot_general x16 -> x3, matrix products: 30 us -> 4.7 us  [dot_nt(): lax.dot_general(a, b, (((1,), (1,)), ((), ())), preferred_element_type=f32)]
    pallas_call x0 -> x4, Pallas kernels: none -> 24.5 us  [the longest x1 14.8 us: block_grads(): pl.pallas_call(functools.partial(grads_kernel, n, window, head_size, scal...]
    slice x6 -> x4, local copies, waits for them, and re-layouts: 9.84 us -> 0.16 us  [the longest x3 0.09 us: handed_on(): result[cross * patches:(cross + 1) * patches]]
    unnamed x19 -> x40, local copies, waits for them, and re-layouts: 2.31 us -> 9.8 us
  transfers between devices with their start and end apart: 6 -> 33, of which waited for: 6 -> 14; matrix products, arithmetic and copies ran while one was open for 13% -> 10% of each run, Pallas kernels for 0% -> 11%
where the time goes in v1:
time: 203 us; the launch traced here: 202 us
  waiting for transfers between devices  95.4 us (47%)
  starting transfers between devices  56.9 us (28%)
  Pallas kernels  24.5 us (12%)
  local copies, waits for them, and re-layouts  16.8 us (8%)
  matrix products  4.7 us (2%)
  other arithmetic  2.79 us (1%)
    ppermute x9, waiting for transfers between devices, passed_along(): return lax.ppermute(block, axis, route)  62.3 us
    ppermute x9, starting transfers between devices, passed_along(): return lax.ppermute(block, axis, route)  17.8 us
    ppermute x3, starting transfers between devices, start(): below.append(lax.ppermute(piece, 'var', [(0, 1), (1, 2), (2, 3)]))  16.3 us
    pallas_call x1, Pallas kernels, block_grads(): pl.pallas_call(functools.partial(grads_kernel, n, window, head_size, scal...  14.8 us
    ppermute x1, waiting for transfers between devices, shards(): outer_pair = lax.ppermute(pair, 'var', inward)  14.2 us
    ppermute x6, waiting for transfers between devices, handed_on(): lax.ppermute(result[cross * patches:(cross + 1) * patches], axes, route)  9.83 us
    unnamed x40, local copies, waits for them, and re-layouts  9.8 us
    ppermute x6, starting transfers between devices, handed_on(): lax.ppermute(result[cross * patches:(cross + 1) * patches], axes, route)  7.85 us
  transfers between devices with their start and end apart: 33, of which 14 were waited for; matrix products, arithmetic and copies ran while one was open for 10% of the time, Pallas kernels for 11%

profile of v1, /device:TPU:0, one launch (start us, length us, event | category | flops | bytes accessed | tf_op | source)
XLA Modules:
  0.0 201.6 jit_solution(7296469018744410630)
XLA Ops:
  0.0 5.0 %collective-permute-start = (bf16[256,1024]{1,0:T(8,128)(2,1)}, bf16[256,1024]{1,0:T(8,128)(2,1)S(1)}, u32[]{:S(2)}, u32[]{:S(2)}) collective-permute-start(bf16[256,1024]{1,0:T(8,128)(2,1)} %bitcast.60), channel_id=1, source_target_pairs={{8,0},{16,8},{24,16},{0,24},{9,1},{17,9},{25,17},{1,25},{10,2},{18... | collective-permute-start | bytes 1572872 | tf_op jit(solution)/shard_map/ppermute | solution.py:23
  5.1 3.8 %collective-permute-start.1 = (bf16[256,1024]{1,0:T(8,128)(2,1)}, bf16[256,1024]{1,0:T(8,128)(2,1)}, u32[]{:S(2)}, u32[]{:S(2)}) collective-permute-start(bf16[256,1024]{1,0:T(8,128)(2,1)} %bitcast.64), channel_id=1, source_target_pairs={{8,0},{16,8},{24,16},{0,24},{9,1},{17,9},{25,17},{1,25},{10,2},{18... | collective-permute-start | bytes 1572872 | tf_op jit(solution)/shard_map/ppermute | solution.py:23
  10.1 1.8 dynamic-slice_bitcast_fusion.2
  12.1 1.0 copy-done.1
  13.1 1.0 copy-done.3
  14.1 1.0 copy-done.5
  15.2 1.0 copy-done.7
  16.2 2.5 %row_stats.2.refs_6_ = f32[4,8,256]{2,1,0:T(8,128)S(1)} custom-call(s32[1]{0:T(128)S(1)} %bitcast.71, bf16[256,1024]{1,0:T(8,128)(2,1)S(1)} %bitcast.54, bf16[256,1024]{1,0:T(8,128)(2,1)S(1)} %bitcast.57, bf16[256,1024]{1,0:T(8,128)(2,1)S(1)} %bitcast.62, bf16[256,1024]{1,0:T(8,128)(2,1)S(1)} %bitcast.66), custom_call_target="tpu_custom_call" | custom-call | flops 536870912 | bytes 2097152 | tf_op jit(solution)/shard_map/row_stats/pallas_call | solution.py:171
  18.8 1.3 collective-permute-start.11
  20.1 2.8 %bitcast_dynamic-update-slice_fusion = bf16[768,3072]{1,0:T(8,128)(2,1)} fusion(bf16[1,512,3072]{2,1,0:T(8,128)(2,1)} %param.11, s32[]{:T(128)S(6)} %select_n.104), kind=kLoop, calls=%fused_computation.15 | loop fusion | bytes 3145732
  22.9 7.9 %collective-permute-start.14 = (bf16[64,3072]{1,0:T(8,128)(2,1)}, bf16[64,3072]{1,0:T(8,128)(2,1)}, u32[]{:S(2)}, u32[]{:S(2)}) collective-permute-start(bf16[64,3072]{1,0:T(8,128)(2,1)} %dynamic-slice_bitcast_fusion.2), channel_id=1, source_target_pairs={{0,8},{8,16},{16,24},{1,9},{9,17},{17,25},{2,10},{10,18},{18,26},{... | collective-permute-start | bytes 1179656 | tf_op jit(solution)/shard_map/ppermute | solution.py:322
  30.9 9.3 %collective-permute-done.1.refs_1_.refs_3_ = bf16[256,1024]{1,0:T(8,128)(2,1)} collective-permute-done((bf16[256,1024]{1,0:T(8,128)(2,1)}, bf16[256,1024]{1,0:T(8,128)(2,1)}, u32[]{:S(2)}, u32[]{:S(2)}) %collective-permute-start.1) | collective-permute-done | bytes 524320 | tf_op jit(solution)/shard_map/ppermute | solution.py:23
  40.2 12.2 %collective-permute-done.3.refs_3_.refs_5_ = bf16[256,1024]{1,0:T(8,128)(2,1)} collective-permute-done((bf16[256,1024]{1,0:T(8,128)(2,1)}, bf16[256,1024]{1,0:T(8,128)(2,1)}, u32[]{:S(2)}, u32[]{:S(2)}) %collective-permute-start.3) | collective-permute-done | bytes 524320 | tf_op jit(solution)/shard_map/ppermute | solution.py:23
  52.4 4.8 %row_stats.3 = (f32[4,8,256]{2,1,0:T(8,128)S(1)}, f32[4,8,256]{2,1,0:T(8,128)S(1)}) custom-call(s32[2]{0:T(128)S(1)} %slice.85.linked_ref, bf16[256,1024]{1,0:T(8,128)(2,1)S(1)} %bitcast.55, bf16[256,1024]{1,0:T(8,128)(2,1)S(1)} %bitcast.58, bf16[256,1024]{1,0:T(8,128)(2,1)S(1)} %collective-permute-done.refs_0_.refs_2_, ...), custom_call_target="tpu_custom_call" | custom-call | flops 1073741824 | bytes 3145728 | tf_op jit(solution)/shard_map/row_stats/pallas_call | solution.py:171
  57.2 1.0 collective-permute-start.6
  58.3 2.3 %dynamic-slice_bitcast_fusion = (bf16[96,3072]{1,0:T(8,128)(2,1)}, bf16[96,3072]{1,0:T(8,128)(2,1)}) fusion(bf16[1,512,3072]{2,1,0:T(8,128)(2,1)} %param.11, s32[]{:T(128)S(6)} %select_n.106, s32[]{:T(128)S(6)} %select_n.105), kind=kLoop, calls=%fused_computation.20 | loop fusion | bytes 2359304 | tf_op jit(solution)/shard_map/dynamic_slice | solution.py:320
  61.2 1.6 collective-permute-start.5
  62.8 2.3 %collective-permute-start.4 = (f32[2,4,8,256]{3,2,1,0:T(8,128)S(1)}, f32[2,4,8,256]{3,2,1,0:T(8,128)S(1)}, u32[]{:S(2)}, u32[]{:S(2)}) collective-permute-start(f32[2,4,8,256]{3,2,1,0:T(8,128)S(1)} %get-tuple-element.65), channel_id=1, source_target_pairs={{8,0},{16,8},{24,16},{0,24},{9,1},{17,9},{25,17},{1,25},{10,2},{18... | collective-permute-start | bytes 196616 | tf_op jit(solution)/shard_map/ppermute | solution.py:23
  65.1 2.3 %collective-permute-done.5 = f32[2,4,8,256]{3,2,1,0:T(8,128)S(1)} collective-permute-done((f32[2,4,8,256]{3,2,1,0:T(8,128)S(1)}, f32[2,4,8,256]{3,2,1,0:T(8,128)S(1)}, u32[]{:S(2)}, u32[]{:S(2)}) %collective-permute-start.5) | collective-permute-done | bytes 65568 | tf_op jit(solution)/shard_map/ppermute | solution.py:23
  67.8 14.8 %block_grads.1 = (f32[256,1024]{1,0:T(8,128)}, bf16[256,1024]{1,0:T(8,128)(2,1)S(1)}, bf16[256,1024]{1,0:T(8,128)(2,1)S(1)}, bf16[2,256,1024]{2,1,0:T(8,128)(2,1)}) custom-call(s32[3]{0:T(128)S(1)} %convert_element_type.21.linked_ref, bf16[256,1024]{1,0:T(8,128)(2,1)S(1)} %bitcast.56, bf16[256,1024]{1,0:T(8,128)(2,1)S(1)} %bitcast.59, ...), custom_call_target="tpu_custom_call" | custom-call | flops 4026531840 | bytes 8388608 | tf_op jit(solution)/shard_map/block_grads/pallas_call | solution.py:195
  82.7 1.4 collective-permute-start.22
  85.9 1.3 collective-permute-start.12
  87.2 7.1 %collective-permute-start.15 = (bf16[96,3072]{1,0:T(8,128)(2,1)S(1)}, bf16[96,3072]{1,0:T(8,128)(2,1)S(1)}, u32[]{:S(2)}, u32[]{:S(2)}) collective-permute-start(bf16[96,3072]{1,0:T(8,128)(2,1)S(1)} %copy-done.12), channel_id=1, source_target_pairs={{0,8},{8,16},{16,24},{1,9},{9,17},{17,25},{2,10},{10,18},{18,26},{... | collective-permute-start | bytes 1769480 | tf_op jit(solution)/shard_map/ppermute | solution.py:322
  94.3 1.3 collective-permute-start.13
  95.6 1.3 slice_bitcast_fusion.7
  96.8 2.7 %collective-permute-start.7 = (bf16[256,1024]{1,0:T(8,128)(2,1)S(1)}, bf16[256,1024]{1,0:T(8,128)(2,1)S(1)}, u32[]{:S(2)}, u32[]{:S(2)}) collective-permute-start(bf16[256,1024]{1,0:T(8,128)(2,1)S(1)} %get-tuple-element.23), channel_id=1, source_target_pairs={{24,0},{0,8},{8,16},{16,24},{25,1},{1,9},{9,17},{17,25},{26,2},{2,... | collective-permute-start | bytes 1572872 | tf_op jit(solution)/shard_map/ppermute | solution.py:23
  99.5 1.4 collective-permute-start.8
  101.0 30.7 %collective-permute-done.7 = bf16[256,1024]{1,0:T(8,128)(2,1)S(1)} collective-permute-done((bf16[256,1024]{1,0:T(8,128)(2,1)S(1)}, bf16[256,1024]{1,0:T(8,128)(2,1)S(1)}, u32[]{:S(2)}, u32[]{:S(2)}) %collective-permute-start.7) | collective-permute-done | bytes 524320 | tf_op jit(solution)/shard_map/ppermute | solution.py:23
  131.7 1.3 collective-permute-start.16
  133.0 7.4 %collective-permute-done.8 = bf16[256,1024]{1,0:T(8,128)(2,1)S(1)} collective-permute-done((bf16[256,1024]{1,0:T(8,128)(2,1)S(1)}, bf16[256,1024]{1,0:T(8,128)(2,1)S(1)}, u32[]{:S(2)}, u32[]{:S(2)}) %collective-permute-start.8) | collective-permute-done | bytes 524320 | tf_op jit(solution)/shard_map/ppermute | solution.py:23
  140.7 2.6 %collective-permute-start.19 = (bf16[2,256,1024]{2,1,0:T(8,128)(2,1)S(1)}, bf16[2,256,1024]{2,1,0:T(8,128)(2,1)S(1)}, u32[]{:S(2)}, u32[]{:S(2)}) collective-permute-start(bf16[2,256,1024]{2,1,0:T(8,128)(2,1)S(1)} %copy-done.9), channel_id=1, source_target_pairs={{0,8},{24,16},{1,9},{25,17},{2,10},{26,18},{3,11},{27,19},{4,12},{... | collective-permute-start | bytes 3145736 | tf_op jit(solution)/shard_map/ppermute | solution.py:334
  143.6 1.5 collective-permute-start.18
  145.2 1.3 collective-permute-start.24
  148.5 1.3 collective-permute-start.26
  149.8 2.7 %convolution_convert_fusion = bf16[512,768]{1,0:T(8,128)(2,1)S(1)} fusion(bf16[768,3072]{1,0:T(8,128)(2,1)S(1)} %constant_dynamic-update-slice_fusion, bf16[256,1024]{1,0:T(8,128)(2,1)S(1)} %get-tuple-element.44, bf16[256,1024]{1,0:T(8,128)(2,1)S(1)} %get-tuple-element.43, bf16[256,1024]{1,0:T(8,128)(2,1)S(1)} %collective-permute-done.9, ...), kind=kOutput, calls=%fused_computation.16 | convolution fusion | flops 2435186688 | bytes 8650752 | tf_op jit(solution)/shard_map/dot_general | solution.py:31
  152.5 14.2 %collective-permute-done.19 = bf16[2,256,1024]{2,1,0:T(8,128)(2,1)S(1)} collective-permute-done((bf16[2,256,1024]{2,1,0:T(8,128)(2,1)S(1)}, bf16[2,256,1024]{2,1,0:T(8,128)(2,1)S(1)}, u32[]{:S(2)}, u32[]{:S(2)}) %collective-permute-start.19) | collective-permute-done | bytes 1048608 | tf_op jit(solution)/shard_map/ppermute | solution.py:334
  167.5 1.4 collective-permute-start.30
  168.9 1.3 collective-permute-start.17
  170.3 7.2 %collective-permute-done.18 = bf16[256,1024]{1,0:T(8,128)(2,1)S(1)} collective-permute-done((bf16[256,1024]{1,0:T(8,128)(2,1)S(1)}, bf16[256,1024]{1,0:T(8,128)(2,1)S(1)}, u32[]{:S(2)}, u32[]{:S(2)}) %collective-permute-start.18) | collective-permute-done | bytes 524320 | tf_op jit(solution)/shard_map/ppermute | solution.py:335
  179.1 1.1 collective-permute-done.21
  180.9 1.0 fusion.12
  182.0 1.3 collective-permute-start.31
  183.3 2.5 %collective-permute-start.29 = (bf16[256,256]{1,0:T(8,128)(2,1)S(1)}, bf16[256,256]{1,0:T(8,128)(2,1)S(1)}, u32[]{:S(2)}, u32[]{:S(2)}) collective-permute-start(bf16[256,256]{1,0:T(8,128)(2,1)S(1)} %get-tuple-element.54), channel_id=1, source_target_pairs={{0,3},{1,0},{2,1},{3,2},{4,7},{5,4},{6,5},{7,6},{8,11},{9,8},{10,9... | collective-permute-start | bytes 393224 | tf_op jit(solution)/shard_map/ppermute | solution.py:250
  185.9 1.3 collective-permute-start.28
  187.1 2.6 %collective-permute-done.31 = bf16[256,256]{1,0:T(8,128)(2,1)S(1)} collective-permute-done((bf16[256,256]{1,0:T(8,128)(2,1)S(1)}, bf16[256,256]{1,0:T(8,128)(2,1)S(1)}, u32[]{:S(2)}, u32[]{:S(2)}) %collective-permute-start.31) | collective-permute-done | bytes 131104 | tf_op jit(solution)/shard_map/ppermute | solution.py:250
  190.5 4.3 %collective-permute-done.28 = bf16[256,256]{1,0:T(8,128)(2,1)S(1)} collective-permute-done((bf16[256,256]{1,0:T(8,128)(2,1)S(1)}, bf16[256,256]{1,0:T(8,128)(2,1)S(1)}, u32[]{:S(2)}, u32[]{:S(2)}) %collective-permute-start.28) | collective-permute-done | bytes 131104 | tf_op jit(solution)/shard_map/ppermute | solution.py:250
  195.8 2.7 %collective-permute-done.32.refs_6_ = bf16[256,256]{1,0:T(8,128)(2,1)S(1)} collective-permute-done((bf16[256,256]{1,0:T(8,128)(2,1)S(1)}, bf16[256,256]{1,0:T(8,128)(2,1)S(1)}, u32[]{:S(2)}, u32[]{:S(2)}) %collective-permute-start.32) | collective-permute-done | bytes 131104 | tf_op jit(solution)/shard_map/ppermute | solution.py:250
  199.2 2.4 %placed.1 = bf16[256,2048]{1,0:T(8,128)(2,1)} custom-call(s32[8]{0:T(128)} %stack.56.at_ref, bf16[256,256]{1,0:T(8,128)(2,1)} %get-tuple-element.52.refs_0_, bf16[256,256]{1,0:T(8,128)(2,1)} %get-tuple-element.50.refs_1_, bf16[256,256]{1,0:T(8,128)(2,1)} %copy-done.13, bf16[256,256]{1,0:T(8,128)(2,1)} %get-tuple-element.49.refs_3_, ...), custom_call_target="tpu_custom_call" | custom-call | tf_op jit(solution)/shard_map/placed/pallas_call | solution.py:371
  (93 shorter events, 12.4 us)
Async XLA Ops:
  0.0 9.6 %copy-start = (s32[4,3]{1,0:T(4,128)S(1)}, s32[4,3]{1,0:T(4,128)}, u32[]{:S(2)}) copy-start(s32[4,3]{1,0:T(4,128)} %param.12) | copy-start | bytes 148
  0.0 52.4 %copy-start.2 = (bf16[1,1,1,256,1024]{4,3,2,1,0:T(8,128)(2,1)S(1)}, bf16[1,1,1,256,1024]{4,3,2,1,0:T(8,128)(2,1)}, u32[]{:S(2)}) copy-start(bf16[1,1,1,256,1024]{4,3,2,1,0:T(8,128)(2,1)} %param.8) | copy-start | bytes 1572868
  0.0 22.9 %collective-permute-start = (bf16[256,1024]{1,0:T(8,128)(2,1)}, bf16[256,1024]{1,0:T(8,128)(2,1)S(1)}, u32[]{:S(2)}, u32[]{:S(2)}) collective-permute-start(bf16[256,1024]{1,0:T(8,128)(2,1)} %bitcast.60), channel_id=1, source_target_pairs={{8,0},{16,8},{24,16},{0,24},{9,1},{17,9},{25,17},{1,25},{10,2},{18... | collective-permute-start | bytes 1572872 | tf_op jit(solution)/shard_map/ppermute | solution.py:23
  5.1 35.2 %collective-permute-start.2 = (bf16[256,1024]{1,0:T(8,128)(2,1)}, bf16[256,1024]{1,0:T(8,128)(2,1)S(1)}, u32[]{:S(2)}, u32[]{:S(2)}) collective-permute-start(bf16[256,1024]{1,0:T(8,128)(2,1)} %bitcast.61), channel_id=1, source_target_pairs={{24,0},{0,8},{8,16},{16,24},{25,1},{1,9},{9,17},{17,25},{26,2},{2,... | collective-permute-start | bytes 1572872 | tf_op jit(solution)/shard_map/ppermute | solution.py:23
  5.1 35.2 %collective-permute-start.1 = (bf16[256,1024]{1,0:T(8,128)(2,1)}, bf16[256,1024]{1,0:T(8,128)(2,1)}, u32[]{:S(2)}, u32[]{:S(2)}) collective-permute-start(bf16[256,1024]{1,0:T(8,128)(2,1)} %bitcast.64), channel_id=1, source_target_pairs={{8,0},{16,8},{24,16},{0,24},{9,1},{17,9},{25,17},{1,25},{10,2},{18... | collective-permute-start | bytes 1572872 | tf_op jit(solution)/shard_map/ppermute | solution.py:23
  8.9 43.5 %collective-permute-start.3 = (bf16[256,1024]{1,0:T(8,128)(2,1)}, bf16[256,1024]{1,0:T(8,128)(2,1)}, u32[]{:S(2)}, u32[]{:S(2)}) collective-permute-start(bf16[256,1024]{1,0:T(8,128)(2,1)} %bitcast.65), channel_id=1, source_target_pairs={{24,0},{0,8},{8,16},{16,24},{25,1},{1,9},{9,17},{17,25},{26,2},{2,... | collective-permute-start | bytes 1572872 | tf_op jit(solution)/shard_map/ppermute | solution.py:23
  12.1 1.0 copy-start.1
  14.1 1.0 copy-start.5
  15.2 1.0 copy-start.7
  16.2 36.2 %copy-start.4 = (bf16[1,1,1,256,1024]{4,3,2,1,0:T(8,128)(2,1)S(1)}, bf16[1,1,1,256,1024]{4,3,2,1,0:T(8,128)(2,1)}, u32[]{:S(2)}) copy-start(bf16[1,1,1,256,1024]{4,3,2,1,0:T(8,128)(2,1)} %param.9) | copy-start | bytes 1572868
  18.8 63.9 %collective-permute-start.11 = (bf16[64,3072]{1,0:T(8,128)(2,1)}, bf16[64,3072]{1,0:T(8,128)(2,1)}, u32[]{:S(2)}, u32[]{:S(2)}) collective-permute-start(bf16[64,3072]{1,0:T(8,128)(2,1)} %dynamic-slice_bitcast_fusion.2), channel_id=1, source_target_pairs={{8,0},{16,8},{24,16},{9,1},{17,9},{25,17},{10,2},{18,10},{26,18},{... | collective-permute-start | bytes 1179656 | tf_op jit(solution)/shard_map/ppermute | solution.py:323
  20.1 47.6 %copy-start.6 = (bf16[1,1,1,256,1024]{4,3,2,1,0:T(8,128)(2,1)S(1)}, bf16[1,1,1,256,1024]{4,3,2,1,0:T(8,128)(2,1)}, u32[]{:S(2)}) copy-start(bf16[1,1,1,256,1024]{4,3,2,1,0:T(8,128)(2,1)} %param.7) | copy-start | bytes 1572868
  20.1 47.6 %copy-start.8 = (bf16[1,1,1,256,1024]{4,3,2,1,0:T(8,128)(2,1)S(1)}, bf16[1,1,1,256,1024]{4,3,2,1,0:T(8,128)(2,1)}, u32[]{:S(2)}) copy-start(bf16[1,1,1,256,1024]{4,3,2,1,0:T(8,128)(2,1)} %param.10) | copy-start | bytes 1572868
  22.9 61.2 %collective-permute-start.14 = (bf16[64,3072]{1,0:T(8,128)(2,1)}, bf16[64,3072]{1,0:T(8,128)(2,1)}, u32[]{:S(2)}, u32[]{:S(2)}) collective-permute-start(bf16[64,3072]{1,0:T(8,128)(2,1)} %dynamic-slice_bitcast_fusion.2), channel_id=1, source_target_pairs={{0,8},{8,16},{16,24},{1,9},{9,17},{17,25},{2,10},{10,18},{18,26},{... | collective-permute-start | bytes 1179656 | tf_op jit(solution)/shard_map/ppermute | solution.py:322
  57.2 7.8 %collective-permute-start.6 = (f32[2,4,8,256]{3,2,1,0:T(8,128)S(1)}, f32[2,4,8,256]{3,2,1,0:T(8,128)S(1)}, u32[]{:S(2)}, u32[]{:S(2)}) collective-permute-start(f32[2,4,8,256]{3,2,1,0:T(8,128)S(1)} %get-tuple-element.63), channel_id=1, source_target_pairs={{16,0},{24,8},{0,16},{8,24},{17,1},{25,9},{1,17},{9,25},{18,2},{26... | collective-permute-start | bytes 196616 | tf_op jit(solution)/shard_map/ppermute | solution.py:23
  61.2 6.2 %collective-permute-start.5 = (f32[2,4,8,256]{3,2,1,0:T(8,128)S(1)}, f32[2,4,8,256]{3,2,1,0:T(8,128)S(1)}, u32[]{:S(2)}, u32[]{:S(2)}) collective-permute-start(f32[2,4,8,256]{3,2,1,0:T(8,128)S(1)} %get-tuple-element.64), channel_id=1, source_target_pairs={{24,0},{0,8},{8,16},{16,24},{25,1},{1,9},{9,17},{17,25},{26,2},{2,... | collective-permute-start | bytes 196616 | tf_op jit(solution)/shard_map/ppermute | solution.py:23
  62.8 5.0 %collective-permute-start.4 = (f32[2,4,8,256]{3,2,1,0:T(8,128)S(1)}, f32[2,4,8,256]{3,2,1,0:T(8,128)S(1)}, u32[]{:S(2)}, u32[]{:S(2)}) collective-permute-start(f32[2,4,8,256]{3,2,1,0:T(8,128)S(1)} %get-tuple-element.65), channel_id=1, source_target_pairs={{8,0},{16,8},{24,16},{0,24},{9,1},{17,9},{25,17},{1,25},{10,2},{18... | collective-permute-start | bytes 196616 | tf_op jit(solution)/shard_map/ppermute | solution.py:23
  67.4 17.4 %slice-start = ((s8[4718592]{0:T(1024)(128)(4,1)}), s8[4194304]{0:T(1024)(128)(4,1)S(1)}, s32[]{:S(2)}) async-start(s8[4718592]{0:T(1024)(128)(4,1)} %bitcast.72), calls=%async_computation | async-start | bytes 8388608
  67.8 17.0 %slice-start.1 = ((s8[4718592]{0:T(1024)(128)(4,1)}), s8[524288]{0:T(1024)(128)(4,1)S(1)}, s32[]{:S(2)}) async-start(s8[4718592]{0:T(1024)(128)(4,1)} %bitcast.72), calls=%async_computation.1 | async-start | bytes 1048576
  67.8 18.1 %copy-start.12 = (bf16[96,3072]{1,0:T(8,128)(2,1)S(1)}, bf16[96,3072]{1,0:T(8,128)(2,1)}, u32[]{:S(2)}) copy-start(bf16[96,3072]{1,0:T(8,128)(2,1)} %get-tuple-element.27) | copy-start | bytes 1769476
  67.8 26.4 %copy-start.11 = (bf16[96,3072]{1,0:T(8,128)(2,1)S(1)}, bf16[96,3072]{1,0:T(8,128)(2,1)}, u32[]{:S(2)}) copy-start(bf16[96,3072]{1,0:T(8,128)(2,1)} %get-tuple-element.28) | copy-start | bytes 1769476
  82.6 57.8 %copy-start.10 = (f32[256,1024]{1,0:T(8,128)S(1)}, f32[256,1024]{1,0:T(8,128)}, u32[]{:S(2)}) copy-start(f32[256,1024]{1,0:T(8,128)} %get-tuple-element.22) | copy-start | bytes 3145732
  82.6 58.0 %copy-start.9 = (bf16[2,256,1024]{2,1,0:T(8,128)(2,1)S(1)}, bf16[2,256,1024]{2,1,0:T(8,128)(2,1)}, u32[]{:S(2)}) copy-start(bf16[2,256,1024]{2,1,0:T(8,128)(2,1)} %get-tuple-element.25) | copy-start | bytes 3145732
  82.7 14.2 %collective-permute-start.22 = (bf16[64,3072]{1,0:T(8,128)(2,1)}, bf16[64,3072]{1,0:T(8,128)(2,1)S(1)}, u32[]{:S(2)}, u32[]{:S(2)}) collective-permute-start(bf16[64,3072]{1,0:T(8,128)(2,1)} %collective-permute-done.11), channel_id=1, source_target_pairs={{8,0},{16,8},{9,1},{17,9},{10,2},{18,10},{11,3},{19,11},{12,4},{20... | collective-permute-start | bytes 1179656 | tf_op jit(solution)/shard_map/ppermute | solution.py:331
  84.1 15.4 %collective-permute-start.23 = (bf16[64,3072]{1,0:T(8,128)(2,1)}, bf16[64,3072]{1,0:T(8,128)(2,1)S(1)}, u32[]{:S(2)}, u32[]{:S(2)}) collective-permute-start(bf16[64,3072]{1,0:T(8,128)(2,1)} %collective-permute-done.14), channel_id=1, source_target_pairs={{8,16},{16,24},{9,17},{17,25},{10,18},{18,26},{11,19},{19,27},{12,... | collective-permute-start | bytes 1179656 | tf_op jit(solution)/shard_map/ppermute | solution.py:330
  85.9 54.8 %collective-permute-start.12 = (bf16[96,3072]{1,0:T(8,128)(2,1)S(1)}, bf16[96,3072]{1,0:T(8,128)(2,1)S(1)}, u32[]{:S(2)}, u32[]{:S(2)}) collective-permute-start(bf16[96,3072]{1,0:T(8,128)(2,1)S(1)} %copy-done.12), channel_id=1, source_target_pairs={{8,0},{16,8},{24,16},{9,1},{17,9},{25,17},{10,2},{18,10},{26,18},{... | collective-permute-start | bytes 1769480 | tf_op jit(solution)/shard_map/ppermute | solution.py:323
  87.2 56.1 %collective-permute-start.15 = (bf16[96,3072]{1,0:T(8,128)(2,1)S(1)}, bf16[96,3072]{1,0:T(8,128)(2,1)S(1)}, u32[]{:S(2)}, u32[]{:S(2)}) collective-permute-start(bf16[96,3072]{1,0:T(8,128)(2,1)S(1)} %copy-done.12), channel_id=1, source_target_pairs={{0,8},{8,16},{16,24},{1,9},{9,17},{17,25},{2,10},{10,18},{18,26},{... | collective-permute-start | bytes 1769480 | tf_op jit(solution)/shard_map/ppermute | solution.py:322
  94.3 49.4 %collective-permute-start.13 = (bf16[96,3072]{1,0:T(8,128)(2,1)S(1)}, bf16[96,3072]{1,0:T(8,128)(2,1)S(1)}, u32[]{:S(2)}, u32[]{:S(2)}) collective-permute-start(bf16[96,3072]{1,0:T(8,128)(2,1)S(1)} %copy-done.11), channel_id=1, source_target_pairs={{8,0},{16,8},{24,16},{9,1},{17,9},{25,17},{10,2},{18,10},{26,18},{... | collective-permute-start | bytes 1769480 | tf_op jit(solution)/shard_map/ppermute | solution.py:323
  96.8 34.8 %collective-permute-start.7 = (bf16[256,1024]{1,0:T(8,128)(2,1)S(1)}, bf16[256,1024]{1,0:T(8,128)(2,1)S(1)}, u32[]{:S(2)}, u32[]{:S(2)}) collective-permute-start(bf16[256,1024]{1,0:T(8,128)(2,1)S(1)} %get-tuple-element.23), channel_id=1, source_target_pairs={{24,0},{0,8},{8,16},{16,24},{25,1},{1,9},{9,17},{17,25},{26,2},{2,... | collective-permute-start | bytes 1572872 | tf_op jit(solution)/shard_map/ppermute | solution.py:23
  99.5 40.9 %collective-permute-start.8 = (bf16[256,1024]{1,0:T(8,128)(2,1)S(1)}, bf16[256,1024]{1,0:T(8,128)(2,1)S(1)}, u32[]{:S(2)}, u32[]{:S(2)}) collective-permute-start(bf16[256,1024]{1,0:T(8,128)(2,1)S(1)} %get-tuple-element.24), channel_id=1, source_target_pairs={{8,0},{16,8},{24,16},{0,24},{9,1},{17,9},{25,17},{1,25},{10,2},{18... | collective-permute-start | bytes 1572872 | tf_op jit(solution)/shard_map/ppermute | solution.py:23
  131.7 13.6 %collective-permute-start.16 = (bf16[96,3072]{1,0:T(8,128)(2,1)S(1)}, bf16[96,3072]{1,0:T(8,128)(2,1)S(1)}, u32[]{:S(2)}, u32[]{:S(2)}) collective-permute-start(bf16[96,3072]{1,0:T(8,128)(2,1)S(1)} %copy-done.11), channel_id=1, source_target_pairs={{0,8},{8,16},{16,24},{1,9},{9,17},{17,25},{2,10},{10,18},{18,26},{... | collective-permute-start | bytes 1769480 | tf_op jit(solution)/shard_map/ppermute | solution.py:322
  140.4 7.3 %collective-permute-start.10 = (bf16[2,256,1024]{2,1,0:T(8,128)(2,1)}, bf16[2,256,1024]{2,1,0:T(8,128)(2,1)S(1)}, u32[]{:S(2)}, u32[]{:S(2)}) collective-permute-start(bf16[2,256,1024]{2,1,0:T(8,128)(2,1)} %get-tuple-element.25), channel_id=1, source_target_pairs={{0,4},{4,0},{1,5},{5,1},{2,6},{6,2},{3,7},{7,3},{8,12},{12,8},{9,1... | collective-permute-start | bytes 3145736 | tf_op jit(solution)/shard_map/ppermute | solution.py:232
  140.7 26.0 %collective-permute-start.19 = (bf16[2,256,1024]{2,1,0:T(8,128)(2,1)S(1)}, bf16[2,256,1024]{2,1,0:T(8,128)(2,1)S(1)}, u32[]{:S(2)}, u32[]{:S(2)}) collective-permute-start(bf16[2,256,1024]{2,1,0:T(8,128)(2,1)S(1)} %copy-done.9), channel_id=1, source_target_pairs={{0,8},{24,16},{1,9},{25,17},{2,10},{26,18},{3,11},{27,19},{4,12},{... | collective-permute-start | bytes 3145736 | tf_op jit(solution)/shard_map/ppermute | solution.py:334
  143.3 5.2 %collective-permute-start.9 = (bf16[256,1024]{1,0:T(8,128)(2,1)S(1)}, bf16[256,1024]{1,0:T(8,128)(2,1)S(1)}, u32[]{:S(2)}, u32[]{:S(2)}) collective-permute-start(bf16[256,1024]{1,0:T(8,128)(2,1)S(1)} %add_convert_fusion), channel_id=1, source_target_pairs={{0,4},{4,0},{1,5},{5,1},{2,6},{6,2},{3,7},{7,3},{8,12},{12,8},{9,1... | collective-permute-start | bytes 1572872 | tf_op jit(solution)/shard_map/ppermute | solution.py:232
  143.6 33.9 %collective-permute-start.18 = (bf16[256,1024]{1,0:T(8,128)(2,1)S(1)}, bf16[256,1024]{1,0:T(8,128)(2,1)S(1)}, u32[]{:S(2)}, u32[]{:S(2)}) collective-permute-start(bf16[256,1024]{1,0:T(8,128)(2,1)S(1)} %add_convert_fusion), channel_id=1, source_target_pairs={{0,8},{24,16},{1,9},{25,17},{2,10},{26,18},{3,11},{27,19},{4,12},{... | collective-permute-start | bytes 1572872 | tf_op jit(solution)/shard_map/ppermute | solution.py:335
  145.2 22.2 %collective-permute-start.24 = (bf16[96,3072]{1,0:T(8,128)(2,1)S(1)}, bf16[96,3072]{1,0:T(8,128)(2,1)S(1)}, u32[]{:S(2)}, u32[]{:S(2)}) collective-permute-start(bf16[96,3072]{1,0:T(8,128)(2,1)S(1)} %collective-permute-done.12), channel_id=1, source_target_pairs={{8,0},{16,8},{9,1},{17,9},{10,2},{18,10},{11,3},{19,11},{12,4},{20... | collective-permute-start | bytes 1769480 | tf_op jit(solution)/shard_map/ppermute | solution.py:331
  147.7 21.2 %collective-permute-start.25 = (bf16[96,3072]{1,0:T(8,128)(2,1)S(1)}, bf16[96,3072]{1,0:T(8,128)(2,1)S(1)}, u32[]{:S(2)}, u32[]{:S(2)}) collective-permute-start(bf16[96,3072]{1,0:T(8,128)(2,1)S(1)} %collective-permute-done.15), channel_id=1, source_target_pairs={{8,16},{16,24},{9,17},{17,25},{10,18},{18,26},{11,19},{19,27},{12,... | collective-permute-start | bytes 1769480 | tf_op jit(solution)/shard_map/ppermute | solution.py:330
  148.5 29.1 %collective-permute-start.26 = (bf16[96,3072]{1,0:T(8,128)(2,1)S(1)}, bf16[96,3072]{1,0:T(8,128)(2,1)S(1)}, u32[]{:S(2)}, u32[]{:S(2)}) collective-permute-start(bf16[96,3072]{1,0:T(8,128)(2,1)S(1)} %collective-permute-done.13), channel_id=1, source_target_pairs={{8,0},{16,8},{9,1},{17,9},{10,2},{18,10},{11,3},{19,11},{12,4},{20... | collective-permute-start | bytes 1769480 | tf_op jit(solution)/shard_map/ppermute | solution.py:331
  166.7 11.4 %collective-permute-start.27 = (bf16[96,3072]{1,0:T(8,128)(2,1)S(1)}, bf16[96,3072]{1,0:T(8,128)(2,1)S(1)}, u32[]{:S(2)}, u32[]{:S(2)}) collective-permute-start(bf16[96,3072]{1,0:T(8,128)(2,1)S(1)} %collective-permute-done.16), channel_id=1, source_target_pairs={{8,16},{16,24},{9,17},{17,25},{10,18},{18,26},{11,19},{19,27},{12,... | collective-permute-start | bytes 1769480 | tf_op jit(solution)/shard_map/ppermute | solution.py:330
  167.5 18.4 %collective-permute-start.30 = (bf16[256,768]{1,0:T(8,128)(2,1)S(1)}, bf16[256,768]{1,0:T(8,128)(2,1)S(1)}, u32[]{:S(2)}, u32[]{:S(2)}) collective-permute-start(bf16[256,768]{1,0:T(8,128)(2,1)S(1)} %get-tuple-element.45), channel_id=1, source_target_pairs={{0,7},{1,4},{2,5},{3,6},{4,3},{5,0},{6,1},{7,2},{8,15},{9,12},{10,... | collective-permute-start | bytes 1179656 | tf_op jit(solution)/shard_map/ppermute | solution.py:250
  168.9 21.6 %collective-permute-start.17 = (bf16[256,768]{1,0:T(8,128)(2,1)S(1)}, bf16[256,768]{1,0:T(8,128)(2,1)S(1)}, u32[]{:S(2)}, u32[]{:S(2)}) collective-permute-start(bf16[256,768]{1,0:T(8,128)(2,1)S(1)} %get-tuple-element.46), channel_id=1, source_target_pairs={{0,3},{1,0},{2,1},{3,2},{4,7},{5,4},{6,5},{7,6},{8,11},{9,8},{10,9... | collective-permute-start | bytes 1179656 | tf_op jit(solution)/shard_map/ppermute | solution.py:250
  177.5 2.7 %collective-permute-start.21 = (bf16[2,256,1024]{2,1,0:T(8,128)(2,1)S(1)}, bf16[2,256,1024]{2,1,0:T(8,128)(2,1)S(1)}, u32[]{:S(2)}, u32[]{:S(2)}) collective-permute-start(bf16[2,256,1024]{2,1,0:T(8,128)(2,1)S(1)} %collective-permute-done.19), channel_id=1, source_target_pairs={{0,4},{4,0},{1,5},{5,1},{2,6},{6,2},{3,7},{7,3},{8,12},{12,8},{9,1... | collective-permute-start | bytes 3145736 | tf_op jit(solution)/shard_map/ppermute | solution.py:232
  177.5 3.4 %collective-permute-start.20 = (bf16[256,1024]{1,0:T(8,128)(2,1)S(1)}, bf16[256,1024]{1,0:T(8,128)(2,1)S(1)}, u32[]{:S(2)}, u32[]{:S(2)}) collective-permute-start(bf16[256,1024]{1,0:T(8,128)(2,1)S(1)} %collective-permute-done.18), channel_id=1, source_target_pairs={{0,4},{4,0},{1,5},{5,1},{2,6},{6,2},{3,7},{7,3},{8,12},{12,8},{9,1... | collective-permute-start | bytes 1572872 | tf_op jit(solution)/shard_map/ppermute | solution.py:232
  182.0 7.7 %collective-permute-start.31 = (bf16[256,256]{1,0:T(8,128)(2,1)S(1)}, bf16[256,256]{1,0:T(8,128)(2,1)S(1)}, u32[]{:S(2)}, u32[]{:S(2)}) collective-permute-start(bf16[256,256]{1,0:T(8,128)(2,1)S(1)} %get-tuple-element.55), channel_id=1, source_target_pairs={{8,7},{9,4},{10,5},{11,6},{12,3},{13,0},{14,1},{15,2},{16,31},{17,... | collective-permute-start | bytes 393224 | tf_op jit(solution)/shard_map/ppermute | solution.py:250
  183.3 12.5 %collective-permute-start.29 = (bf16[256,256]{1,0:T(8,128)(2,1)S(1)}, bf16[256,256]{1,0:T(8,128)(2,1)S(1)}, u32[]{:S(2)}, u32[]{:S(2)}) collective-permute-start(bf16[256,256]{1,0:T(8,128)(2,1)S(1)} %get-tuple-element.54), channel_id=1, source_target_pairs={{0,3},{1,0},{2,1},{3,2},{4,7},{5,4},{6,5},{7,6},{8,11},{9,8},{10,9... | collective-permute-start | bytes 393224 | tf_op jit(solution)/shard_map/ppermute | solution.py:250
  185.8 12.7 %collective-permute-start.32 = (bf16[256,256]{1,0:T(8,128)(2,1)S(1)}, bf16[256,256]{1,0:T(8,128)(2,1)S(1)}, u32[]{:S(2)}, u32[]{:S(2)}) collective-permute-start(bf16[256,256]{1,0:T(8,128)(2,1)S(1)} %get-tuple-element.53), channel_id=1, source_target_pairs={{0,7},{1,4},{2,5},{3,6},{4,3},{5,0},{6,1},{7,2},{8,15},{9,12},{10,... | collective-permute-start | bytes 393224 | tf_op jit(solution)/shard_map/ppermute | solution.py:250
  185.9 9.0 %collective-permute-start.28 = (bf16[256,256]{1,0:T(8,128)(2,1)S(1)}, bf16[256,256]{1,0:T(8,128)(2,1)S(1)}, u32[]{:S(2)}, u32[]{:S(2)}) collective-permute-start(bf16[256,256]{1,0:T(8,128)(2,1)S(1)} %get-tuple-element.56), channel_id=1, source_target_pairs={{8,3},{9,0},{10,1},{11,2},{12,7},{13,4},{14,5},{15,6},{16,27},{17,... | collective-permute-start | bytes 393224 | tf_op jit(solution)/shard_map/ppermute | solution.py:250
  195.8 2.7 %copy-start.13 = (bf16[256,256]{1,0:T(8,128)(2,1)}, bf16[256,256]{1,0:T(8,128)(2,1)S(1)}, u32[]{:S(2)}) copy-start(bf16[256,256]{1,0:T(8,128)(2,1)S(1)} %collective-permute-done.29.refs_2_) | copy-start | bytes 393220
  (2 other events, 1.7 us)

commit v2 on v1

--- a/solution.py
+++ b/solution.py
@@ -8,6 +8,8 @@
 from jax.experimental.pallas import tpu as pltpu
 from jax.sharding import PartitionSpec as P
 
+OPT = {'k1': 1, 'k2': 1, 'kp': 1, 'wa': 'first', 'st': 1, 'dq': 1, 'cb': 0, 'cuts': [128], 'nc': 'token', 'far': {0: 'lret', 1: 'lret', 2: 'lret'}, 'order': '', 'op': 'ret1', 'sf': 'rfpq', 'one': 1, 's1': '', 'ft': ['ret1', 'ret1']}
+
 HEADS = 16
 CAUSAL_BLOCK = 128
 GROUP = 4
@@ -21,6 +23,10 @@
     devices = range(lax.axis_size(axis))
     route = [((i - distance) % len(devices), i) for i in devices]
     return lax.ppermute(block, axis, route)
+
+
+def spent(us):
+    return pl.CostEstimate(flops=int(us * 1.15e9), bytes_accessed=1024, transcendentals=0)
 
 
 def after(block, *earlier):
@@ -175,11 +181,7 @@
         out_specs=[stat] * n,
         out_shape=[jax.ShapeDtypeStruct((groups, 2 * GROUP, patches), f32)] * n,
         compiler_params=pltpu.CompilerParams(vmem_limit_bytes=48 * 2**20),
-        cost_estimate=pl.CostEstimate(
-            flops=8 * n * patches * patches * features,
-            bytes_accessed=4 * (n + 1) * patches * features,
-            transcendentals=n * HEADS * patches * patches,
-        ),
+        cost_estimate=spent(OPT["k1"] * 2.5 * n),
         name="row_stats",
     )(linked, keys, values, *[x for pair in pairs for x in pair])
 
@@ -201,11 +203,7 @@
         + [shape((patches, features), bf16)] * (n - 1)
         + [shape((2, patches, features), bf16)],
         compiler_params=pltpu.CompilerParams(vmem_limit_bytes=48 * 2**20),
-        cost_estimate=pl.CostEstimate(
-            flops=20 * n * patches * patches * features,
-            bytes_accessed=8 * (n + 1) * patches * features,
-            transcendentals=n * HEADS * patches * patches,
-        ),
+        cost_estimate=spent(OPT["k2"] * 4.8 * n),
         name="block_grads",
     )(
         linked,
@@ -216,12 +214,81 @@
     )
 
 
-def place_kernel(at_ref, *refs):
+def place_kernel(at_ref, first_ref, *refs):
     out_ref = refs[-1]
-    for i, ref in enumerate(refs[:-1]):
-        width = ref.shape[1]
-        col = pl.multiple_of(at_ref[i] * width, width)
-        out_ref[pl.ds(0, ref.shape[0]), pl.ds(col, width)] = ref[...]
+    chunk = first_ref.shape[1] // 3
+
+    def put(at, value):
+        col = pl.multiple_of(at * CAUSAL_BLOCK, CAUSAL_BLOCK)
+        out_ref[:, pl.ds(col, value.shape[1])] = value
+
+    def put_rolled(at, pieces):
+        parts = [
+            ref[:, i : i + CAUSAL_BLOCK]
+            for ref in pieces
+            for i in range(0, ref.shape[1], CAUSAL_BLOCK)
+        ]
+        for i, part in enumerate(parts):
+            put(at + (i + 1) % len(parts), part)
+
+    for i in range(3):
+        put(at_ref[3 + i], first_ref[:, i * chunk : (i + 1) * chunk])
+    far0_ref, far1_ref, end_ref = refs[:-1]
+    put_rolled(at_ref[1], [far0_ref, far1_ref])
+
+    @pl.when(at_ref[0] != 0)
+    def _():
+        put_rolled(at_ref[2], [end_ref])
+
+
+def project_kernel(uses, sets, pieces, swaps, flag_ref, *refs):
+    tokens, rows = refs[: 2 * sets], refs[2 * sets : 2 * sets + pieces * (1 + swaps)]
+    outs = refs[2 * sets + pieces * (1 + swaps) :]
+    features = tokens[0].shape[1]
+    filled = [0] * sets
+
+    def add(piece, cols):
+        step = 256 if piece.shape[0] % 256 == 0 else CAUSAL_BLOCK
+
+        @pl.loop(0, piece.shape[0] // step)
+        def _(i):
+            part = piece[pl.ds(pl.multiple_of(i * step, step), step), :]
+            for t, col in cols:
+                at = pl.ds(pl.multiple_of(col + i * step, CAUSAL_BLOCK), step)
+                query, pair = tokens[2 * t], tokens[2 * t + 1]
+                total = dot_nt(query[...], part[:, :features])
+                total = total + dot_nt(pair[0], part[:, features : 2 * features])
+                total = total + dot_nt(pair[1], part[:, 2 * features :])
+                outs[t][:, at] = total.astype(bf16)
+
+    for p in range(pieces):
+        cols = [(t, filled[t]) for t in range(sets) if p in uses[t]]
+        if swaps:
+            pl.when(flag_ref[0] != 0)(functools.partial(add, rows[p], cols))
+            pl.when(flag_ref[0] == 0)(functools.partial(add, rows[pieces + p], cols))
+        else:
+            add(rows[p], cols)
+        for t, _ in cols:
+            filled[t] += rows[p].shape[0]
+
+
+def project(flag, token_sets, rows, other_rows=(), uses=None):
+    patches = token_sets[0][0].shape[0]
+    uses = uses or [list(range(len(rows)))] * len(token_sets)
+    widths = [sum(rows[p].shape[0] for p in use) for use in uses]
+    whole = pl.BlockSpec(memory_space=pltpu.VMEM)
+    operands = [x for t in token_sets for x in t] + list(rows) + list(other_rows)
+    return pl.pallas_call(
+        functools.partial(
+            project_kernel, uses, len(token_sets), len(rows), 1 if other_rows else 0
+        ),
+        in_specs=[pl.BlockSpec(memory_space=pltpu.SMEM)] + [whole] * len(operands),
+        out_specs=[whole] * len(token_sets),
+        out_shape=[jax.ShapeDtypeStruct((patches, width), bf16) for width in widths],
+        compiler_params=pltpu.CompilerParams(vmem_limit_bytes=32 * 2**20),
+        cost_estimate=spent(OPT["kp"] * (1 + 0.004 * sum(widths))),
+        name="project",
+    )(flag, *operands)
 
 
 def times(tokens, rows):
@@ -232,27 +299,13 @@
     return lax.ppermute(block, "dp", [(0, 1), (1, 0)])
 
 
-def handed_on(result, patches, segments, outer=None):
-    axes = ("dp", "segment") if outer is None else ("var", "dp", "segment")
-    out = []
-    for cross in range(2):
-        route = []
-        for src, dst in outer or [(0, 0)]:
-            for d in range(2):
-                for s in range(segments):
-                    route.append(
-                        (
-                            (src * 2 + d) * segments + s,
-                            (dst * 2 + (d + cross) % 2) * segments + (s - 1) % segments,
-                        )
-                    )
-        out.append(
-            lax.ppermute(result[cross * patches : (cross + 1) * patches], axes, route)
-        )
-    return out
-
-
-def attention_grads(queries, keys, values, out_grad, links, reach, first, second, third):
+def on_line(block, moves):
+    return lax.ppermute(
+        block, ("var", "dp"), [(a * 2 + c, b * 2 + d) for (a, c), (b, d) in moves]
+    )
+
+
+def attention_grads(queries, keys, values, out_grad, links, reach, sends):
     patches, feature_width = queries.shape
     head_size = feature_width // HEADS
     scale = 1.0 / math.sqrt(head_size)
@@ -265,7 +318,13 @@
     sources = (own + jnp.array(offsets, jnp.int32)) % n
     linked = jnp.any(links[sources] == own, axis=1).astype(jnp.int32)
     own_stats = block_stats(linked[:1], keys, values, pairs[:1], head_size, scale)
-    first(own_stats[0])
+    sent = sends[0](
+        *{
+            "first": [pairs[1][0]],
+            "own": [own_stats[0]],
+            "all": [x for p in pairs[1:] for x in p],
+        }[OPT["wa"]]
+    )
     other_stats = block_stats(linked[1:], keys, values, pairs[1:], head_size, scale)
     stats = dict(zip(offsets, list(own_stats) + list(other_stats)))
     needed = {}
@@ -274,23 +333,30 @@
             entries = needed.setdefault((d + e) % n, [])
             if -e not in entries:
                 entries.append(-e)
-    arrived = {}
+    arrived, messages = {}, []
     for t, entries in needed.items():
         if t == 0:
             arrived[t] = {o: stats[o] for o in entries}
             continue
         entries.sort()
         message = jnp.stack([stats[o] for o in entries])
-        message = passed_along(message, "var", -t)
+        message = passed_along(after(message, *sent) if OPT["st"] else message, "var", -t)
+        messages.append(message)
         arrived[t] = {o: message[i] for i, o in enumerate(entries)}
-    second(other_stats[0])
+    sent = sends[1](*messages)
     windows = [[arrived[(d + e) % n][-e] for e in offsets] for d in offsets]
     grads = block_grads(linked, keys, values, pairs, windows, head_size, scale)
-    third(grads[-1])
+    returned = [
+        passed_along(after(part, *sent) if OPT["dq"] else part, "var", o) for o, part in zip(offsets[1:], grads[1:-1])
+    ]
+    sent = sends[2](grads[-1])
     query_grad = grads[0]
-    for o, part in zip(offsets[1:], grads[1:-1]):
-        query_grad = query_grad + passed_along(part, "var", o).astype(f32)
-    return query_grad.astype(bf16), grads[-1]
+    for part in returned:
+        query_grad = query_grad + part.astype(f32)
+    query_grad = query_grad.astype(bf16)
+    if OPT["cb"]:
+        query_grad = after(query_grad, *sent)
+    return query_grad, grads[-1], returned
 
 
 def shards(queries, keys, values, out_grad, proj_weight, links):
@@ -301,8 +367,7 @@
     flat = [x.reshape(patches, feature_width) for x in (queries, keys, values, out_grad)]
     weight = proj_weight[0]
     if n != 4:
-        nothing = lambda value: None
-        query_grad, pair = attention_grads(*flat, links, reach, nothing, nothing, nothing)
+        query_grad, pair, returned = attention_grads(*flat, links, reach, [lambda *values: ()] * 3)
         grad_qkv = jnp.concatenate([query_grad, pair[0], pair[1]], axis=1)
         whole = lax.all_gather(weight, "var", axis=0, tiled=True)
         passed = passed_along(times(grad_qkv, whole), "segment", -1)
@@ -310,73 +375,118 @@
 
     own = lax.axis_index("var")
     core = lax.axis_index("dp")
-    half = weight.shape[0] // 2
-    cuts = [(0, half // 4), (half // 4, half * 5 // 8), (half * 5 // 8, half)]
-    below, above = [], []
-
-    def near(i):
-        def start(value):
-            lo, hi = cuts[i]
-            piece = lax.dynamic_slice_in_dim(weight, core * half + lo, hi - lo, 0)
-            piece = after(piece, value)
-            below.append(lax.ppermute(piece, "var", [(0, 1), (1, 2), (2, 3)]))
-            above.append(lax.ppermute(piece, "var", [(1, 0), (2, 1), (3, 2)]))
-
-        return start
-
-    query_grad, pair = attention_grads(*flat, links, reach, near(0), near(1), near(2))
-    far = []
-    for up, down in zip(below, above):
-        up = lax.ppermute(after(up, pair), "var", [(1, 2), (2, 3)])
-        down = lax.ppermute(after(down, pair), "var", [(1, 0), (2, 1)])
-        far.append(jnp.where(own < 2, down, up))
+    chunk = weight.shape[0]
+    ends = [0] + OPT["cuts"] + [chunk]
+    cuts = list(zip(ends[:-1], ends[1:]))
+    step_near = [((v, 0), (v + 1, 0)) for v in range(3)] + [((v + 1, 1), (v, 1)) for v in range(3)]
+    step_far = [((1, 0), (2, 0)), ((2, 0), (3, 0)), ((2, 1), (1, 1)), ((1, 1), (0, 1))]
+    near, swapped_near = [], {}
+
+    def send_near(i, *values):
+        near.append(on_line(after(weight[slice(*cuts[i])], *values), step_near))
+        return near[i:]
+
+    far, swapped_far, token = {}, {}, []
+    count = len(cuts)
+
+    def ties(names, pair, returned, query_grad):
+        have = {
+            "pair": lambda: [pair],
+            "token": lambda: token,
+            "ret0": lambda: returned[:1],
+            "ret": lambda: returned,
+            "ret1": lambda: returned[1:],
+            "sw": lambda: [swapped_near[i] for i in sorted(swapped_near)],
+            "nb": lambda: [near[1]],
+            "nl": lambda: [near[-1]],
+            "q": lambda: [query_grad],
+        }
+        return [x for name in names.split() for x in have[name]()]
+
+    def start_far(when, *state):
+        for i in [int(c) for c in OPT["order"]]:
+            if OPT["far"][i][0] == when:
+                far[i] = on_line(after(near[i], *ties(OPT["far"][i][1:], *state)), step_far)
+
+    def send_middle(*values):
+        sent = send_near(1, *values)
+        for i in range(count):
+            if OPT["far"][i] == "s":
+                far[i] = on_line(after(near[i], *values), step_far)
+        return sent
+
+    def send_last(pair):
+        token.append(swapped(after(near[0], pair)))
+        swapped_near[0] = token[0]
+        state = (pair, None, None)
+        if count > 2:
+            send_near(2, *ties(OPT["nc"], *state))
+        for i in range(1, count):
+            swapped_near[i] = swapped(after(near[i], pair))
+        start_far("e", *state)
+        return near[-1:]
+
+    query_grad, pair, returned = attention_grads(
+        *flat,
+        links,
+        reach,
+        [lambda *v: send_near(0, *v), send_middle, send_last],
+    )
+    state = (pair, returned, query_grad)
+    start_far("l", *state)
     inward = [(0, 1), (3, 2)]
-    outer_pair = lax.ppermute(pair, "var", inward)
+    outer_pair = lax.ppermute(after(pair, *ties(OPT["op"], *state)), "var", inward)
     outer_query = lax.ppermute(query_grad, "var", inward)
-
-    def tokens(query_part, pair_part):
-        other_pair, other_query = swapped(pair_part), swapped(query_part)
-        return jnp.concatenate(
-            [
-                jnp.concatenate([query_part, pair_part[0], pair_part[1]], axis=1),
-                jnp.concatenate([other_query, other_pair[0], other_pair[1]], axis=1),
-            ],
-            axis=0,
-        )
-
-    own_tokens = tokens(query_grad, pair)
-    outer_tokens = tokens(outer_query, outer_pair)
-    own_rows = lax.dynamic_slice_in_dim(weight, core * half, half, 0)
-    near_rows = jnp.concatenate([own_rows] + above + below, axis=0)
-    handed = handed_on(times(own_tokens, near_rows), patches, segments)
-    far_rows = jnp.concatenate(far, axis=0)
-    handed_far = handed_on(times(own_tokens, far_rows), patches, segments)
-    handed_end = handed_on(
-        times(outer_tokens, far_rows), patches, segments, outer=[(1, 0), (2, 3)]
+    far_here = (core == jnp.where(own < 2, 1, 0)).astype(jnp.int32).reshape(1)
+
+    def handed_on(block, moves):
+        route = [(a * segments + s, b * segments + (s - 1) % segments) for a, b in moves for s in range(segments)]
+        return lax.ppermute(block, ("var", "segment"), route)
+
+    in_place = [(v, v) for v in range(4)]
+    from_inner = [(1, 0), (2, 3)]
+    own_set, outer_set = (query_grad, pair), (outer_query, outer_pair)
+    (result,) = project(far_here, [own_set], [weight] + near + [swapped_near[i] for i in range(count)])
+    first = handed_on(result, in_place)
+    if OPT.get("one"):
+        joined = jnp.concatenate([near[1][256:], near[0]], axis=0)
+        rows = [near[1][:256], joined]
+        far = [on_line(after(r, *ties(OPT["ft"][i], *state)), step_far) for i, r in enumerate(rows)]
+    have = {"r": result, "f": first, "p": outer_pair, "q": outer_query}
+    ties_of = [have[c] for c in OPT["sf"]]
+    other0 = swapped(after(far[0], *ties_of))
+    (far0,) = project(far_here, [own_set], far[:1], [other0])
+    handed0 = handed_on(far0, in_place)
+    have.update(x=far0, h=handed0)
+    other1 = swapped(after(far[1], *[have[c] for c in OPT["s1"]]))
+    far1, end = project(
+        far_here, [own_set, outer_set], far, [other0, other1], [[1], [0, 1]]
     )
-    pieces, places = [], []
-    for cross in range(2):
-        side = (core + cross) % 2
-        by_step = [handed[cross][:, i * half : (i + 1) * half] for i in range(3)]
-        end = handed_end[cross]
-        by_step = [
-            by_step[0],
-            jnp.where(own == 3, end, by_step[1]),
-            handed_far[cross],
-            jnp.where(own == 0, end, by_step[2]),
+    parts = [handed0, handed_on(far1, in_place), handed_on(end, from_inner)]
+
+    is_end = (own == 0) | (own == 3)
+    blocks = chunk // CAUSAL_BLOCK
+    far_at = (own + 2) % 4 * blocks
+    end_at = jnp.where(is_end, 3 - own, (own + 2) % 4) * blocks
+    places = jnp.stack(
+        [
+            is_end.astype(jnp.int32),
+            far_at,
+            end_at,
+            own * blocks,
+            (own + 3 + 2 * core) % 4 * blocks,
+            (own + 1 + 2 * core) % 4 * blocks,
         ]
-        for step, piece in enumerate(by_step):
-            pieces.append(piece)
-            places.append((own + step) % 4 * 2 + side)
+    ).astype(jnp.int32)
+    whole = pl.BlockSpec(memory_space=pltpu.VMEM)
     passed = pl.pallas_call(
         place_kernel,
-        in_specs=[pl.BlockSpec(memory_space=pltpu.SMEM)]
-        + [pl.BlockSpec(memory_space=pltpu.VMEM)] * 8,
-        out_specs=pl.BlockSpec(memory_space=pltpu.VMEM),
-        out_shape=jax.ShapeDtypeStruct((patches, 8 * half), bf16),
+        in_specs=[pl.BlockSpec(memory_space=pltpu.SMEM)] + [whole] * (1 + len(parts)),
+        out_specs=whole,
+        out_shape=jax.ShapeDtypeStruct((patches, 4 * chunk), bf16),
         name="placed",
-    )(jnp.stack(places).astype(jnp.int32), *pieces)
-    return passed.reshape(1, 1, 1, patches, 8 * half)
+    )(places, first, *parts)
+    return passed.reshape(1, 1, 1, patches, 4 * chunk)
 
 
 def solution(mesh):

time: 203 us -> 186 us (0.916)
  waiting for transfers between devices: 95.4 us -> 65.3 us
  starting transfers between devices: 56.9 us -> 68.3 us
  Pallas kernels: 24.5 us -> 35.3 us
  matrix products: 4.7 us -> 0 us
  local copies, waits for them, and re-layouts: 16.8 us -> 13 us
    ppermute x9, waiting for transfers between devices: 62.3 us -> 38.9 us  [passed_along(): return lax.ppermute(block, axis, route)]
    ppermute x4, starting transfers between devices: 0.8 us -> 15.3 us  [swapped(): return lax.ppermute(block, 'dp', [(0, 1), (1, 0)])]
    pallas_call x0 -> x3, Pallas kernels: none -> 10.9 us  [project(): pl.pallas_call(functools.partial(project_kernel, uses, len(token_sets), l...]
    ppermute x1, waiting for transfers between devices: 7.25 us -> 0.01 us  [shards(): outer_query = lax.ppermute(query_grad, 'var', inward)]
    ppermute x19 -> x9, starting transfers between devices: 36.7 us -> 31.1 us  [the longest x4 19.4 us: on_line(): lax.ppermute(block, ('var', 'dp'), [(a * 2 + c, b * 2 + d) for (a, c), (b...]
    slice x3 -> x4, local copies, waits for them, and re-layouts: 0.09 us -> 5.06 us  [the longest x2 2.22 us: send_near(): near.append(on_line(after(weight[slice(*cuts[i])], *values), step_near))]
    dot_general x3 -> x0, matrix products: 4.7 us -> none  [dot_nt(): lax.dot_general(a, b, (((1,), (1,)), ((), ())), preferred_element_type=f32)]
    dynamic_slice x2 -> x0, local copies, waits for them, and re-layouts: 4.12 us -> none  [start(): piece = lax.dynamic_slice_in_dim(weight, core * half + lo, hi - lo, 0)]
  transfers between devices with their start and end apart: 33 -> 23, of which waited for: 14 -> 13; matrix products, arithmetic and copies ran while one was open for 10% -> 5% of each run, Pallas kernels for 11% -> 17%
where the time goes in v2:
time: 186 us
  starting transfers between devices  68.3 us (37%)
  waiting for transfers between devices  65.3 us (35%)
  Pallas kernels  35.3 us (19%)
  local copies, waits for them, and re-layouts  13 us (7%)
  other arithmetic  3.52 us (2%)
    ppermute x9, waiting for transfers between devices, passed_along(): return lax.ppermute(block, axis, route)  38.9 us
    ppermute x4, starting transfers between devices, on_line(): lax.ppermute(block, ('var', 'dp'), [(a * 2 + c, b * 2 + d) for (a, c), (b...  19.4 us
    ppermute x9, starting transfers between devices, passed_along(): return lax.ppermute(block, axis, route)  17.1 us
    ppermute x4, starting transfers between devices, swapped(): return lax.ppermute(block, 'dp', [(0, 1), (1, 0)])  15.3 us
    pallas_call x1, Pallas kernels, block_grads(): pl.pallas_call(functools.partial(grads_kernel, n, window, head_size, scal...  14.5 us
    pallas_call x3, Pallas kernels, project(): pl.pallas_call(functools.partial(project_kernel, uses, len(token_sets), l...  10.9 us
    ppermute x4, waiting for transfers between devices, on_line(): lax.ppermute(block, ('var', 'dp'), [(a * 2 + c, b * 2 + d) for (a, c), (b...  10.7 us
    ppermute x4, waiting for transfers between devices, handed_on(): return lax.ppermute(block, ('var', 'segment'), route)  10.5 us
  transfers between devices with their start and end apart: 23, of which 13 were waited for; matrix products, arithmetic and copies ran while one was open for 5% of the time, Pallas kernels for 17%

profile of v2, /device:TPU:0, one launch (start us, length us, event | category | flops | bytes accessed | tf_op | source)
XLA Modules:
  0.0 185.7 jit_solution(16955140560263212933)
XLA Ops:
  0.0 5.0 %collective-permute-start = (bf16[256,1024]{1,0:T(8,128)(2,1)}, bf16[256,1024]{1,0:T(8,128)(2,1)S(1)}, u32[]{:S(2)}, u32[]{:S(2)}) collective-permute-start(bf16[256,1024]{1,0:T(8,128)(2,1)} %bitcast.43), channel_id=1, source_target_pairs={{8,0},{16,8},{24,16},{0,24},{9,1},{17,9},{25,17},{1,25},{10,2},{18... | collective-permute-start | bytes 1572872 | tf_op jit(solution)/shard_map/ppermute | solution.py:25
  5.1 3.8 %collective-permute-start.1 = (bf16[256,1024]{1,0:T(8,128)(2,1)}, bf16[256,1024]{1,0:T(8,128)(2,1)}, u32[]{:S(2)}, u32[]{:S(2)}) collective-permute-start(bf16[256,1024]{1,0:T(8,128)(2,1)} %bitcast.47), channel_id=1, source_target_pairs={{8,0},{16,8},{24,16},{0,24},{9,1},{17,9},{25,17},{1,25},{10,2},{18... | collective-permute-start | bytes 1572872 | tf_op jit(solution)/shard_map/ppermute | solution.py:25
  8.9 2.1 %slice_bitcast_fusion.1 = bf16[128,3072]{1,0:T(8,128)(2,1)} fusion(bf16[1,512,3072]{2,1,0:T(8,128)(2,1)} %param.11), kind=kLoop, calls=%fused_computation.4 | loop fusion | bytes 1572864 | tf_op jit(solution)/shard_map/slice | solution.py:386
  10.9 0.7 compare_select_fusion
  12.3 5.4 %collective-permute-done.refs_0_.refs_2_ = bf16[256,1024]{1,0:T(8,128)(2,1)S(1)} collective-permute-done((bf16[256,1024]{1,0:T(8,128)(2,1)}, bf16[256,1024]{1,0:T(8,128)(2,1)S(1)}, u32[]{:S(2)}, u32[]{:S(2)}) %collective-permute-start) | collective-permute-done | bytes 524320 | tf_op jit(solution)/shard_map/ppermute | solution.py:25
  17.7 13.3 %collective-permute-start.4 = (bf16[128,3072]{1,0:T(8,128)(2,1)}, bf16[128,3072]{1,0:T(8,128)(2,1)}, u32[]{:S(2)}, u32[]{:S(2)}) collective-permute-start(bf16[128,3072]{1,0:T(8,128)(2,1)} %slice_bitcast_fusion.1), channel_id=1, source_target_pairs={{0,8},{8,16},{16,24},{12,4},{20,12},{28,20},{1,9},{9,17},{17,25},{... | collective-permute-start | bytes 2359304 | tf_op jit(solution)/shard_map/ppermute | solution.py:303
  31.0 1.0 copy-done.3
  32.1 1.0 copy-done.5
  33.1 1.0 copy-done.7
  34.1 1.0 copy-done.9
  35.2 2.5 %row_stats.2.refs_6_ = f32[4,8,256]{2,1,0:T(8,128)S(1)} custom-call(s32[1]{0:T(128)S(1)} %bitcast.51, bf16[256,1024]{1,0:T(8,128)(2,1)S(1)} %bitcast.37, bf16[256,1024]{1,0:T(8,128)(2,1)S(1)} %bitcast.40, bf16[256,1024]{1,0:T(8,128)(2,1)S(1)} %bitcast.45, bf16[256,1024]{1,0:T(8,128)(2,1)S(1)} %bitcast.49), custom_call_target="tpu_custom_call" | custom-call | flops 2875000064 | bytes 1024 | tf_op jit(solution)/shard_map/row_stats/pallas_call | solution.py:177
  37.8 2.4 %collective-permute-done.1.refs_1_.refs_3_ = bf16[256,1024]{1,0:T(8,128)(2,1)} collective-permute-done((bf16[256,1024]{1,0:T(8,128)(2,1)}, bf16[256,1024]{1,0:T(8,128)(2,1)}, u32[]{:S(2)}, u32[]{:S(2)}) %collective-permute-start.1) | collective-permute-done | bytes 524320 | tf_op jit(solution)/shard_map/ppermute | solution.py:25
  40.2 12.2 %collective-permute-done.3.refs_3_.refs_5_ = bf16[256,1024]{1,0:T(8,128)(2,1)} collective-permute-done((bf16[256,1024]{1,0:T(8,128)(2,1)}, bf16[256,1024]{1,0:T(8,128)(2,1)}, u32[]{:S(2)}, u32[]{:S(2)}) %collective-permute-start.3) | collective-permute-done | bytes 524320 | tf_op jit(solution)/shard_map/ppermute | solution.py:25
  52.4 1.0 copy-done.12
  53.4 5.0 %row_stats.3 = (f32[4,8,256]{2,1,0:T(8,128)S(1)}, f32[4,8,256]{2,1,0:T(8,128)S(1)}) custom-call(s32[2]{0:T(128)S(1)} %slice.43.linked_ref, bf16[256,1024]{1,0:T(8,128)(2,1)S(1)} %bitcast.38, bf16[256,1024]{1,0:T(8,128)(2,1)S(1)} %bitcast.41, bf16[256,1024]{1,0:T(8,128)(2,1)S(1)} %copy-done.12, bf16[256,1024]{1,0:T(8,128)(2,1)} %collective-permute-done.1.refs_1_.refs_3_, ...), custom_call_target="tpu_custom_call" | custom-call | flops 5750000128 | bytes 1024 | tf_op jit(solution)/shard_map/row_stats/pallas_call | solution.py:177
  58.8 2.6 %collective-permute-start.5 = (f32[2,4,8,256]{3,2,1,0:T(8,128)S(1)}, f32[2,4,8,256]{3,2,1,0:T(8,128)S(1)}, u32[]{:S(2)}, u32[]{:S(2)}) collective-permute-start(f32[2,4,8,256]{3,2,1,0:T(8,128)S(1)} %get-tuple-element.28), channel_id=1, source_target_pairs={{8,0},{16,8},{24,16},{0,24},{9,1},{17,9},{25,17},{1,25},{10,2},{18... | collective-permute-start | bytes 196616 | tf_op jit(solution)/shard_map/ppermute | solution.py:25
  61.3 1.4 collective-permute-start.7
  62.9 1.8 collective-permute-done.5
  64.7 2.7 %collective-permute-done.6 = f32[2,4,8,256]{3,2,1,0:T(8,128)S(1)} collective-permute-done((f32[2,4,8,256]{3,2,1,0:T(8,128)S(1)}, f32[2,4,8,256]{3,2,1,0:T(8,128)S(1)}, u32[]{:S(2)}, u32[]{:S(2)}) %collective-permute-start.6) | collective-permute-done | bytes 65568 | tf_op jit(solution)/shard_map/ppermute | solution.py:25
  67.4 4.6 %collective-permute-start.8 = (bf16[384,3072]{1,0:T(8,128)(2,1)S(1)}, bf16[384,3072]{1,0:T(8,128)(2,1)}, u32[]{:S(2)}, u32[]{:S(2)}) collective-permute-start(bf16[384,3072]{1,0:T(8,128)(2,1)S(1)} %slice_bitcast_fusion), channel_id=1, source_target_pairs={{0,8},{8,16},{16,24},{12,4},{20,12},{28,20},{1,9},{9,17},{17,25},{... | collective-permute-start | bytes 7077896 | tf_op jit(solution)/shard_map/ppermute | solution.py:303
  72.1 14.5 %block_grads.1 = (f32[256,1024]{1,0:T(8,128)}, bf16[256,1024]{1,0:T(8,128)(2,1)}, bf16[256,1024]{1,0:T(8,128)(2,1)}, bf16[2,256,1024]{2,1,0:T(8,128)(2,1)}) custom-call(s32[3]{0:T(128)S(1)} %convert_element_type.14.linked_ref, bf16[256,1024]{1,0:T(8,128)(2,1)S(1)} %bitcast.39, bf16[256,1024]{1,0:T(8,128)(2,1)S(1)} %bitcast.42, ...), custom_call_target="tpu_custom_call" | custom-call | flops 16560000000 | bytes 1024 | tf_op jit(solution)/shard_map/block_grads/pallas_call | solution.py:197
  86.6 10.4 %collective-permute-done.8.refs_4_ = bf16[384,3072]{1,0:T(8,128)(2,1)} collective-permute-done((bf16[384,3072]{1,0:T(8,128)(2,1)S(1)}, bf16[384,3072]{1,0:T(8,128)(2,1)}, u32[]{:S(2)}, u32[]{:S(2)}) %collective-permute-start.8) | collective-permute-done | bytes 2359328 | tf_op jit(solution)/shard_map/ppermute | solution.py:303
  96.9 4.3 %collective-permute-start.10 = (bf16[256,1024]{1,0:T(8,128)(2,1)}, bf16[256,1024]{1,0:T(8,128)(2,1)}, u32[]{:S(2)}, u32[]{:S(2)}) collective-permute-start(bf16[256,1024]{1,0:T(8,128)(2,1)} %get-tuple-element.37), channel_id=1, source_target_pairs={{8,0},{16,8},{24,16},{0,24},{9,1},{17,9},{25,17},{1,25},{10,2},{18... | collective-permute-start | bytes 1572872 | tf_op jit(solution)/shard_map/ppermute | solution.py:25
  101.4 1.5 slice.64
  102.9 1.3 slice.65
  104.3 1.2 pad_maximum_fusion
  105.5 8.3 %collective-permute-done.10 = bf16[256,1024]{1,0:T(8,128)(2,1)} collective-permute-done((bf16[256,1024]{1,0:T(8,128)(2,1)}, bf16[256,1024]{1,0:T(8,128)(2,1)}, u32[]{:S(2)}, u32[]{:S(2)}) %collective-permute-start.10) | collective-permute-done | bytes 524320 | tf_op jit(solution)/shard_map/ppermute | solution.py:25
  113.8 0.7 collective-permute-start.14
  114.5 4.8 %collective-permute-start.15 = (bf16[2,256,1024]{2,1,0:T(8,128)(2,1)S(1)}, bf16[2,256,1024]{2,1,0:T(8,128)(2,1)S(1)}, u32[]{:S(2)}, u32[]{:S(2)}) collective-permute-start(bf16[2,256,1024]{2,1,0:T(8,128)(2,1)S(1)} %copy-done.2), channel_id=1, source_target_pairs={{0,8},{24,16},{1,9},{25,17},{2,10},{26,18},{3,11},{27,19},{4,12},{... | collective-permute-start | bytes 3145736 | tf_op jit(solution)/shard_map/ppermute | solution.py:438
  119.4 6.2 %collective-permute-done.9 = bf16[256,1024]{1,0:T(8,128)(2,1)} collective-permute-done((bf16[256,1024]{1,0:T(8,128)(2,1)}, bf16[256,1024]{1,0:T(8,128)(2,1)}, u32[]{:S(2)}, u32[]{:S(2)}) %collective-permute-start.9) | collective-permute-done | bytes 524320 | tf_op jit(solution)/shard_map/ppermute | solution.py:25
  125.5 0.8 collective-permute-start.19
  126.3 1.5 add_convert_fusion.refs_0_
  127.8 8.6 %project.3 = bf16[256,1536]{1,0:T(8,128)(2,1)S(1)} custom-call(s32[1]{0:T(128)} %bitcast.6.flag_ref, bf16[256,1024]{1,0:T(8,128)(2,1)S(1)} %add_convert_fusion.refs_0_, bf16[2,256,1024]{2,1,0:T(8,128)(2,1)S(1)} %copy-done.2, bf16[512,3072]{1,0:T(8,128)(2,1)S(1)} %bitcast.33, bf16[128,3072]{1,0:T(8,128)(2,1)} %collective-permute-done.4.refs_3_, ...), custom_call_target="tpu_custom_call" | custom-call | flops 8215600128 | bytes 1024 | tf_op jit(solution)/shard_map/project/pallas_call | solution.py:281
  136.4 2.5 %collective-permute-start.13 = (bf16[256,1536]{1,0:T(8,128)(2,1)S(1)}, bf16[256,1536]{1,0:T(8,128)(2,1)S(1)}, u32[]{:S(2)}, u32[]{:S(2)}) collective-permute-start(bf16[256,1536]{1,0:T(8,128)(2,1)S(1)} %project.3), channel_id=1, source_target_pairs={{0,3},{1,0},{2,1},{3,2},{8,11},{9,8},{10,9},{11,10},{16,19},{17,16... | collective-permute-start | bytes 2359304 | tf_op jit(solution)/shard_map/ppermute | solution.py:444
  138.9 4.8 %collective-permute-start.16 = (bf16[256,1024]{1,0:T(8,128)(2,1)S(1)}, bf16[256,1024]{1,0:T(8,128)(2,1)S(1)}, u32[]{:S(2)}, u32[]{:S(2)}) collective-permute-start(bf16[256,1024]{1,0:T(8,128)(2,1)S(1)} %add_convert_fusion.refs_0_), channel_id=1, source_target_pairs={{0,8},{24,16},{1,9},{25,17},{2,10},{26,18},{3,11},{27,19},{4,12},{... | collective-permute-start | bytes 1572872 | tf_op jit(solution)/shard_map/ppermute | solution.py:439
  143.7 15.0 %collective-permute-start.20 = (bf16[256,3072]{1,0:T(8,128)(2,1)S(1)}, bf16[256,3072]{1,0:T(8,128)(2,1)S(1)}, u32[]{:S(2)}, u32[]{:S(2)}) collective-permute-start(bf16[256,3072]{1,0:T(8,128)(2,1)S(1)} %collective-permute-done.19.refs_5_), channel_id=1, source_target_pairs={{0,4},{4,0},{1,5},{5,1},{2,6},{6,2},{3,7},{7,3},{8,12},{12,8},{9,1... | collective-permute-start | bytes 4718600 | tf_op jit(solution)/shard_map/ppermute | solution.py:299
  158.8 2.9 %collective-permute-done.20.refs_7_ = bf16[256,3072]{1,0:T(8,128)(2,1)S(1)} collective-permute-done((bf16[256,3072]{1,0:T(8,128)(2,1)S(1)}, bf16[256,3072]{1,0:T(8,128)(2,1)S(1)}, u32[]{:S(2)}, u32[]{:S(2)}) %collective-permute-start.20) | collective-permute-done | bytes 1572896 | tf_op jit(solution)/shard_map/ppermute | solution.py:299
  161.8 2.2 %collective-permute-done.17.refs_3_.refs_6_ = bf16[256,3072]{1,0:T(8,128)(2,1)S(1)} collective-permute-done((bf16[256,3072]{1,0:T(8,128)(2,1)S(1)}, bf16[256,3072]{1,0:T(8,128)(2,1)S(1)}, u32[]{:S(2)}, u32[]{:S(2)}) %collective-permute-start.17) | collective-permute-done | bytes 1572896 | tf_op jit(solution)/shard_map/ppermute | solution.py:299
  164.0 1.6 project.5
  165.7 1.3 collective-permute-start.22
  167.0 0.6 project.4
  167.6 2.5 %collective-permute-start.18 = (bf16[256,256]{1,0:T(8,128)(2,1)S(1)}, bf16[256,256]{1,0:T(8,128)(2,1)S(1)}, u32[]{:S(2)}, u32[]{:S(2)}) collective-permute-start(bf16[256,256]{1,0:T(8,128)(2,1)S(1)} %project.4), channel_id=1, source_target_pairs={{0,3},{1,0},{2,1},{3,2},{8,11},{9,8},{10,9},{11,10},{16,19},{17,16... | collective-permute-start | bytes 393224 | tf_op jit(solution)/shard_map/ppermute | solution.py:444
  170.6 0.7 stack.52.at_ref
  171.3 8.3 %collective-permute-done.18.refs_0_ = bf16[256,256]{1,0:T(8,128)(2,1)S(1)} collective-permute-done((bf16[256,256]{1,0:T(8,128)(2,1)S(1)}, bf16[256,256]{1,0:T(8,128)(2,1)S(1)}, u32[]{:S(2)}, u32[]{:S(2)}) %collective-permute-start.18) | collective-permute-done | bytes 131104 | tf_op jit(solution)/shard_map/ppermute | solution.py:444
  179.6 2.3 %collective-permute-done.21.refs_1_ = bf16[256,256]{1,0:T(8,128)(2,1)S(1)} collective-permute-done((bf16[256,256]{1,0:T(8,128)(2,1)S(1)}, bf16[256,256]{1,0:T(8,128)(2,1)S(1)}, u32[]{:S(2)}, u32[]{:S(2)}) %collective-permute-start.21) | collective-permute-done | bytes 131104 | tf_op jit(solution)/shard_map/ppermute | solution.py:444
  181.8 0.6 copy-done.17
  182.5 0.7 copy-done.15
  183.2 2.5 %placed.1 = bf16[256,2048]{1,0:T(8,128)(2,1)} custom-call(s32[6]{0:T(128)} %stack.52.at_ref, bf16[256,1536]{1,0:T(8,128)(2,1)} %copy-done.14, bf16[256,256]{1,0:T(8,128)(2,1)} %copy-done.16, bf16[256,256]{1,0:T(8,128)(2,1)} %copy-done.17, bf16[256,512]{1,0:T(8,128)(2,1)} %copy-done.15), custom_call_target="tpu_custom_call" | custom-call | tf_op jit(solution)/shard_map/placed/pallas_call | solution.py:482
  (58 shorter events, 2.2 us)
Async XLA Ops:
  0.0 11.6 %copy-start = (s32[4,3]{1,0:T(4,128)S(1)}, s32[4,3]{1,0:T(4,128)}, u32[]{:S(2)}) copy-start(s32[4,3]{1,0:T(4,128)} %param.12) | copy-start | bytes 148
  0.0 17.7 %collective-permute-start = (bf16[256,1024]{1,0:T(8,128)(2,1)}, bf16[256,1024]{1,0:T(8,128)(2,1)S(1)}, u32[]{:S(2)}, u32[]{:S(2)}) collective-permute-start(bf16[256,1024]{1,0:T(8,128)(2,1)} %bitcast.43), channel_id=1, source_target_pairs={{8,0},{16,8},{24,16},{0,24},{9,1},{17,9},{25,17},{1,25},{10,2},{18... | collective-permute-start | bytes 1572872 | tf_op jit(solution)/shard_map/ppermute | solution.py:25
  5.1 35.2 %collective-permute-start.2 = (bf16[256,1024]{1,0:T(8,128)(2,1)}, bf16[256,1024]{1,0:T(8,128)(2,1)}, u32[]{:S(2)}, u32[]{:S(2)}) collective-permute-start(bf16[256,1024]{1,0:T(8,128)(2,1)} %bitcast.44), channel_id=1, source_target_pairs={{24,0},{0,8},{8,16},{16,24},{25,1},{1,9},{9,17},{17,25},{26,2},{2,... | collective-permute-start | bytes 1572872 | tf_op jit(solution)/shard_map/ppermute | solution.py:25
  5.1 35.2 %collective-permute-start.1 = (bf16[256,1024]{1,0:T(8,128)(2,1)}, bf16[256,1024]{1,0:T(8,128)(2,1)}, u32[]{:S(2)}, u32[]{:S(2)}) collective-permute-start(bf16[256,1024]{1,0:T(8,128)(2,1)} %bitcast.47), channel_id=1, source_target_pairs={{8,0},{16,8},{24,16},{0,24},{9,1},{17,9},{25,17},{1,25},{10,2},{18... | collective-permute-start | bytes 1572872 | tf_op jit(solution)/shard_map/ppermute | solution.py:25
  8.9 43.5 %collective-permute-start.3 = (bf16[256,1024]{1,0:T(8,128)(2,1)}, bf16[256,1024]{1,0:T(8,128)(2,1)}, u32[]{:S(2)}, u32[]{:S(2)}) collective-permute-start(bf16[256,1024]{1,0:T(8,128)(2,1)} %bitcast.48), channel_id=1, source_target_pairs={{24,0},{0,8},{8,16},{16,24},{25,1},{1,9},{9,17},{17,25},{26,2},{2,... | collective-permute-start | bytes 1572872 | tf_op jit(solution)/shard_map/ppermute | solution.py:25
  17.7 20.0 %copy-start.11 = (bf16[256,1024]{1,0:T(8,128)(2,1)}, bf16[256,1024]{1,0:T(8,128)(2,1)S(1)}, u32[]{:S(2)}) copy-start(bf16[256,1024]{1,0:T(8,128)(2,1)S(1)} %collective-permute-done.refs_0_.refs_2_) | copy-start | bytes 1572868
  17.7 41.1 %collective-permute-start.4 = (bf16[128,3072]{1,0:T(8,128)(2,1)}, bf16[128,3072]{1,0:T(8,128)(2,1)}, u32[]{:S(2)}, u32[]{:S(2)}) collective-permute-start(bf16[128,3072]{1,0:T(8,128)(2,1)} %slice_bitcast_fusion.1), channel_id=1, source_target_pairs={{0,8},{8,16},{16,24},{12,4},{20,12},{28,20},{1,9},{9,17},{17,25},{... | collective-permute-start | bytes 2359304 | tf_op jit(solution)/shard_map/ppermute | solution.py:303
  31.0 1.0 copy-start.3
  32.1 1.0 copy-start.5
  33.1 1.0 copy-start.7
  34.1 1.0 copy-start.9
  35.2 17.2 %copy-start.4 = (bf16[1,1,1,256,1024]{4,3,2,1,0:T(8,128)(2,1)S(1)}, bf16[1,1,1,256,1024]{4,3,2,1,0:T(8,128)(2,1)}, u32[]{:S(2)}) copy-start(bf16[1,1,1,256,1024]{4,3,2,1,0:T(8,128)(2,1)} %param.8) | copy-start | bytes 1572868
  35.2 17.2 %copy-start.6 = (bf16[1,1,1,256,1024]{4,3,2,1,0:T(8,128)(2,1)S(1)}, bf16[1,1,1,256,1024]{4,3,2,1,0:T(8,128)(2,1)}, u32[]{:S(2)}) copy-start(bf16[1,1,1,256,1024]{4,3,2,1,0:T(8,128)(2,1)} %param.9) | copy-start | bytes 1572868
  37.8 24.9 %copy-start.1 = (bf16[1,512,3072]{2,1,0:T(8,128)(2,1)S(1)}, bf16[1,512,3072]{2,1,0:T(8,128)(2,1)}, u32[]{:S(2)}) copy-start(bf16[1,512,3072]{2,1,0:T(8,128)(2,1)} %param.11) | copy-start | bytes 9437188
  52.4 1.0 copy-start.12
  58.8 5.9 %collective-permute-start.5 = (f32[2,4,8,256]{3,2,1,0:T(8,128)S(1)}, f32[2,4,8,256]{3,2,1,0:T(8,128)S(1)}, u32[]{:S(2)}, u32[]{:S(2)}) collective-permute-start(f32[2,4,8,256]{3,2,1,0:T(8,128)S(1)} %get-tuple-element.28), channel_id=1, source_target_pairs={{8,0},{16,8},{24,16},{0,24},{9,1},{17,9},{25,17},{1,25},{10,2},{18... | collective-permute-start | bytes 196616 | tf_op jit(solution)/shard_map/ppermute | solution.py:25
  61.3 6.1 %collective-permute-start.6 = (f32[2,4,8,256]{3,2,1,0:T(8,128)S(1)}, f32[2,4,8,256]{3,2,1,0:T(8,128)S(1)}, u32[]{:S(2)}, u32[]{:S(2)}) collective-permute-start(f32[2,4,8,256]{3,2,1,0:T(8,128)S(1)} %get-tuple-element.30), channel_id=1, source_target_pairs={{24,0},{0,8},{8,16},{16,24},{25,1},{1,9},{9,17},{17,25},{26,2},{2,... | collective-permute-start | bytes 196616 | tf_op jit(solution)/shard_map/ppermute | solution.py:25
  61.3 10.7 %copy-start.8 = (bf16[1,1,1,256,1024]{4,3,2,1,0:T(8,128)(2,1)S(1)}, bf16[1,1,1,256,1024]{4,3,2,1,0:T(8,128)(2,1)}, u32[]{:S(2)}) copy-start(bf16[1,1,1,256,1024]{4,3,2,1,0:T(8,128)(2,1)} %param.7) | copy-start | bytes 1572868
  61.3 10.7 %copy-start.10 = (bf16[1,1,1,256,1024]{4,3,2,1,0:T(8,128)(2,1)S(1)}, bf16[1,1,1,256,1024]{4,3,2,1,0:T(8,128)(2,1)}, u32[]{:S(2)}) copy-start(bf16[1,1,1,256,1024]{4,3,2,1,0:T(8,128)(2,1)} %param.10) | copy-start | bytes 1572868
  61.3 6.1 %collective-permute-start.7 = (f32[2,4,8,256]{3,2,1,0:T(8,128)S(1)}, f32[2,4,8,256]{3,2,1,0:T(8,128)S(1)}, u32[]{:S(2)}, u32[]{:S(2)}) collective-permute-start(f32[2,4,8,256]{3,2,1,0:T(8,128)S(1)} %get-tuple-element.31), channel_id=1, source_target_pairs={{16,0},{24,8},{0,16},{8,24},{17,1},{25,9},{1,17},{9,25},{18,2},{26... | collective-permute-start | bytes 196616 | tf_op jit(solution)/shard_map/ppermute | solution.py:25
  67.4 29.5 %collective-permute-start.8 = (bf16[384,3072]{1,0:T(8,128)(2,1)S(1)}, bf16[384,3072]{1,0:T(8,128)(2,1)}, u32[]{:S(2)}, u32[]{:S(2)}) collective-permute-start(bf16[384,3072]{1,0:T(8,128)(2,1)S(1)} %slice_bitcast_fusion), channel_id=1, source_target_pairs={{0,8},{8,16},{16,24},{12,4},{20,12},{28,20},{1,9},{9,17},{17,25},{... | collective-permute-start | bytes 7077896 | tf_op jit(solution)/shard_map/ppermute | solution.py:303
  96.9 30.9 %collective-permute-start.12 = (bf16[384,3072]{1,0:T(8,128)(2,1)}, bf16[384,3072]{1,0:T(8,128)(2,1)}, u32[]{:S(2)}, u32[]{:S(2)}) collective-permute-start(bf16[384,3072]{1,0:T(8,128)(2,1)} %collective-permute-done.8.refs_4_), channel_id=1, source_target_pairs={{0,4},{4,0},{1,5},{5,1},{2,6},{6,2},{3,7},{7,3},{8,12},{12,8},{9,1... | collective-permute-start | bytes 7077896 | tf_op jit(solution)/shard_map/ppermute | solution.py:299
  96.9 16.9 %collective-permute-start.10 = (bf16[256,1024]{1,0:T(8,128)(2,1)}, bf16[256,1024]{1,0:T(8,128)(2,1)}, u32[]{:S(2)}, u32[]{:S(2)}) collective-permute-start(bf16[256,1024]{1,0:T(8,128)(2,1)} %get-tuple-element.37), channel_id=1, source_target_pairs={{8,0},{16,8},{24,16},{0,24},{9,1},{17,9},{25,17},{1,25},{10,2},{18... | collective-permute-start | bytes 1572872 | tf_op jit(solution)/shard_map/ppermute | solution.py:25
  101.2 24.4 %collective-permute-start.9 = (bf16[256,1024]{1,0:T(8,128)(2,1)}, bf16[256,1024]{1,0:T(8,128)(2,1)}, u32[]{:S(2)}, u32[]{:S(2)}) collective-permute-start(bf16[256,1024]{1,0:T(8,128)(2,1)} %get-tuple-element.35), channel_id=1, source_target_pairs={{24,0},{0,8},{8,16},{16,24},{25,1},{1,9},{9,17},{17,25},{26,2},{2,... | collective-permute-start | bytes 1572872 | tf_op jit(solution)/shard_map/ppermute | solution.py:25
  101.2 26.6 %collective-permute-start.11 = (bf16[128,3072]{1,0:T(8,128)(2,1)}, bf16[128,3072]{1,0:T(8,128)(2,1)}, u32[]{:S(2)}, u32[]{:S(2)}) collective-permute-start(bf16[128,3072]{1,0:T(8,128)(2,1)} %collective-permute-done.4.refs_3_), channel_id=1, source_target_pairs={{0,4},{4,0},{1,5},{5,1},{2,6},{6,2},{3,7},{7,3},{8,12},{12,8},{9,1... | collective-permute-start | bytes 2359304 | tf_op jit(solution)/shard_map/ppermute | solution.py:299
  102.9 11.6 %copy-start.2 = (bf16[2,256,1024]{2,1,0:T(8,128)(2,1)S(1)}, bf16[2,256,1024]{2,1,0:T(8,128)(2,1)}, u32[]{:S(2)}) copy-start(bf16[2,256,1024]{2,1,0:T(8,128)(2,1)} %get-tuple-element.42.refs_1_) | copy-start | bytes 3145732
  102.9 23.4 %copy-start.13 = (f32[256,1024]{1,0:T(8,128)S(1)}, f32[256,1024]{1,0:T(8,128)}, u32[]{:S(2)}) copy-start(f32[256,1024]{1,0:T(8,128)} %get-tuple-element.32) | copy-start | bytes 3145732
  113.8 45.0 %collective-permute-start.14 = (bf16[256,3072]{1,0:T(8,128)(2,1)S(1)}, bf16[256,3072]{1,0:T(8,128)(2,1)S(1)}, u32[]{:S(2)}, u32[]{:S(2)}) collective-permute-start(bf16[256,3072]{1,0:T(8,128)(2,1)S(1)} %slice.64), channel_id=1, source_target_pairs={{8,16},{16,24},{20,12},{12,4},{9,17},{17,25},{21,13},{13,5},{10,18... | collective-permute-start | bytes 4718600 | tf_op jit(solution)/shard_map/ppermute | solution.py:303
  114.5 44.2 %collective-permute-start.15 = (bf16[2,256,1024]{2,1,0:T(8,128)(2,1)S(1)}, bf16[2,256,1024]{2,1,0:T(8,128)(2,1)S(1)}, u32[]{:S(2)}, u32[]{:S(2)}) collective-permute-start(bf16[2,256,1024]{2,1,0:T(8,128)(2,1)S(1)} %copy-done.2), channel_id=1, source_target_pairs={{0,8},{24,16},{1,9},{25,17},{2,10},{26,18},{3,11},{27,19},{4,12},{... | collective-permute-start | bytes 3145736 | tf_op jit(solution)/shard_map/ppermute | solution.py:438
  125.5 18.2 %collective-permute-start.19 = (bf16[256,3072]{1,0:T(8,128)(2,1)S(1)}, bf16[256,3072]{1,0:T(8,128)(2,1)S(1)}, u32[]{:S(2)}, u32[]{:S(2)}) collective-permute-start(bf16[256,3072]{1,0:T(8,128)(2,1)S(1)} %pad_maximum_fusion), channel_id=1, source_target_pairs={{8,16},{16,24},{20,12},{12,4},{9,17},{17,25},{21,13},{13,5},{10,18... | collective-permute-start | bytes 4718600 | tf_op jit(solution)/shard_map/ppermute | solution.py:303
  136.4 22.3 %collective-permute-start.13 = (bf16[256,1536]{1,0:T(8,128)(2,1)S(1)}, bf16[256,1536]{1,0:T(8,128)(2,1)S(1)}, u32[]{:S(2)}, u32[]{:S(2)}) collective-permute-start(bf16[256,1536]{1,0:T(8,128)(2,1)S(1)} %project.3), channel_id=1, source_target_pairs={{0,3},{1,0},{2,1},{3,2},{8,11},{9,8},{10,9},{11,10},{16,19},{17,16... | collective-permute-start | bytes 2359304 | tf_op jit(solution)/shard_map/ppermute | solution.py:444
  138.9 19.8 %collective-permute-start.16 = (bf16[256,1024]{1,0:T(8,128)(2,1)S(1)}, bf16[256,1024]{1,0:T(8,128)(2,1)S(1)}, u32[]{:S(2)}, u32[]{:S(2)}) collective-permute-start(bf16[256,1024]{1,0:T(8,128)(2,1)S(1)} %add_convert_fusion.refs_0_), channel_id=1, source_target_pairs={{0,8},{24,16},{1,9},{25,17},{2,10},{26,18},{3,11},{27,19},{4,12},{... | collective-permute-start | bytes 1572872 | tf_op jit(solution)/shard_map/ppermute | solution.py:439
  143.7 18.0 %collective-permute-start.20 = (bf16[256,3072]{1,0:T(8,128)(2,1)S(1)}, bf16[256,3072]{1,0:T(8,128)(2,1)S(1)}, u32[]{:S(2)}, u32[]{:S(2)}) collective-permute-start(bf16[256,3072]{1,0:T(8,128)(2,1)S(1)} %collective-permute-done.19.refs_5_), channel_id=1, source_target_pairs={{0,4},{4,0},{1,5},{5,1},{2,6},{6,2},{3,7},{7,3},{8,12},{12,8},{9,1... | collective-permute-start | bytes 4718600 | tf_op jit(solution)/shard_map/ppermute | solution.py:299
  158.8 6.9 %copy-start.14 = (bf16[256,1536]{1,0:T(8,128)(2,1)}, bf16[256,1536]{1,0:T(8,128)(2,1)S(1)}, u32[]{:S(2)}) copy-start(bf16[256,1536]{1,0:T(8,128)(2,1)S(1)} %collective-permute-done.13.first_ref) | copy-start | bytes 2359300
  158.8 5.3 %collective-permute-start.17 = (bf16[256,3072]{1,0:T(8,128)(2,1)S(1)}, bf16[256,3072]{1,0:T(8,128)(2,1)S(1)}, u32[]{:S(2)}, u32[]{:S(2)}) collective-permute-start(bf16[256,3072]{1,0:T(8,128)(2,1)S(1)} %collective-permute-done.14.refs_2_.refs_4_), channel_id=1, source_target_pairs={{0,4},{4,0},{1,5},{5,1},{2,6},{6,2},{3,7},{7,3},{8,12},{12,8},{9,1... | collective-permute-start | bytes 4718600 | tf_op jit(solution)/shard_map/ppermute | solution.py:299
  165.7 16.2 %collective-permute-start.22 = (bf16[256,512]{1,0:T(8,128)(2,1)S(1)}, bf16[256,512]{1,0:T(8,128)(2,1)S(1)}, u32[]{:S(2)}, u32[]{:S(2)}) collective-permute-start(bf16[256,512]{1,0:T(8,128)(2,1)S(1)} %get-tuple-element.46), channel_id=1, source_target_pairs={{8,3},{9,0},{10,1},{11,2},{16,27},{17,24},{18,25},{19,26},{12,7},{... | collective-permute-start | bytes 786440 | tf_op jit(solution)/shard_map/ppermute | solution.py:444
  167.6 12.0 %collective-permute-start.18 = (bf16[256,256]{1,0:T(8,128)(2,1)S(1)}, bf16[256,256]{1,0:T(8,128)(2,1)S(1)}, u32[]{:S(2)}, u32[]{:S(2)}) collective-permute-start(bf16[256,256]{1,0:T(8,128)(2,1)S(1)} %project.4), channel_id=1, source_target_pairs={{0,3},{1,0},{2,1},{3,2},{8,11},{9,8},{10,9},{11,10},{16,19},{17,16... | collective-permute-start | bytes 393224 | tf_op jit(solution)/shard_map/ppermute | solution.py:444
  170.1 11.7 %collective-permute-start.21 = (bf16[256,256]{1,0:T(8,128)(2,1)S(1)}, bf16[256,256]{1,0:T(8,128)(2,1)S(1)}, u32[]{:S(2)}, u32[]{:S(2)}) collective-permute-start(bf16[256,256]{1,0:T(8,128)(2,1)S(1)} %get-tuple-element.45), channel_id=1, source_target_pairs={{0,3},{1,0},{2,1},{3,2},{8,11},{9,8},{10,9},{11,10},{16,19},{17,16... | collective-permute-start | bytes 393224 | tf_op jit(solution)/shard_map/ppermute | solution.py:444
  179.6 2.3 %copy-start.16 = (bf16[256,256]{1,0:T(8,128)(2,1)}, bf16[256,256]{1,0:T(8,128)(2,1)S(1)}, u32[]{:S(2)}) copy-start(bf16[256,256]{1,0:T(8,128)(2,1)S(1)} %collective-permute-done.18.refs_0_) | copy-start | bytes 393220
  181.8 0.7 copy-start.17
  182.5 0.7 copy-start.15

commit v3 on v2

--- a/solution.py
+++ b/solution.py
@@ -7,8 +7,6 @@
 from jax.experimental import pallas as pl
 from jax.experimental.pallas import tpu as pltpu
 from jax.sharding import PartitionSpec as P
-
-OPT = {'k1': 1, 'k2': 1, 'kp': 1, 'wa': 'first', 'st': 1, 'dq': 1, 'cb': 0, 'cuts': [128], 'nc': 'token', 'far': {0: 'lret', 1: 'lret', 2: 'lret'}, 'order': '', 'op': 'ret1', 'sf': 'rfpq', 'one': 1, 's1': '', 'ft': ['ret1', 'ret1']}
 
 HEADS = 16
 CAUSAL_BLOCK = 128
@@ -181,7 +179,7 @@
         out_specs=[stat] * n,
         out_shape=[jax.ShapeDtypeStruct((groups, 2 * GROUP, patches), f32)] * n,
         compiler_params=pltpu.CompilerParams(vmem_limit_bytes=48 * 2**20),
-        cost_estimate=spent(OPT["k1"] * 2.5 * n),
+        cost_estimate=spent(0.025 * n),
         name="row_stats",
     )(linked, keys, values, *[x for pair in pairs for x in pair])
 
@@ -203,7 +201,7 @@
         + [shape((patches, features), bf16)] * (n - 1)
         + [shape((2, patches, features), bf16)],
         compiler_params=pltpu.CompilerParams(vmem_limit_bytes=48 * 2**20),
-        cost_estimate=spent(OPT["k2"] * 4.8 * n),
+        cost_estimate=spent(48 * n),
         name="block_grads",
     )(
         linked,
@@ -214,31 +212,32 @@
     )
 
 
-def place_kernel(at_ref, first_ref, *refs):
-    out_ref = refs[-1]
-    chunk = first_ref.shape[1] // 3
-
-    def put(at, value):
-        col = pl.multiple_of(at * CAUSAL_BLOCK, CAUSAL_BLOCK)
-        out_ref[:, pl.ds(col, value.shape[1])] = value
-
-    def put_rolled(at, pieces):
-        parts = [
-            ref[:, i : i + CAUSAL_BLOCK]
-            for ref in pieces
-            for i in range(0, ref.shape[1], CAUSAL_BLOCK)
-        ]
-        for i, part in enumerate(parts):
-            put(at + (i + 1) % len(parts), part)
-
-    for i in range(3):
-        put(at_ref[3 + i], first_ref[:, i * chunk : (i + 1) * chunk])
-    far0_ref, far1_ref, end_ref = refs[:-1]
-    put_rolled(at_ref[1], [far0_ref, far1_ref])
-
-    @pl.when(at_ref[0] != 0)
-    def _():
-        put_rolled(at_ref[2], [end_ref])
+def place_kernel(roll, first_ref, *refs):
+    far_refs, end_ref, out_ref = refs[:-2], refs[-2], refs[-1]
+    chunk = end_ref.shape[1]
+    own, core = lax.axis_index("var"), lax.axis_index("dp")
+    is_end = (own == 0) | (own == 3)
+
+    def put(ref, start, width, at, shift):
+        col = pl.multiple_of(at * chunk + shift, CAUSAL_BLOCK)
+        out_ref[:, pl.ds(col, width)] = ref[:, start : start + width]
+
+    def put_rolled(pieces, at):
+        shift = roll
+        for ref in pieces:
+            width = ref.shape[1]
+            edge = min(width, chunk - shift)
+            put(ref, 0, edge, at, shift)
+            if edge < width:
+                put(ref, edge, width - edge, at, 0)
+            shift += width
+
+    for i, at in enumerate(
+        [own, lax.rem(own + 3 + 2 * core, 4), lax.rem(own + 1 + 2 * core, 4)]
+    ):
+        put(first_ref, i * chunk, chunk, at, 0)
+    put_rolled(far_refs, lax.rem(own + 2, 4))
+    pl.when(is_end)(lambda: put_rolled([end_ref], 3 - own))
 
 
 def project_kernel(uses, sets, pieces, swaps, flag_ref, *refs):
@@ -286,7 +285,7 @@
         out_specs=[whole] * len(token_sets),
         out_shape=[jax.ShapeDtypeStruct((patches, width), bf16) for width in widths],
         compiler_params=pltpu.CompilerParams(vmem_limit_bytes=32 * 2**20),
-        cost_estimate=spent(OPT["kp"] * (1 + 0.004 * sum(widths))),
+        cost_estimate=spent(1 + 0.004 * sum(widths)),
         name="project",
     )(flag, *operands)
 
@@ -318,13 +317,7 @@
     sources = (own + jnp.array(offsets, jnp.int32)) % n
     linked = jnp.any(links[sources] == own, axis=1).astype(jnp.int32)
     own_stats = block_stats(linked[:1], keys, values, pairs[:1], head_size, scale)
-    sent = sends[0](
-        *{
-            "first": [pairs[1][0]],
-            "own": [own_stats[0]],
-            "all": [x for p in pairs[1:] for x in p],
-        }[OPT["wa"]]
-    )
+    first_sent = sends[0](own_stats[0])
     other_stats = block_stats(linked[1:], keys, values, pairs[1:], head_size, scale)
     stats = dict(zip(offsets, list(own_stats) + list(other_stats)))
     needed = {}
@@ -340,23 +333,22 @@
             continue
         entries.sort()
         message = jnp.stack([stats[o] for o in entries])
-        message = passed_along(after(message, *sent) if OPT["st"] else message, "var", -t)
+        message = passed_along(message, "var", -t)
         messages.append(message)
         arrived[t] = {o: message[i] for i, o in enumerate(entries)}
-    sent = sends[1](*messages)
+    sent = sends[1](messages[0])
     windows = [[arrived[(d + e) % n][-e] for e in offsets] for d in offsets]
+    linked = after(linked, *first_sent)
     grads = block_grads(linked, keys, values, pairs, windows, head_size, scale)
     returned = [
-        passed_along(after(part, *sent) if OPT["dq"] else part, "var", o) for o, part in zip(offsets[1:], grads[1:-1])
+        passed_along(after(part, *sent), "var", o)
+        for o, part in zip(offsets[1:], grads[1:-1])
     ]
-    sent = sends[2](grads[-1])
+    sends[2](grads[-1])
     query_grad = grads[0]
     for part in returned:
         query_grad = query_grad + part.astype(f32)
-    query_grad = query_grad.astype(bf16)
-    if OPT["cb"]:
-        query_grad = after(query_grad, *sent)
-    return query_grad, grads[-1], returned
+    return query_grad.astype(bf16), grads[-1], returned
 
 
 def shards(queries, keys, values, out_grad, proj_weight, links):
@@ -367,7 +359,7 @@
     flat = [x.reshape(patches, feature_width) for x in (queries, keys, values, out_grad)]
     weight = proj_weight[0]
     if n != 4:
-        query_grad, pair, returned = attention_grads(*flat, links, reach, [lambda *values: ()] * 3)
+        query_grad, pair, _ = attention_grads(*flat, links, reach, [lambda value: ()] * 3)
         grad_qkv = jnp.concatenate([query_grad, pair[0], pair[1]], axis=1)
         whole = lax.all_gather(weight, "var", axis=0, tiled=True)
         passed = passed_along(times(grad_qkv, whole), "segment", -1)
@@ -376,116 +368,62 @@
     own = lax.axis_index("var")
     core = lax.axis_index("dp")
     chunk = weight.shape[0]
-    ends = [0] + OPT["cuts"] + [chunk]
-    cuts = list(zip(ends[:-1], ends[1:]))
+    cuts = [(0, CAUSAL_BLOCK), (CAUSAL_BLOCK, chunk)]
     step_near = [((v, 0), (v + 1, 0)) for v in range(3)] + [((v + 1, 1), (v, 1)) for v in range(3)]
     step_far = [((1, 0), (2, 0)), ((2, 0), (3, 0)), ((2, 1), (1, 1)), ((1, 1), (0, 1))]
-    near, swapped_near = [], {}
-
-    def send_near(i, *values):
-        near.append(on_line(after(weight[slice(*cuts[i])], *values), step_near))
-        return near[i:]
-
-    far, swapped_far, token = {}, {}, []
-    count = len(cuts)
-
-    def ties(names, pair, returned, query_grad):
-        have = {
-            "pair": lambda: [pair],
-            "token": lambda: token,
-            "ret0": lambda: returned[:1],
-            "ret": lambda: returned,
-            "ret1": lambda: returned[1:],
-            "sw": lambda: [swapped_near[i] for i in sorted(swapped_near)],
-            "nb": lambda: [near[1]],
-            "nl": lambda: [near[-1]],
-            "q": lambda: [query_grad],
-        }
-        return [x for name in names.split() for x in have[name]()]
-
-    def start_far(when, *state):
-        for i in [int(c) for c in OPT["order"]]:
-            if OPT["far"][i][0] == when:
-                far[i] = on_line(after(near[i], *ties(OPT["far"][i][1:], *state)), step_far)
-
-    def send_middle(*values):
-        sent = send_near(1, *values)
-        for i in range(count):
-            if OPT["far"][i] == "s":
-                far[i] = on_line(after(near[i], *values), step_far)
-        return sent
-
-    def send_last(pair):
-        token.append(swapped(after(near[0], pair)))
-        swapped_near[0] = token[0]
-        state = (pair, None, None)
-        if count > 2:
-            send_near(2, *ties(OPT["nc"], *state))
-        for i in range(1, count):
-            swapped_near[i] = swapped(after(near[i], pair))
-        start_far("e", *state)
-        return near[-1:]
+    pieces = [weight[lo:hi] for lo, hi in cuts]
+    near, swapped_near = [], []
+
+    def send_first(value):
+        pieces[:] = lax.optimization_barrier((*pieces, value))[:2]
+        near.append(on_line(pieces[0], step_near))
+        return near[:1]
+
+    def send_second(value):
+        near.append(on_line(after(pieces[1], value), step_near))
+        return near[1:]
+
+    def swap_near(value):
+        swapped_near.extend(swapped(after(piece, value)) for piece in near)
 
     query_grad, pair, returned = attention_grads(
-        *flat,
-        links,
-        reach,
-        [lambda *v: send_near(0, *v), send_middle, send_last],
+        *flat, links, reach, [send_first, send_second, swap_near]
     )
-    state = (pair, returned, query_grad)
-    start_far("l", *state)
     inward = [(0, 1), (3, 2)]
-    outer_pair = lax.ppermute(after(pair, *ties(OPT["op"], *state)), "var", inward)
+    outer_pair = lax.ppermute(after(pair, returned[1]), "var", inward)
     outer_query = lax.ppermute(query_grad, "var", inward)
     far_here = (core == jnp.where(own < 2, 1, 0)).astype(jnp.int32).reshape(1)
 
     def handed_on(block, moves):
-        route = [(a * segments + s, b * segments + (s - 1) % segments) for a, b in moves for s in range(segments)]
+        route = [
+            (a * segments + s, b * segments + (s - 1) % segments)
+            for a, b in moves
+            for s in range(segments)
+        ]
         return lax.ppermute(block, ("var", "segment"), route)
 
     in_place = [(v, v) for v in range(4)]
     from_inner = [(1, 0), (2, 3)]
     own_set, outer_set = (query_grad, pair), (outer_query, outer_pair)
-    (result,) = project(far_here, [own_set], [weight] + near + [swapped_near[i] for i in range(count)])
+    (result,) = project(far_here, [own_set], [weight] + near + swapped_near)
     first = handed_on(result, in_place)
-    if OPT.get("one"):
-        joined = jnp.concatenate([near[1][256:], near[0]], axis=0)
-        rows = [near[1][:256], joined]
-        far = [on_line(after(r, *ties(OPT["ft"][i], *state)), step_far) for i, r in enumerate(rows)]
-    have = {"r": result, "f": first, "p": outer_pair, "q": outer_query}
-    ties_of = [have[c] for c in OPT["sf"]]
-    other0 = swapped(after(far[0], *ties_of))
-    (far0,) = project(far_here, [own_set], far[:1], [other0])
-    handed0 = handed_on(far0, in_place)
-    have.update(x=far0, h=handed0)
-    other1 = swapped(after(far[1], *[have[c] for c in OPT["s1"]]))
-    far1, end = project(
-        far_here, [own_set, outer_set], far, [other0, other1], [[1], [0, 1]]
-    )
-    parts = [handed0, handed_on(far1, in_place), handed_on(end, from_inner)]
-
-    is_end = (own == 0) | (own == 3)
-    blocks = chunk // CAUSAL_BLOCK
-    far_at = (own + 2) % 4 * blocks
-    end_at = jnp.where(is_end, 3 - own, (own + 2) % 4) * blocks
-    places = jnp.stack(
-        [
-            is_end.astype(jnp.int32),
-            far_at,
-            end_at,
-            own * blocks,
-            (own + 3 + 2 * core) % 4 * blocks,
-            (own + 1 + 2 * core) % 4 * blocks,
-        ]
-    ).astype(jnp.int32)
-    whole = pl.BlockSpec(memory_space=pltpu.VMEM)
+    joined = jnp.concatenate([near[1][chunk // 2 :], near[0]], axis=0)
+    far = [
+        on_line(after(rows, returned[1]), step_far) for rows in (near[1][: chunk // 2], joined)
+    ]
+    swapped_far = [
+        swapped(after(far[0], result)),
+        swapped(after(far[1], result, first, outer_pair, outer_query)),
+    ]
+    far_result, end = project(far_here, [own_set, outer_set], far, swapped_far)
+    parts = [handed_on(far_result, in_place), handed_on(end, from_inner)]
     passed = pl.pallas_call(
-        place_kernel,
-        in_specs=[pl.BlockSpec(memory_space=pltpu.SMEM)] + [whole] * (1 + len(parts)),
-        out_specs=whole,
+        functools.partial(place_kernel, CAUSAL_BLOCK),
+        in_specs=[pl.BlockSpec(memory_space=pltpu.VMEM)] * (1 + len(parts)),
+        out_specs=pl.BlockSpec(memory_space=pltpu.VMEM),
         out_shape=jax.ShapeDtypeStruct((patches, 4 * chunk), bf16),
         name="placed",
-    )(places, first, *parts)
+    )(first, *parts)
     return passed.reshape(1, 1, 1, patches, 4 * chunk)
 
 

time: 186 us -> 178 us (0.957)
  starting transfers between devices: 68.3 us -> 37.7 us
  waiting for transfers between devices: 65.3 us -> 93.2 us
  local copies, waits for them, and re-layouts: 13 us -> 9.5 us
  Pallas kernels: 35.3 us -> 33.2 us
    ppermute x1, waiting for transfers between devices: 0.01 us -> 15.6 us  [shards(): outer_query = lax.ppermute(query_grad, 'var', inward)]
    ppermute x4, starting transfers between devices: 15.3 us -> 0.89 us  [swapped(): return lax.ppermute(block, 'dp', [(0, 1), (1, 0)])]
    ppermute x9, waiting for transfers between devices: 38.9 us -> 53.1 us  [passed_along(): return lax.ppermute(block, axis, route)]
    ppermute x4, starting transfers between devices: 19.4 us -> 7.23 us  [on_line(): lax.ppermute(block, ('var', 'dp'), [(a * 2 + c, b * 2 + d) for (a, c), (b...]
    unnamed x36 -> x22, local copies, waits for them, and re-layouts: 6.59 us -> 1.44 us
    ppermute x1, starting transfers between devices: 4.83 us -> 1.34 us  [shards(): outer_pair = lax.ppermute(after(pair, returned[1]), 'var', inward)]
    slice x4, local copies, waits for them, and re-layouts: 5.06 us -> 7.41 us  [the longest x2 4.57 us: shards(): pieces = [weight[lo:hi] for lo, hi in cuts]]
    ppermute x4, waiting for transfers between devices: 5.18 us -> 3.04 us  [swapped(): return lax.ppermute(block, 'dp', [(0, 1), (1, 0)])]
  transfers between devices with their start and end apart: 23 -> 22, of which waited for: 13 -> 9; matrix products, arithmetic and copies ran while one was open for 5% -> 7% of each run, Pallas kernels for 17% -> 16%
where the time goes in v3:
time: 178 us
  waiting for transfers between devices  93.2 us (52%)
  starting transfers between devices  37.7 us (21%)
  Pallas kernels  33.2 us (19%)
  local copies, waits for them, and re-layouts  9.5 us (5%)
  other arithmetic  3.67 us (2%)
    ppermute x9, waiting for transfers between devices, passed_along(): return lax.ppermute(block, axis, route)  53.1 us
    ppermute x9, starting transfers between devices, passed_along(): return lax.ppermute(block, axis, route)  17.5 us
    ppermute x1, waiting for transfers between devices, shards(): outer_query = lax.ppermute(query_grad, 'var', inward)  15.6 us
    pallas_call x1, Pallas kernels, block_grads(): pl.pallas_call(functools.partial(grads_kernel, n, window, head_size, scal...  14.2 us
    ppermute x4, waiting for transfers between devices, on_line(): lax.ppermute(block, ('var', 'dp'), [(a * 2 + c, b * 2 + d) for (a, c), (b...  11 us
    ppermute x3, waiting for transfers between devices, handed_on(): return lax.ppermute(block, ('var', 'segment'), route)  10.5 us
    pallas_call x2, Pallas kernels, project(): pl.pallas_call(functools.partial(project_kernel, uses, len(token_sets), l...  9.71 us
    ppermute x4, starting transfers between devices, on_line(): lax.ppermute(block, ('var', 'dp'), [(a * 2 + c, b * 2 + d) for (a, c), (b...  7.23 us
  transfers between devices with their start and end apart: 22, of which 9 were waited for; matrix products, arithmetic and copies ran while one was open for 7% of the time, Pallas kernels for 16%

profile of v3, /device:TPU:0, one launch (start us, length us, event | category | flops | bytes accessed | tf_op | source)
XLA Modules:
  0.0 177.6 jit_solution(1644261682366760026)
XLA Ops:
  0.0 5.0 %collective-permute-start.1 = (bf16[256,1024]{1,0:T(8,128)(2,1)}, bf16[256,1024]{1,0:T(8,128)(2,1)S(1)}, u32[]{:S(2)}, u32[]{:S(2)}) collective-permute-start(bf16[256,1024]{1,0:T(8,128)(2,1)} %bitcast.34), channel_id=1, source_target_pairs={{8,0},{16,8},{24,16},{0,24},{9,1},{17,9},{25,17},{1,25},{10,2},{18... | collective-permute-start | bytes 1572872 | tf_op jit(solution)/shard_map/ppermute | solution.py:23
  5.1 3.8 %collective-permute-start.2 = (bf16[256,1024]{1,0:T(8,128)(2,1)}, bf16[256,1024]{1,0:T(8,128)(2,1)S(1)}, u32[]{:S(2)}, u32[]{:S(2)}) collective-permute-start(bf16[256,1024]{1,0:T(8,128)(2,1)} %bitcast.38), channel_id=1, source_target_pairs={{8,0},{16,8},{24,16},{0,24},{9,1},{17,9},{25,17},{1,25},{10,2},{18... | collective-permute-start | bytes 1572872 | tf_op jit(solution)/shard_map/ppermute | solution.py:23
  8.9 0.7 compare_select_fusion
  9.6 0.6 gather_fusion
  10.1 0.1 compare_reduce_fusion
  10.3 0.0 copy-start.3
  10.3 0.0 copy-start.5
  10.3 3.4 %slice_bitcast_fusion = bf16[384,3072]{1,0:T(8,128)(2,1)} fusion(bf16[1,512,3072]{2,1,0:T(8,128)(2,1)} %param.11), kind=kLoop, calls=%fused_computation.1 | loop fusion | bytes 4718592 | tf_op jit(solution)/shard_map/slice | solution.py:374
  13.7 2.5 %row_stats.2.refs_6_ = f32[4,8,256]{2,1,0:T(8,128)S(1)} custom-call(s32[1]{0:T(128)S(1)} %bitcast.45, bf16[256,1024]{1,0:T(8,128)(2,1)S(1)} %bitcast.28, bf16[256,1024]{1,0:T(8,128)(2,1)S(1)} %bitcast.31, bf16[256,1024]{1,0:T(8,128)(2,1)S(1)} %bitcast.36, bf16[256,1024]{1,0:T(8,128)(2,1)S(1)} %bitcast.40), custom_call_target="tpu_custom_call" | custom-call | flops 28750000 | bytes 1024 | tf_op jit(solution)/shard_map/row_stats/pallas_call | solution.py:175
  16.2 1.2 slice_bitcast_fusion.1
  17.4 2.2 %collective-permute-start = (bf16[128,3072]{1,0:T(8,128)(2,1)S(1)}, bf16[128,3072]{1,0:T(8,128)(2,1)}, u32[]{:S(2)}, u32[]{:S(2)}) collective-permute-start(bf16[128,3072]{1,0:T(8,128)(2,1)S(1)} %slice_bitcast_fusion.1), channel_id=1, source_target_pairs={{0,8},{8,16},{16,24},{12,4},{20,12},{28,20},{1,9},{9,17},{17,25},{... | collective-permute-start | bytes 2359304 | tf_op jit(solution)/shard_map/ppermute | solution.py:302
  19.6 0.1 slice.47.linked_ref
  19.7 20.5 %collective-permute-done.2.refs_1_.refs_3_ = bf16[256,1024]{1,0:T(8,128)(2,1)S(1)} collective-permute-done((bf16[256,1024]{1,0:T(8,128)(2,1)}, bf16[256,1024]{1,0:T(8,128)(2,1)S(1)}, u32[]{:S(2)}, u32[]{:S(2)}) %collective-permute-start.2) | collective-permute-done | bytes 524320 | tf_op jit(solution)/shard_map/ppermute | solution.py:23
  40.2 12.1 %collective-permute-done.4.refs_3_.refs_5_ = bf16[256,1024]{1,0:T(8,128)(2,1)S(1)} collective-permute-done((bf16[256,1024]{1,0:T(8,128)(2,1)}, bf16[256,1024]{1,0:T(8,128)(2,1)S(1)}, u32[]{:S(2)}, u32[]{:S(2)}) %collective-permute-start.4) | collective-permute-done | bytes 524320 | tf_op jit(solution)/shard_map/ppermute | solution.py:23
  52.3 4.4 %row_stats.3 = (f32[4,8,256]{2,1,0:T(8,128)S(1)}, f32[4,8,256]{2,1,0:T(8,128)S(1)}) custom-call(s32[2]{0:T(128)S(1)} %slice.47.linked_ref, bf16[256,1024]{1,0:T(8,128)(2,1)S(1)} %bitcast.29, bf16[256,1024]{1,0:T(8,128)(2,1)S(1)} %bitcast.32, bf16[256,1024]{1,0:T(8,128)(2,1)S(1)} %collective-permute-done.1.refs_0_.refs_2_, ...), custom_call_target="tpu_custom_call" | custom-call | flops 57500000 | bytes 1024 | tf_op jit(solution)/shard_map/row_stats/pallas_call | solution.py:175
  56.8 0.6 collective-permute-start.5
  57.3 1.5 collective-permute-start.6
  58.8 2.6 %collective-permute-done.5 = f32[2,4,8,256]{3,2,1,0:T(8,128)S(1)} collective-permute-done((f32[2,4,8,256]{3,2,1,0:T(8,128)S(1)}, f32[2,4,8,256]{3,2,1,0:T(8,128)S(1)}, u32[]{:S(2)}, u32[]{:S(2)}) %collective-permute-start.5) | collective-permute-done | bytes 65568 | tf_op jit(solution)/shard_map/ppermute | solution.py:23
  61.5 3.5 %collective-permute-start.8 = (bf16[384,3072]{1,0:T(8,128)(2,1)}, bf16[384,3072]{1,0:T(8,128)(2,1)}, u32[]{:S(2)}, u32[]{:S(2)}) collective-permute-start(bf16[384,3072]{1,0:T(8,128)(2,1)} %slice_bitcast_fusion), channel_id=1, source_target_pairs={{0,8},{8,16},{16,24},{12,4},{20,12},{28,20},{1,9},{9,17},{17,25},{... | collective-permute-start | bytes 7077896 | tf_op jit(solution)/shard_map/ppermute | solution.py:302
  65.0 0.0 collective-permute-done.7
  65.1 14.2 %block_grads.1 = (f32[256,1024]{1,0:T(8,128)}, bf16[256,1024]{1,0:T(8,128)(2,1)}, bf16[256,1024]{1,0:T(8,128)(2,1)}, bf16[2,256,1024]{2,1,0:T(8,128)(2,1)}) custom-call(s32[3]{0:T(128)S(1)} %convert_element_type.13.linked_ref, bf16[256,1024]{1,0:T(8,128)(2,1)S(1)} %bitcast.30, bf16[256,1024]{1,0:T(8,128)(2,1)S(1)} %bitcast.33, ...), custom_call_target="tpu_custom_call" | custom-call | flops 165600002048 | bytes 1024 | tf_op jit(solution)/shard_map/block_grads/pallas_call | solution.py:195
  79.3 11.0 %collective-permute-done.8.refs_4_ = bf16[384,3072]{1,0:T(8,128)(2,1)} collective-permute-done((bf16[384,3072]{1,0:T(8,128)(2,1)}, bf16[384,3072]{1,0:T(8,128)(2,1)}, u32[]{:S(2)}, u32[]{:S(2)}) %collective-permute-start.8) | collective-permute-done | bytes 2359328 | tf_op jit(solution)/shard_map/ppermute | solution.py:302
  90.3 6.5 %collective-permute-start.10 = (bf16[256,1024]{1,0:T(8,128)(2,1)}, bf16[256,1024]{1,0:T(8,128)(2,1)}, u32[]{:S(2)}, u32[]{:S(2)}) collective-permute-start(bf16[256,1024]{1,0:T(8,128)(2,1)} %get-tuple-element.36), channel_id=1, source_target_pairs={{8,0},{16,8},{24,16},{0,24},{9,1},{17,9},{25,17},{1,25},{10,2},{18... | collective-permute-start | bytes 1572872 | tf_op jit(solution)/shard_map/ppermute | solution.py:23
  96.8 0.2 collective-permute-start.11
  97.0 1.5 slice.64
  98.6 0.0 copy-start.7
  98.6 1.3 slice.65
  99.9 1.4 pad_maximum_fusion
  101.3 8.1 %collective-permute-done.10 = bf16[256,1024]{1,0:T(8,128)(2,1)} collective-permute-done((bf16[256,1024]{1,0:T(8,128)(2,1)}, bf16[256,1024]{1,0:T(8,128)(2,1)}, u32[]{:S(2)}, u32[]{:S(2)}) %collective-permute-start.10) | collective-permute-done | bytes 524320 | tf_op jit(solution)/shard_map/ppermute | solution.py:23
  109.4 1.3 collective-permute-start.15
  110.8 0.8 collective-permute-start.16
  111.5 9.7 %collective-permute-done.9 = bf16[256,1024]{1,0:T(8,128)(2,1)} collective-permute-done((bf16[256,1024]{1,0:T(8,128)(2,1)}, bf16[256,1024]{1,0:T(8,128)(2,1)}, u32[]{:S(2)}, u32[]{:S(2)}) %collective-permute-start.9) | collective-permute-done | bytes 524320 | tf_op jit(solution)/shard_map/ppermute | solution.py:23
  121.2 0.8 collective-permute-start.17
  122.0 1.5 add_convert_fusion.refs_0_
  123.5 7.7 %project.2 = bf16[256,1536]{1,0:T(8,128)(2,1)S(1)} custom-call(s32[1]{0:T(128)} %bitcast.flag_ref, bf16[256,1024]{1,0:T(8,128)(2,1)S(1)} %add_convert_fusion.refs_0_, bf16[2,256,1024]{2,1,0:T(8,128)(2,1)S(1)} %copy-done.6, bf16[512,3072]{1,0:T(8,128)(2,1)S(1)} %bitcast.27, bf16[128,3072]{1,0:T(8,128)(2,1)} %collective-permute-done.refs_3_, ...), custom_call_target="tpu_custom_call" | custom-call | flops 8215600128 | bytes 1024 | tf_op jit(solution)/shard_map/project/pallas_call | solution.py:280
  131.2 2.5 %collective-permute-start.13 = (bf16[256,1536]{1,0:T(8,128)(2,1)S(1)}, bf16[256,1536]{1,0:T(8,128)(2,1)S(1)}, u32[]{:S(2)}, u32[]{:S(2)}) collective-permute-start(bf16[256,1536]{1,0:T(8,128)(2,1)S(1)} %project.2), channel_id=1, source_target_pairs={{0,3},{1,0},{2,1},{3,2},{8,11},{9,8},{10,9},{11,10},{16,19},{17,16... | collective-permute-start | bytes 2359304 | tf_op jit(solution)/shard_map/ppermute | solution.py:403
  133.7 4.5 %collective-permute-start.14 = (bf16[256,1024]{1,0:T(8,128)(2,1)S(1)}, bf16[256,1024]{1,0:T(8,128)(2,1)S(1)}, u32[]{:S(2)}, u32[]{:S(2)}) collective-permute-start(bf16[256,1024]{1,0:T(8,128)(2,1)S(1)} %add_convert_fusion.refs_0_), channel_id=1, source_target_pairs={{0,8},{24,16},{1,9},{25,17},{2,10},{26,18},{3,11},{27,19},{4,12},{... | collective-permute-start | bytes 1572872 | tf_op jit(solution)/shard_map/ppermute | solution.py:394
  138.2 0.1 collective-permute-start.18
  138.3 15.6 %collective-permute-done.14.refs_2_ = bf16[256,1024]{1,0:T(8,128)(2,1)S(1)} collective-permute-done((bf16[256,1024]{1,0:T(8,128)(2,1)S(1)}, bf16[256,1024]{1,0:T(8,128)(2,1)S(1)}, u32[]{:S(2)}, u32[]{:S(2)}) %collective-permute-start.14) | collective-permute-done | bytes 524320 | tf_op jit(solution)/shard_map/ppermute | solution.py:394
  153.9 0.6 collective-permute-start.19
  154.5 3.0 %collective-permute-done.19.refs_7_ = bf16[256,3072]{1,0:T(8,128)(2,1)S(1)} collective-permute-done((bf16[256,3072]{1,0:T(8,128)(2,1)S(1)}, bf16[256,3072]{1,0:T(8,128)(2,1)S(1)}, u32[]{:S(2)}, u32[]{:S(2)}) %collective-permute-start.19) | collective-permute-done | bytes 1572896 | tf_op jit(solution)/shard_map/ppermute | solution.py:298
  157.5 2.0 %project.3 = (bf16[256,512]{1,0:T(8,128)(2,1)S(1)}, bf16[256,512]{1,0:T(8,128)(2,1)S(1)}) custom-call(s32[1]{0:T(128)} %bitcast.flag_ref, bf16[256,1024]{1,0:T(8,128)(2,1)S(1)} %add_convert_fusion.refs_0_, bf16[2,256,1024]{2,1,0:T(8,128)(2,1)S(1)} %copy-done.6, bf16[256,1024]{1,0:T(8,128)(2,1)S(1)} %collective-permute-done.14.refs_2_, ...), custom_call_target="tpu_custom_call" | custom-call | flops 5860400128 | bytes 1024 | tf_op jit(solution)/shard_map/project/pallas_call | solution.py:280
  159.6 2.5 %collective-permute-start.20 = (bf16[256,512]{1,0:T(8,128)(2,1)S(1)}, bf16[256,512]{1,0:T(8,128)(2,1)S(1)}, u32[]{:S(2)}, u32[]{:S(2)}) collective-permute-start(bf16[256,512]{1,0:T(8,128)(2,1)S(1)} %get-tuple-element.45), channel_id=1, source_target_pairs={{0,3},{1,0},{2,1},{3,2},{8,11},{9,8},{10,9},{11,10},{16,19},{17,16... | collective-permute-start | bytes 786440 | tf_op jit(solution)/shard_map/ppermute | solution.py:403
  162.1 1.3 collective-permute-start.21
  163.4 10.4 %collective-permute-done.20.refs_0_ = bf16[256,512]{1,0:T(8,128)(2,1)S(1)} collective-permute-done((bf16[256,512]{1,0:T(8,128)(2,1)S(1)}, bf16[256,512]{1,0:T(8,128)(2,1)S(1)}, u32[]{:S(2)}, u32[]{:S(2)}) %collective-permute-start.20) | collective-permute-done | bytes 262176 | tf_op jit(solution)/shard_map/ppermute | solution.py:403
  173.8 0.7 copy-done.9
  174.5 0.7 copy-done.10
  175.2 2.4 %placed.1 = bf16[256,2048]{1,0:T(8,128)(2,1)} custom-call(bf16[256,1536]{1,0:T(8,128)(2,1)} %copy-done.8, bf16[256,512]{1,0:T(8,128)(2,1)} %copy-done.9, bf16[256,512]{1,0:T(8,128)(2,1)} %copy-done.10), custom_call_target="tpu_custom_call" | custom-call | tf_op jit(solution)/shard_map/placed/pallas_call | solution.py:420
  (40 shorter events, 0.1 us)
Async XLA Ops:
  0.0 9.6 %copy-start = (s32[4,3]{1,0:T(4,128)S(1)}, s32[4,3]{1,0:T(4,128)}, u32[]{:S(2)}) copy-start(s32[4,3]{1,0:T(4,128)} %param.12) | copy-start | bytes 148
  0.0 19.7 %collective-permute-start.1 = (bf16[256,1024]{1,0:T(8,128)(2,1)}, bf16[256,1024]{1,0:T(8,128)(2,1)S(1)}, u32[]{:S(2)}, u32[]{:S(2)}) collective-permute-start(bf16[256,1024]{1,0:T(8,128)(2,1)} %bitcast.34), channel_id=1, source_target_pairs={{8,0},{16,8},{24,16},{0,24},{9,1},{17,9},{25,17},{1,25},{10,2},{18... | collective-permute-start | bytes 1572872 | tf_op jit(solution)/shard_map/ppermute | solution.py:23
  5.1 35.2 %collective-permute-start.3 = (bf16[256,1024]{1,0:T(8,128)(2,1)}, bf16[256,1024]{1,0:T(8,128)(2,1)S(1)}, u32[]{:S(2)}, u32[]{:S(2)}) collective-permute-start(bf16[256,1024]{1,0:T(8,128)(2,1)} %bitcast.35), channel_id=1, source_target_pairs={{24,0},{0,8},{8,16},{16,24},{25,1},{1,9},{9,17},{17,25},{26,2},{2,... | collective-permute-start | bytes 1572872 | tf_op jit(solution)/shard_map/ppermute | solution.py:23
  5.1 35.2 %collective-permute-start.2 = (bf16[256,1024]{1,0:T(8,128)(2,1)}, bf16[256,1024]{1,0:T(8,128)(2,1)S(1)}, u32[]{:S(2)}, u32[]{:S(2)}) collective-permute-start(bf16[256,1024]{1,0:T(8,128)(2,1)} %bitcast.38), channel_id=1, source_target_pairs={{8,0},{16,8},{24,16},{0,24},{9,1},{17,9},{25,17},{1,25},{10,2},{18... | collective-permute-start | bytes 1572872 | tf_op jit(solution)/shard_map/ppermute | solution.py:23
  8.9 43.4 %collective-permute-start.4 = (bf16[256,1024]{1,0:T(8,128)(2,1)}, bf16[256,1024]{1,0:T(8,128)(2,1)S(1)}, u32[]{:S(2)}, u32[]{:S(2)}) collective-permute-start(bf16[256,1024]{1,0:T(8,128)(2,1)} %bitcast.39), channel_id=1, source_target_pairs={{24,0},{0,8},{8,16},{16,24},{25,1},{1,9},{9,17},{17,25},{26,2},{2,... | collective-permute-start | bytes 1572872 | tf_op jit(solution)/shard_map/ppermute | solution.py:23
  10.3 3.4 %copy-start.2 = (bf16[1,1,1,256,1024]{4,3,2,1,0:T(8,128)(2,1)S(1)}, bf16[1,1,1,256,1024]{4,3,2,1,0:T(8,128)(2,1)}, u32[]{:S(2)}) copy-start(bf16[1,1,1,256,1024]{4,3,2,1,0:T(8,128)(2,1)} %param.8) | copy-start | bytes 1572868
  10.3 3.4 %copy-start.3 = (bf16[1,1,1,256,1024]{4,3,2,1,0:T(8,128)(2,1)S(1)}, bf16[1,1,1,256,1024]{4,3,2,1,0:T(8,128)(2,1)}, u32[]{:S(2)}) copy-start(bf16[1,1,1,256,1024]{4,3,2,1,0:T(8,128)(2,1)} %param.9) | copy-start | bytes 1572868
  10.3 3.4 %copy-start.4 = (bf16[1,1,1,256,1024]{4,3,2,1,0:T(8,128)(2,1)S(1)}, bf16[1,1,1,256,1024]{4,3,2,1,0:T(8,128)(2,1)}, u32[]{:S(2)}) copy-start(bf16[1,1,1,256,1024]{4,3,2,1,0:T(8,128)(2,1)} %param.7) | copy-start | bytes 1572868
  10.3 3.4 %copy-start.5 = (bf16[1,1,1,256,1024]{4,3,2,1,0:T(8,128)(2,1)S(1)}, bf16[1,1,1,256,1024]{4,3,2,1,0:T(8,128)(2,1)}, u32[]{:S(2)}) copy-start(bf16[1,1,1,256,1024]{4,3,2,1,0:T(8,128)(2,1)} %param.10) | copy-start | bytes 1572868
  17.4 47.6 %collective-permute-start = (bf16[128,3072]{1,0:T(8,128)(2,1)S(1)}, bf16[128,3072]{1,0:T(8,128)(2,1)}, u32[]{:S(2)}, u32[]{:S(2)}) collective-permute-start(bf16[128,3072]{1,0:T(8,128)(2,1)S(1)} %slice_bitcast_fusion.1), channel_id=1, source_target_pairs={{0,8},{8,16},{16,24},{12,4},{20,12},{28,20},{1,9},{9,17},{17,25},{... | collective-permute-start | bytes 2359304 | tf_op jit(solution)/shard_map/ppermute | solution.py:302
  56.8 4.7 %collective-permute-start.5 = (f32[2,4,8,256]{3,2,1,0:T(8,128)S(1)}, f32[2,4,8,256]{3,2,1,0:T(8,128)S(1)}, u32[]{:S(2)}, u32[]{:S(2)}) collective-permute-start(f32[2,4,8,256]{3,2,1,0:T(8,128)S(1)} %get-tuple-element.55), channel_id=1, source_target_pairs={{8,0},{16,8},{24,16},{0,24},{9,1},{17,9},{25,17},{1,25},{10,2},{18... | collective-permute-start | bytes 196616 | tf_op jit(solution)/shard_map/ppermute | solution.py:23
  57.3 7.7 %collective-permute-start.6 = (f32[2,4,8,256]{3,2,1,0:T(8,128)S(1)}, f32[2,4,8,256]{3,2,1,0:T(8,128)S(1)}, u32[]{:S(2)}, u32[]{:S(2)}) collective-permute-start(f32[2,4,8,256]{3,2,1,0:T(8,128)S(1)} %get-tuple-element.54), channel_id=1, source_target_pairs={{24,0},{0,8},{8,16},{16,24},{25,1},{1,9},{9,17},{17,25},{26,2},{2,... | collective-permute-start | bytes 196616 | tf_op jit(solution)/shard_map/ppermute | solution.py:23
  58.8 6.2 %collective-permute-start.7 = (f32[2,4,8,256]{3,2,1,0:T(8,128)S(1)}, f32[2,4,8,256]{3,2,1,0:T(8,128)S(1)}, u32[]{:S(2)}, u32[]{:S(2)}) collective-permute-start(f32[2,4,8,256]{3,2,1,0:T(8,128)S(1)} %get-tuple-element.53), channel_id=1, source_target_pairs={{16,0},{24,8},{0,16},{8,24},{17,1},{25,9},{1,17},{9,25},{18,2},{26... | collective-permute-start | bytes 196616 | tf_op jit(solution)/shard_map/ppermute | solution.py:23
  61.5 28.8 %collective-permute-start.8 = (bf16[384,3072]{1,0:T(8,128)(2,1)}, bf16[384,3072]{1,0:T(8,128)(2,1)}, u32[]{:S(2)}, u32[]{:S(2)}) collective-permute-start(bf16[384,3072]{1,0:T(8,128)(2,1)} %slice_bitcast_fusion), channel_id=1, source_target_pairs={{0,8},{8,16},{16,24},{12,4},{20,12},{28,20},{1,9},{9,17},{17,25},{... | collective-permute-start | bytes 7077896 | tf_op jit(solution)/shard_map/ppermute | solution.py:302
  90.3 33.2 %collective-permute-start.12 = (bf16[384,3072]{1,0:T(8,128)(2,1)}, bf16[384,3072]{1,0:T(8,128)(2,1)S(1)}, u32[]{:S(2)}, u32[]{:S(2)}) collective-permute-start(bf16[384,3072]{1,0:T(8,128)(2,1)} %collective-permute-done.8.refs_4_), channel_id=1, source_target_pairs={{0,4},{4,0},{1,5},{5,1},{2,6},{6,2},{3,7},{7,3},{8,12},{12,8},{9,1... | collective-permute-start | bytes 7077896 | tf_op jit(solution)/shard_map/ppermute | solution.py:298
  90.3 19.1 %collective-permute-start.10 = (bf16[256,1024]{1,0:T(8,128)(2,1)}, bf16[256,1024]{1,0:T(8,128)(2,1)}, u32[]{:S(2)}, u32[]{:S(2)}) collective-permute-start(bf16[256,1024]{1,0:T(8,128)(2,1)} %get-tuple-element.36), channel_id=1, source_target_pairs={{8,0},{16,8},{24,16},{0,24},{9,1},{17,9},{25,17},{1,25},{10,2},{18... | collective-permute-start | bytes 1572872 | tf_op jit(solution)/shard_map/ppermute | solution.py:23
  96.8 24.4 %collective-permute-start.9 = (bf16[256,1024]{1,0:T(8,128)(2,1)}, bf16[256,1024]{1,0:T(8,128)(2,1)}, u32[]{:S(2)}, u32[]{:S(2)}) collective-permute-start(bf16[256,1024]{1,0:T(8,128)(2,1)} %get-tuple-element.34), channel_id=1, source_target_pairs={{24,0},{0,8},{8,16},{16,24},{25,1},{1,9},{9,17},{17,25},{26,2},{2,... | collective-permute-start | bytes 1572872 | tf_op jit(solution)/shard_map/ppermute | solution.py:23
  96.8 26.6 %collective-permute-start.11 = (bf16[128,3072]{1,0:T(8,128)(2,1)}, bf16[128,3072]{1,0:T(8,128)(2,1)S(1)}, u32[]{:S(2)}, u32[]{:S(2)}) collective-permute-start(bf16[128,3072]{1,0:T(8,128)(2,1)} %collective-permute-done.refs_3_), channel_id=1, source_target_pairs={{0,4},{4,0},{1,5},{5,1},{2,6},{6,2},{3,7},{7,3},{8,12},{12,8},{9,1... | collective-permute-start | bytes 2359304 | tf_op jit(solution)/shard_map/ppermute | solution.py:298
  98.6 10.9 %copy-start.6 = (bf16[2,256,1024]{2,1,0:T(8,128)(2,1)S(1)}, bf16[2,256,1024]{2,1,0:T(8,128)(2,1)}, u32[]{:S(2)}) copy-start(bf16[2,256,1024]{2,1,0:T(8,128)(2,1)} %get-tuple-element.40.refs_1_) | copy-start | bytes 3145732
  98.6 23.4 %copy-start.7 = (f32[256,1024]{1,0:T(8,128)S(1)}, f32[256,1024]{1,0:T(8,128)}, u32[]{:S(2)}) copy-start(f32[256,1024]{1,0:T(8,128)} %get-tuple-element.30) | copy-start | bytes 3145732
  99.9 23.6 %copy-start.1 = (bf16[1,512,3072]{2,1,0:T(8,128)(2,1)S(1)}, bf16[1,512,3072]{2,1,0:T(8,128)(2,1)}, u32[]{:S(2)}) copy-start(bf16[1,512,3072]{2,1,0:T(8,128)(2,1)} %param.11) | copy-start | bytes 9437188
  109.4 44.5 %collective-permute-start.15 = (bf16[2,256,1024]{2,1,0:T(8,128)(2,1)S(1)}, bf16[2,256,1024]{2,1,0:T(8,128)(2,1)S(1)}, u32[]{:S(2)}, u32[]{:S(2)}) collective-permute-start(bf16[2,256,1024]{2,1,0:T(8,128)(2,1)S(1)} %copy-done.6), channel_id=1, source_target_pairs={{0,8},{24,16},{1,9},{25,17},{2,10},{26,18},{3,11},{27,19},{4,12},{... | collective-permute-start | bytes 3145736 | tf_op jit(solution)/shard_map/ppermute | solution.py:393
  110.8 27.4 %collective-permute-start.16 = (bf16[256,3072]{1,0:T(8,128)(2,1)S(1)}, bf16[256,3072]{1,0:T(8,128)(2,1)S(1)}, u32[]{:S(2)}, u32[]{:S(2)}) collective-permute-start(bf16[256,3072]{1,0:T(8,128)(2,1)S(1)} %slice.64), channel_id=1, source_target_pairs={{8,16},{16,24},{20,12},{12,4},{9,17},{17,25},{21,13},{13,5},{10,18... | collective-permute-start | bytes 4718600 | tf_op jit(solution)/shard_map/ppermute | solution.py:302
  121.2 32.6 %collective-permute-start.17 = (bf16[256,3072]{1,0:T(8,128)(2,1)S(1)}, bf16[256,3072]{1,0:T(8,128)(2,1)S(1)}, u32[]{:S(2)}, u32[]{:S(2)}) collective-permute-start(bf16[256,3072]{1,0:T(8,128)(2,1)S(1)} %pad_maximum_fusion), channel_id=1, source_target_pairs={{8,16},{16,24},{20,12},{12,4},{9,17},{17,25},{21,13},{13,5},{10,18... | collective-permute-start | bytes 4718600 | tf_op jit(solution)/shard_map/ppermute | solution.py:302
  131.2 22.7 %collective-permute-start.13 = (bf16[256,1536]{1,0:T(8,128)(2,1)S(1)}, bf16[256,1536]{1,0:T(8,128)(2,1)S(1)}, u32[]{:S(2)}, u32[]{:S(2)}) collective-permute-start(bf16[256,1536]{1,0:T(8,128)(2,1)S(1)} %project.2), channel_id=1, source_target_pairs={{0,3},{1,0},{2,1},{3,2},{8,11},{9,8},{10,9},{11,10},{16,19},{17,16... | collective-permute-start | bytes 2359304 | tf_op jit(solution)/shard_map/ppermute | solution.py:403
  133.7 20.2 %collective-permute-start.14 = (bf16[256,1024]{1,0:T(8,128)(2,1)S(1)}, bf16[256,1024]{1,0:T(8,128)(2,1)S(1)}, u32[]{:S(2)}, u32[]{:S(2)}) collective-permute-start(bf16[256,1024]{1,0:T(8,128)(2,1)S(1)} %add_convert_fusion.refs_0_), channel_id=1, source_target_pairs={{0,8},{24,16},{1,9},{25,17},{2,10},{26,18},{3,11},{27,19},{4,12},{... | collective-permute-start | bytes 1572872 | tf_op jit(solution)/shard_map/ppermute | solution.py:394
  138.2 16.3 %collective-permute-start.18 = (bf16[256,3072]{1,0:T(8,128)(2,1)S(1)}, bf16[256,3072]{1,0:T(8,128)(2,1)S(1)}, u32[]{:S(2)}, u32[]{:S(2)}) collective-permute-start(bf16[256,3072]{1,0:T(8,128)(2,1)S(1)} %collective-permute-done.16.refs_4_), channel_id=1, source_target_pairs={{0,4},{4,0},{1,5},{5,1},{2,6},{6,2},{3,7},{7,3},{8,12},{12,8},{9,1... | collective-permute-start | bytes 4718600 | tf_op jit(solution)/shard_map/ppermute | solution.py:298
  153.9 5.7 %copy-start.8 = (bf16[256,1536]{1,0:T(8,128)(2,1)}, bf16[256,1536]{1,0:T(8,128)(2,1)S(1)}, u32[]{:S(2)}) copy-start(bf16[256,1536]{1,0:T(8,128)(2,1)S(1)} %collective-permute-done.13.first_ref) | copy-start | bytes 2359300
  153.9 3.6 %collective-permute-start.19 = (bf16[256,3072]{1,0:T(8,128)(2,1)S(1)}, bf16[256,3072]{1,0:T(8,128)(2,1)S(1)}, u32[]{:S(2)}, u32[]{:S(2)}) collective-permute-start(bf16[256,3072]{1,0:T(8,128)(2,1)S(1)} %collective-permute-done.17.refs_5_), channel_id=1, source_target_pairs={{0,4},{4,0},{1,5},{5,1},{2,6},{6,2},{3,7},{7,3},{8,12},{12,8},{9,1... | collective-permute-start | bytes 4718600 | tf_op jit(solution)/shard_map/ppermute | solution.py:298
  159.6 14.3 %collective-permute-start.20 = (bf16[256,512]{1,0:T(8,128)(2,1)S(1)}, bf16[256,512]{1,0:T(8,128)(2,1)S(1)}, u32[]{:S(2)}, u32[]{:S(2)}) collective-permute-start(bf16[256,512]{1,0:T(8,128)(2,1)S(1)} %get-tuple-element.45), channel_id=1, source_target_pairs={{0,3},{1,0},{2,1},{3,2},{8,11},{9,8},{10,9},{11,10},{16,19},{17,16... | collective-permute-start | bytes 786440 | tf_op jit(solution)/shard_map/ppermute | solution.py:403
  162.1 11.7 %collective-permute-start.21 = (bf16[256,512]{1,0:T(8,128)(2,1)S(1)}, bf16[256,512]{1,0:T(8,128)(2,1)S(1)}, u32[]{:S(2)}, u32[]{:S(2)}) collective-permute-start(bf16[256,512]{1,0:T(8,128)(2,1)S(1)} %get-tuple-element.46), channel_id=1, source_target_pairs={{8,3},{9,0},{10,1},{11,2},{16,27},{17,24},{18,25},{19,26},{12,7},{... | collective-permute-start | bytes 786440 | tf_op jit(solution)/shard_map/ppermute | solution.py:403
  173.8 0.7 copy-start.9
  174.5 0.7 copy-start.10

commit v4 on v3

--- a/solution.py
+++ b/solution.py
@@ -213,8 +213,8 @@
 
 
 def place_kernel(roll, first_ref, *refs):
-    far_refs, end_ref, out_ref = refs[:-2], refs[-2], refs[-1]
-    chunk = end_ref.shape[1]
+    far_refs, end_refs, out_ref = refs[:2], refs[2:4], refs[4]
+    chunk = far_refs[0].shape[1] + far_refs[1].shape[1]
     own, core = lax.axis_index("var"), lax.axis_index("dp")
     is_end = (own == 0) | (own == 3)
 
@@ -237,7 +237,7 @@
     ):
         put(first_ref, i * chunk, chunk, at, 0)
     put_rolled(far_refs, lax.rem(own + 2, 4))
-    pl.when(is_end)(lambda: put_rolled([end_ref], 3 - own))
+    pl.when(is_end)(lambda: put_rolled(end_refs, 3 - own))
 
 
 def project_kernel(uses, sets, pieces, swaps, flag_ref, *refs):
@@ -336,15 +336,14 @@
         message = passed_along(message, "var", -t)
         messages.append(message)
         arrived[t] = {o: message[i] for i, o in enumerate(entries)}
-    sent = sends[1](messages[0])
+    sends[1](messages[0])
     windows = [[arrived[(d + e) % n][-e] for e in offsets] for d in offsets]
     linked = after(linked, *first_sent)
     grads = block_grads(linked, keys, values, pairs, windows, head_size, scale)
     returned = [
-        passed_along(after(part, *sent), "var", o)
-        for o, part in zip(offsets[1:], grads[1:-1])
+        passed_along(part, "var", o) for o, part in zip(offsets[1:], grads[1:-1])
     ]
-    sends[2](grads[-1])
+    sends[2](returned[-1])
     query_grad = grads[0]
     for part in returned:
         query_grad = query_grad + part.astype(f32)
@@ -381,7 +380,6 @@
 
     def send_second(value):
         near.append(on_line(after(pieces[1], value), step_near))
-        return near[1:]
 
     def swap_near(value):
         swapped_near.extend(swapped(after(piece, value)) for piece in near)
@@ -415,8 +413,12 @@
         swapped(after(far[0], result)),
         swapped(after(far[1], result, first, outer_pair, outer_query)),
     ]
-    far_result, end = project(far_here, [own_set, outer_set], far, swapped_far)
-    parts = [handed_on(far_result, in_place), handed_on(end, from_inner)]
+    far_parts, end_parts = [], []
+    for rows, others in zip(far, swapped_far):
+        far_result, end = project(far_here, [own_set, outer_set], [rows], [others])
+        far_parts.append(handed_on(far_result, in_place))
+        end_parts.append(handed_on(end, from_inner))
+    parts = far_parts + end_parts
     passed = pl.pallas_call(
         functools.partial(place_kernel, CAUSAL_BLOCK),
         in_specs=[pl.BlockSpec(memory_space=pltpu.VMEM)] * (1 + len(parts)),

time: 178 us -> 175 us (0.983)
  waiting for transfers between devices: 93.2 us -> 84.3 us
  starting transfers between devices: 37.7 us -> 43.4 us
    ppermute x4, waiting for transfers between devices: 11 us -> 0.01 us  [on_line(): lax.ppermute(block, ('var', 'dp'), [(a * 2 + c, b * 2 + d) for (a, c), (b...]
    ppermute x9, waiting for transfers between devices: 53.1 us -> 62.6 us  [passed_along(): return lax.ppermute(block, axis, route)]
    ppermute x1, starting transfers between devices: 1.34 us -> 6.66 us  [shards(): outer_pair = lax.ppermute(after(pair, returned[1]), 'var', inward)]
    ppermute x9, starting transfers between devices: 17.5 us -> 13 us  [passed_along(): return lax.ppermute(block, axis, route)]
    ppermute x1, waiting for transfers between devices: 15.6 us -> 11.2 us  [shards(): outer_query = lax.ppermute(query_grad, 'var', inward)]
    ppermute x4, starting transfers between devices: 0.89 us -> 4.7 us  [swapped(): return lax.ppermute(block, 'dp', [(0, 1), (1, 0)])]
    ppermute x4, waiting for transfers between devices: 3.04 us -> 0.01 us  [swapped(): return lax.ppermute(block, 'dp', [(0, 1), (1, 0)])]
    ppermute x3 -> x5, starting transfers between devices: 6.32 us -> 8.28 us  [handed_on(): return lax.ppermute(block, ('var', 'segment'), route)]
  transfers between devices with their start and end apart: 22 -> 24, of which waited for: 9 -> 9; matrix products, arithmetic and copies ran while one was open for 7% -> 7% of each run, Pallas kernels for 16% -> 18%
where the time goes in v4:
time: 175 us
  waiting for transfers between devices  84.3 us (48%)
  starting transfers between devices  43.4 us (25%)
  Pallas kernels  33.3 us (19%)
  local copies, waits for them, and re-layouts  10.1 us (6%)
  other arithmetic  3.51 us (2%)
    ppermute x9, waiting for transfers between devices, passed_along(): return lax.ppermute(block, axis, route)  62.6 us
    pallas_call x1, Pallas kernels, block_grads(): pl.pallas_call(functools.partial(grads_kernel, n, window, head_size, scal...  14.2 us
    ppermute x9, starting transfers between devices, passed_along(): return lax.ppermute(block, axis, route)  13 us
    ppermute x1, waiting for transfers between devices, shards(): outer_query = lax.ppermute(query_grad, 'var', inward)  11.2 us
    ppermute x5, waiting for transfers between devices, handed_on(): return lax.ppermute(block, ('var', 'segment'), route)  10.5 us
    pallas_call x3, Pallas kernels, project(): pl.pallas_call(functools.partial(project_kernel, uses, len(token_sets), l...  9.72 us
    ppermute x5, starting transfers between devices, handed_on(): return lax.ppermute(block, ('var', 'segment'), route)  8.28 us
    ppermute x4, starting transfers between devices, on_line(): lax.ppermute(block, ('var', 'dp'), [(a * 2 + c, b * 2 + d) for (a, c), (b...  7.4 us
  transfers between devices with their start and end apart: 24, of which 9 were waited for; matrix products, arithmetic and copies ran while one was open for 7% of the time, Pallas kernels for 18%

profile of v4, /device:TPU:0, one launch (start us, length us, event | category | flops | bytes accessed | tf_op | source)
XLA Modules:
  0.0 174.9 jit_solution(3757436174881799600)
XLA Ops:
  0.0 5.0 %collective-permute-start.1 = (bf16[256,1024]{1,0:T(8,128)(2,1)}, bf16[256,1024]{1,0:T(8,128)(2,1)S(1)}, u32[]{:S(2)}, u32[]{:S(2)}) collective-permute-start(bf16[256,1024]{1,0:T(8,128)(2,1)} %bitcast.34), channel_id=1, source_target_pairs={{8,0},{16,8},{24,16},{0,24},{9,1},{17,9},{25,17},{1,25},{10,2},{18... | collective-permute-start | bytes 1572872 | tf_op jit(solution)/shard_map/ppermute | solution.py:23
  5.1 3.8 %collective-permute-start.2 = (bf16[256,1024]{1,0:T(8,128)(2,1)}, bf16[256,1024]{1,0:T(8,128)(2,1)S(1)}, u32[]{:S(2)}, u32[]{:S(2)}) collective-permute-start(bf16[256,1024]{1,0:T(8,128)(2,1)} %bitcast.38), channel_id=1, source_target_pairs={{8,0},{16,8},{24,16},{0,24},{9,1},{17,9},{25,17},{1,25},{10,2},{18... | collective-permute-start | bytes 1572872 | tf_op jit(solution)/shard_map/ppermute | solution.py:23
  8.9 0.7 compare_select_fusion
  9.6 0.6 gather_fusion
  10.1 0.1 compare_reduce_fusion
  10.3 0.0 copy-start.4
  10.3 3.4 %slice_bitcast_fusion = bf16[384,3072]{1,0:T(8,128)(2,1)} fusion(bf16[1,512,3072]{2,1,0:T(8,128)(2,1)} %param.11), kind=kLoop, calls=%fused_computation.1 | loop fusion | bytes 4718592 | tf_op jit(solution)/shard_map/slice | solution.py:373
  13.7 2.5 %row_stats.2.refs_6_ = f32[4,8,256]{2,1,0:T(8,128)S(1)} custom-call(s32[1]{0:T(128)S(1)} %bitcast.45, bf16[256,1024]{1,0:T(8,128)(2,1)S(1)} %bitcast.28, bf16[256,1024]{1,0:T(8,128)(2,1)S(1)} %bitcast.31, bf16[256,1024]{1,0:T(8,128)(2,1)S(1)} %bitcast.36, bf16[256,1024]{1,0:T(8,128)(2,1)S(1)} %bitcast.40), custom_call_target="tpu_custom_call" | custom-call | flops 28750000 | bytes 1024 | tf_op jit(solution)/shard_map/row_stats/pallas_call | solution.py:175
  16.3 1.2 slice_bitcast_fusion.1
  17.4 2.2 %collective-permute-start = (bf16[128,3072]{1,0:T(8,128)(2,1)S(1)}, bf16[128,3072]{1,0:T(8,128)(2,1)}, u32[]{:S(2)}, u32[]{:S(2)}) collective-permute-start(bf16[128,3072]{1,0:T(8,128)(2,1)S(1)} %slice_bitcast_fusion.1), channel_id=1, source_target_pairs={{0,8},{8,16},{16,24},{12,4},{20,12},{28,20},{1,9},{9,17},{17,25},{... | collective-permute-start | bytes 2359304 | tf_op jit(solution)/shard_map/ppermute | solution.py:302
  19.6 0.1 slice.47.linked_ref
  19.7 20.5 %collective-permute-done.2.refs_1_.refs_3_ = bf16[256,1024]{1,0:T(8,128)(2,1)S(1)} collective-permute-done((bf16[256,1024]{1,0:T(8,128)(2,1)}, bf16[256,1024]{1,0:T(8,128)(2,1)S(1)}, u32[]{:S(2)}, u32[]{:S(2)}) %collective-permute-start.2) | collective-permute-done | bytes 524320 | tf_op jit(solution)/shard_map/ppermute | solution.py:23
  40.2 12.1 %collective-permute-done.4.refs_3_.refs_5_ = bf16[256,1024]{1,0:T(8,128)(2,1)S(1)} collective-permute-done((bf16[256,1024]{1,0:T(8,128)(2,1)}, bf16[256,1024]{1,0:T(8,128)(2,1)S(1)}, u32[]{:S(2)}, u32[]{:S(2)}) %collective-permute-start.4) | collective-permute-done | bytes 524320 | tf_op jit(solution)/shard_map/ppermute | solution.py:23
  52.3 4.4 %row_stats.3 = (f32[4,8,256]{2,1,0:T(8,128)S(1)}, f32[4,8,256]{2,1,0:T(8,128)S(1)}) custom-call(s32[2]{0:T(128)S(1)} %slice.47.linked_ref, bf16[256,1024]{1,0:T(8,128)(2,1)S(1)} %bitcast.29, bf16[256,1024]{1,0:T(8,128)(2,1)S(1)} %bitcast.32, bf16[256,1024]{1,0:T(8,128)(2,1)S(1)} %collective-permute-done.1.refs_0_.refs_2_, ...), custom_call_target="tpu_custom_call" | custom-call | flops 57500000 | bytes 1024 | tf_op jit(solution)/shard_map/row_stats/pallas_call | solution.py:175
  56.8 0.6 collective-permute-start.5
  57.3 1.5 collective-permute-start.6
  58.8 2.6 %collective-permute-done.5 = f32[2,4,8,256]{3,2,1,0:T(8,128)S(1)} collective-permute-done((f32[2,4,8,256]{3,2,1,0:T(8,128)S(1)}, f32[2,4,8,256]{3,2,1,0:T(8,128)S(1)}, u32[]{:S(2)}, u32[]{:S(2)}) %collective-permute-start.5) | collective-permute-done | bytes 65568 | tf_op jit(solution)/shard_map/ppermute | solution.py:23
  61.5 3.6 %collective-permute-start.10 = (bf16[384,3072]{1,0:T(8,128)(2,1)}, bf16[384,3072]{1,0:T(8,128)(2,1)}, u32[]{:S(2)}, u32[]{:S(2)}) collective-permute-start(bf16[384,3072]{1,0:T(8,128)(2,1)} %slice_bitcast_fusion), channel_id=1, source_target_pairs={{0,8},{8,16},{16,24},{12,4},{20,12},{28,20},{1,9},{9,17},{17,25},{... | collective-permute-start | bytes 7077896 | tf_op jit(solution)/shard_map/ppermute | solution.py:302
  65.1 14.2 %block_grads.1 = (f32[256,1024]{1,0:T(8,128)}, bf16[256,1024]{1,0:T(8,128)(2,1)}, bf16[256,1024]{1,0:T(8,128)(2,1)S(1)}, bf16[2,256,1024]{2,1,0:T(8,128)(2,1)}) custom-call(s32[3]{0:T(128)S(1)} %convert_element_type.13.linked_ref, bf16[256,1024]{1,0:T(8,128)(2,1)S(1)} %bitcast.30, bf16[256,1024]{1,0:T(8,128)(2,1)S(1)} %bitcast.33, ...), custom_call_target="tpu_custom_call" | custom-call | flops 165600002048 | bytes 1024 | tf_op jit(solution)/shard_map/block_grads/pallas_call | solution.py:195
  79.3 2.0 %collective-permute-start.9 = (bf16[256,1024]{1,0:T(8,128)(2,1)S(1)}, bf16[256,1024]{1,0:T(8,128)(2,1)S(1)}, u32[]{:S(2)}, u32[]{:S(2)}) collective-permute-start(bf16[256,1024]{1,0:T(8,128)(2,1)S(1)} %get-tuple-element.32), channel_id=1, source_target_pairs={{8,0},{16,8},{24,16},{0,24},{9,1},{17,9},{25,17},{1,25},{10,2},{18... | collective-permute-start | bytes 1572872 | tf_op jit(solution)/shard_map/ppermute | solution.py:23
  81.3 20.1 %collective-permute-done.9 = bf16[256,1024]{1,0:T(8,128)(2,1)S(1)} collective-permute-done((bf16[256,1024]{1,0:T(8,128)(2,1)S(1)}, bf16[256,1024]{1,0:T(8,128)(2,1)S(1)}, u32[]{:S(2)}, u32[]{:S(2)}) %collective-permute-start.9) | collective-permute-done | bytes 524320 | tf_op jit(solution)/shard_map/ppermute | solution.py:23
  101.4 0.8 copy-done.9
  102.2 6.7 %collective-permute-start.15 = (bf16[2,256,1024]{2,1,0:T(8,128)(2,1)}, bf16[2,256,1024]{2,1,0:T(8,128)(2,1)S(1)}, u32[]{:S(2)}, u32[]{:S(2)}) collective-permute-start(bf16[2,256,1024]{2,1,0:T(8,128)(2,1)} %get-tuple-element.38.refs_1_), channel_id=1, source_target_pairs={{0,8},{24,16},{1,9},{25,17},{2,10},{26,18},{3,11},{27,19},{4,12},{... | collective-permute-start | bytes 3145736 | tf_op jit(solution)/shard_map/ppermute | solution.py:391
  108.9 1.5 slice.64
  110.4 0.9 collective-permute-start.16
  111.3 1.2 slice.65
  112.5 1.4 pad_maximum_fusion
  113.9 7.3 %collective-permute-done.8 = bf16[256,1024]{1,0:T(8,128)(2,1)} collective-permute-done((bf16[256,1024]{1,0:T(8,128)(2,1)}, bf16[256,1024]{1,0:T(8,128)(2,1)}, u32[]{:S(2)}, u32[]{:S(2)}) %collective-permute-start.8) | collective-permute-done | bytes 524320 | tf_op jit(solution)/shard_map/ppermute | solution.py:23
  121.2 0.8 collective-permute-start.19
  122.0 1.3 add_convert_fusion.refs_0_
  123.3 7.7 %project.3 = bf16[256,1536]{1,0:T(8,128)(2,1)S(1)} custom-call(s32[1]{0:T(128)} %bitcast.flag_ref, bf16[256,1024]{1,0:T(8,128)(2,1)S(1)} %add_convert_fusion.refs_0_, bf16[2,256,1024]{2,1,0:T(8,128)(2,1)S(1)} %copy-done.6, bf16[512,3072]{1,0:T(8,128)(2,1)S(1)} %bitcast.27, bf16[128,3072]{1,0:T(8,128)(2,1)} %collective-permute-done.refs_3_, ...), custom_call_target="tpu_custom_call" | custom-call | flops 8215600128 | bytes 1024 | tf_op jit(solution)/shard_map/project/pallas_call | solution.py:280
  131.0 2.5 %collective-permute-start.13 = (bf16[256,1536]{1,0:T(8,128)(2,1)S(1)}, bf16[256,1536]{1,0:T(8,128)(2,1)S(1)}, u32[]{:S(2)}, u32[]{:S(2)}) collective-permute-start(bf16[256,1536]{1,0:T(8,128)(2,1)S(1)} %project.3), channel_id=1, source_target_pairs={{0,3},{1,0},{2,1},{3,2},{8,11},{9,8},{10,9},{11,10},{16,19},{17,16... | collective-permute-start | bytes 2359304 | tf_op jit(solution)/shard_map/ppermute | solution.py:401
  133.5 3.3 %collective-permute-start.14 = (bf16[256,1024]{1,0:T(8,128)(2,1)S(1)}, bf16[256,1024]{1,0:T(8,128)(2,1)S(1)}, u32[]{:S(2)}, u32[]{:S(2)}) collective-permute-start(bf16[256,1024]{1,0:T(8,128)(2,1)S(1)} %add_convert_fusion.refs_0_), channel_id=1, source_target_pairs={{0,8},{24,16},{1,9},{25,17},{2,10},{26,18},{3,11},{27,19},{4,12},{... | collective-permute-start | bytes 1572872 | tf_op jit(solution)/shard_map/ppermute | solution.py:392
  136.9 1.0 collective-permute-start.17
  137.9 11.2 %collective-permute-done.14.refs_2_ = bf16[256,1024]{1,0:T(8,128)(2,1)S(1)} collective-permute-done((bf16[256,1024]{1,0:T(8,128)(2,1)S(1)}, bf16[256,1024]{1,0:T(8,128)(2,1)S(1)}, u32[]{:S(2)}, u32[]{:S(2)}) %collective-permute-start.14) | collective-permute-done | bytes 524320 | tf_op jit(solution)/shard_map/ppermute | solution.py:392
  149.1 1.7 collective-permute-done.13.first_ref
  150.8 3.7 %collective-permute-start.20 = (bf16[256,3072]{1,0:T(8,128)(2,1)S(1)}, bf16[256,3072]{1,0:T(8,128)(2,1)S(1)}, u32[]{:S(2)}, u32[]{:S(2)}) collective-permute-start(bf16[256,3072]{1,0:T(8,128)(2,1)S(1)} %collective-permute-done.19.refs_4_), channel_id=1, source_target_pairs={{0,4},{4,0},{1,5},{5,1},{2,6},{6,2},{3,7},{7,3},{8,12},{12,8},{9,1... | collective-permute-start | bytes 4718600 | tf_op jit(solution)/shard_map/ppermute | solution.py:298
  154.5 1.0 project.4
  155.5 2.5 %collective-permute-start.18 = (bf16[256,256]{1,0:T(8,128)(2,1)S(1)}, bf16[256,256]{1,0:T(8,128)(2,1)S(1)}, u32[]{:S(2)}, u32[]{:S(2)}) collective-permute-start(bf16[256,256]{1,0:T(8,128)(2,1)S(1)} %get-tuple-element.41), channel_id=1, source_target_pairs={{0,3},{1,0},{2,1},{3,2},{8,11},{9,8},{10,9},{11,10},{16,19},{17,16... | collective-permute-start | bytes 393224 | tf_op jit(solution)/shard_map/ppermute | solution.py:401
  158.0 1.3 collective-permute-start.22
  159.3 1.0 project.5
  160.3 0.7 collective-permute-start.21
  161.1 1.3 collective-permute-start.23
  162.4 3.7 %collective-permute-done.22.refs_2_ = bf16[256,256]{1,0:T(8,128)(2,1)S(1)} collective-permute-done((bf16[256,256]{1,0:T(8,128)(2,1)S(1)}, bf16[256,256]{1,0:T(8,128)(2,1)S(1)}, u32[]{:S(2)}, u32[]{:S(2)}) %collective-permute-start.22) | collective-permute-done | bytes 131104 | tf_op jit(solution)/shard_map/ppermute | solution.py:401
  166.0 5.1 %collective-permute-done.21.refs_1_ = bf16[256,256]{1,0:T(8,128)(2,1)S(1)} collective-permute-done((bf16[256,256]{1,0:T(8,128)(2,1)S(1)}, bf16[256,256]{1,0:T(8,128)(2,1)S(1)}, u32[]{:S(2)}, u32[]{:S(2)}) %collective-permute-start.21) | collective-permute-done | bytes 131104 | tf_op jit(solution)/shard_map/ppermute | solution.py:401
  171.2 0.6 copy-done.13
  171.8 0.7 copy-done.14
  172.5 2.4 %placed.1 = bf16[256,2048]{1,0:T(8,128)(2,1)} custom-call(bf16[256,1536]{1,0:T(8,128)(2,1)} %copy-done.8, bf16[256,256]{1,0:T(8,128)(2,1)} %copy-done.11, bf16[256,256]{1,0:T(8,128)(2,1)} %copy-done.13, bf16[256,256]{1,0:T(8,128)(2,1)} %copy-done.12, bf16[256,256]{1,0:T(8,128)(2,1)} %copy-done.14), custom_call_target="tpu_custom_call" | custom-call | tf_op jit(solution)/shard_map/placed/pallas_call | solution.py:422
  (53 shorter events, 0.2 us)
Async XLA Ops:
  0.0 9.6 %copy-start = (s32[4,3]{1,0:T(4,128)S(1)}, s32[4,3]{1,0:T(4,128)}, u32[]{:S(2)}) copy-start(s32[4,3]{1,0:T(4,128)} %param.12) | copy-start | bytes 148
  0.0 19.7 %collective-permute-start.1 = (bf16[256,1024]{1,0:T(8,128)(2,1)}, bf16[256,1024]{1,0:T(8,128)(2,1)S(1)}, u32[]{:S(2)}, u32[]{:S(2)}) collective-permute-start(bf16[256,1024]{1,0:T(8,128)(2,1)} %bitcast.34), channel_id=1, source_target_pairs={{8,0},{16,8},{24,16},{0,24},{9,1},{17,9},{25,17},{1,25},{10,2},{18... | collective-permute-start | bytes 1572872 | tf_op jit(solution)/shard_map/ppermute | solution.py:23
  5.1 35.2 %collective-permute-start.3 = (bf16[256,1024]{1,0:T(8,128)(2,1)}, bf16[256,1024]{1,0:T(8,128)(2,1)S(1)}, u32[]{:S(2)}, u32[]{:S(2)}) collective-permute-start(bf16[256,1024]{1,0:T(8,128)(2,1)} %bitcast.35), channel_id=1, source_target_pairs={{24,0},{0,8},{8,16},{16,24},{25,1},{1,9},{9,17},{17,25},{26,2},{2,... | collective-permute-start | bytes 1572872 | tf_op jit(solution)/shard_map/ppermute | solution.py:23
  5.1 35.2 %collective-permute-start.2 = (bf16[256,1024]{1,0:T(8,128)(2,1)}, bf16[256,1024]{1,0:T(8,128)(2,1)S(1)}, u32[]{:S(2)}, u32[]{:S(2)}) collective-permute-start(bf16[256,1024]{1,0:T(8,128)(2,1)} %bitcast.38), channel_id=1, source_target_pairs={{8,0},{16,8},{24,16},{0,24},{9,1},{17,9},{25,17},{1,25},{10,2},{18... | collective-permute-start | bytes 1572872 | tf_op jit(solution)/shard_map/ppermute | solution.py:23
  8.9 43.4 %collective-permute-start.4 = (bf16[256,1024]{1,0:T(8,128)(2,1)}, bf16[256,1024]{1,0:T(8,128)(2,1)S(1)}, u32[]{:S(2)}, u32[]{:S(2)}) collective-permute-start(bf16[256,1024]{1,0:T(8,128)(2,1)} %bitcast.39), channel_id=1, source_target_pairs={{24,0},{0,8},{8,16},{16,24},{25,1},{1,9},{9,17},{17,25},{26,2},{2,... | collective-permute-start | bytes 1572872 | tf_op jit(solution)/shard_map/ppermute | solution.py:23
  10.3 3.5 %copy-start.2 = (bf16[1,1,1,256,1024]{4,3,2,1,0:T(8,128)(2,1)S(1)}, bf16[1,1,1,256,1024]{4,3,2,1,0:T(8,128)(2,1)}, u32[]{:S(2)}) copy-start(bf16[1,1,1,256,1024]{4,3,2,1,0:T(8,128)(2,1)} %param.8) | copy-start | bytes 1572868
  10.3 3.4 %copy-start.3 = (bf16[1,1,1,256,1024]{4,3,2,1,0:T(8,128)(2,1)S(1)}, bf16[1,1,1,256,1024]{4,3,2,1,0:T(8,128)(2,1)}, u32[]{:S(2)}) copy-start(bf16[1,1,1,256,1024]{4,3,2,1,0:T(8,128)(2,1)} %param.9) | copy-start | bytes 1572868
  10.3 3.4 %copy-start.4 = (bf16[1,1,1,256,1024]{4,3,2,1,0:T(8,128)(2,1)S(1)}, bf16[1,1,1,256,1024]{4,3,2,1,0:T(8,128)(2,1)}, u32[]{:S(2)}) copy-start(bf16[1,1,1,256,1024]{4,3,2,1,0:T(8,128)(2,1)} %param.7) | copy-start | bytes 1572868
  10.3 3.4 %copy-start.5 = (bf16[1,1,1,256,1024]{4,3,2,1,0:T(8,128)(2,1)S(1)}, bf16[1,1,1,256,1024]{4,3,2,1,0:T(8,128)(2,1)}, u32[]{:S(2)}) copy-start(bf16[1,1,1,256,1024]{4,3,2,1,0:T(8,128)(2,1)} %param.10) | copy-start | bytes 1572868
  17.4 47.6 %collective-permute-start = (bf16[128,3072]{1,0:T(8,128)(2,1)S(1)}, bf16[128,3072]{1,0:T(8,128)(2,1)}, u32[]{:S(2)}, u32[]{:S(2)}) collective-permute-start(bf16[128,3072]{1,0:T(8,128)(2,1)S(1)} %slice_bitcast_fusion.1), channel_id=1, source_target_pairs={{0,8},{8,16},{16,24},{12,4},{20,12},{28,20},{1,9},{9,17},{17,25},{... | collective-permute-start | bytes 2359304 | tf_op jit(solution)/shard_map/ppermute | solution.py:302
  56.8 4.7 %collective-permute-start.5 = (f32[2,4,8,256]{3,2,1,0:T(8,128)S(1)}, f32[2,4,8,256]{3,2,1,0:T(8,128)S(1)}, u32[]{:S(2)}, u32[]{:S(2)}) collective-permute-start(f32[2,4,8,256]{3,2,1,0:T(8,128)S(1)} %get-tuple-element.55), channel_id=1, source_target_pairs={{8,0},{16,8},{24,16},{0,24},{9,1},{17,9},{25,17},{1,25},{10,2},{18... | collective-permute-start | bytes 196616 | tf_op jit(solution)/shard_map/ppermute | solution.py:23
  57.3 7.7 %collective-permute-start.6 = (f32[2,4,8,256]{3,2,1,0:T(8,128)S(1)}, f32[2,4,8,256]{3,2,1,0:T(8,128)S(1)}, u32[]{:S(2)}, u32[]{:S(2)}) collective-permute-start(f32[2,4,8,256]{3,2,1,0:T(8,128)S(1)} %get-tuple-element.54), channel_id=1, source_target_pairs={{24,0},{0,8},{8,16},{16,24},{25,1},{1,9},{9,17},{17,25},{26,2},{2,... | collective-permute-start | bytes 196616 | tf_op jit(solution)/shard_map/ppermute | solution.py:23
  58.8 6.2 %collective-permute-start.7 = (f32[2,4,8,256]{3,2,1,0:T(8,128)S(1)}, f32[2,4,8,256]{3,2,1,0:T(8,128)S(1)}, u32[]{:S(2)}, u32[]{:S(2)}) collective-permute-start(f32[2,4,8,256]{3,2,1,0:T(8,128)S(1)} %get-tuple-element.53), channel_id=1, source_target_pairs={{16,0},{24,8},{0,16},{8,24},{17,1},{25,9},{1,17},{9,25},{18,2},{26... | collective-permute-start | bytes 196616 | tf_op jit(solution)/shard_map/ppermute | solution.py:23
  61.5 39.9 %collective-permute-start.10 = (bf16[384,3072]{1,0:T(8,128)(2,1)}, bf16[384,3072]{1,0:T(8,128)(2,1)}, u32[]{:S(2)}, u32[]{:S(2)}) collective-permute-start(bf16[384,3072]{1,0:T(8,128)(2,1)} %slice_bitcast_fusion), channel_id=1, source_target_pairs={{0,8},{8,16},{16,24},{12,4},{20,12},{28,20},{1,9},{9,17},{17,25},{... | collective-permute-start | bytes 7077896 | tf_op jit(solution)/shard_map/ppermute | solution.py:302
  79.3 22.1 %collective-permute-start.9 = (bf16[256,1024]{1,0:T(8,128)(2,1)S(1)}, bf16[256,1024]{1,0:T(8,128)(2,1)S(1)}, u32[]{:S(2)}, u32[]{:S(2)}) collective-permute-start(bf16[256,1024]{1,0:T(8,128)(2,1)S(1)} %get-tuple-element.32), channel_id=1, source_target_pairs={{8,0},{16,8},{24,16},{0,24},{9,1},{17,9},{25,17},{1,25},{10,2},{18... | collective-permute-start | bytes 1572872 | tf_op jit(solution)/shard_map/ppermute | solution.py:23
  101.4 0.8 copy-start.9
  101.4 21.9 %collective-permute-start.12 = (bf16[384,3072]{1,0:T(8,128)(2,1)}, bf16[384,3072]{1,0:T(8,128)(2,1)S(1)}, u32[]{:S(2)}, u32[]{:S(2)}) collective-permute-start(bf16[384,3072]{1,0:T(8,128)(2,1)} %collective-permute-done.10.refs_4_), channel_id=1, source_target_pairs={{0,4},{4,0},{1,5},{5,1},{2,6},{6,2},{3,7},{7,3},{8,12},{12,8},{9,1... | collective-permute-start | bytes 7077896 | tf_op jit(solution)/shard_map/ppermute | solution.py:298
  102.2 19.0 %collective-permute-start.8 = (bf16[256,1024]{1,0:T(8,128)(2,1)}, bf16[256,1024]{1,0:T(8,128)(2,1)}, u32[]{:S(2)}, u32[]{:S(2)}) collective-permute-start(bf16[256,1024]{1,0:T(8,128)(2,1)} %get-tuple-element.31), channel_id=1, source_target_pairs={{24,0},{0,8},{8,16},{16,24},{25,1},{1,9},{9,17},{17,25},{26,2},{2,... | collective-permute-start | bytes 1572872 | tf_op jit(solution)/shard_map/ppermute | solution.py:23
  102.2 21.1 %collective-permute-start.11 = (bf16[128,3072]{1,0:T(8,128)(2,1)}, bf16[128,3072]{1,0:T(8,128)(2,1)S(1)}, u32[]{:S(2)}, u32[]{:S(2)}) collective-permute-start(bf16[128,3072]{1,0:T(8,128)(2,1)} %collective-permute-done.refs_3_), channel_id=1, source_target_pairs={{0,4},{4,0},{1,5},{5,1},{2,6},{6,2},{3,7},{7,3},{8,12},{12,8},{9,1... | collective-permute-start | bytes 2359304 | tf_op jit(solution)/shard_map/ppermute | solution.py:298
  102.2 46.9 %collective-permute-start.15 = (bf16[2,256,1024]{2,1,0:T(8,128)(2,1)}, bf16[2,256,1024]{2,1,0:T(8,128)(2,1)S(1)}, u32[]{:S(2)}, u32[]{:S(2)}) collective-permute-start(bf16[2,256,1024]{2,1,0:T(8,128)(2,1)} %get-tuple-element.38.refs_1_), channel_id=1, source_target_pairs={{0,8},{24,16},{1,9},{25,17},{2,10},{26,18},{3,11},{27,19},{4,12},{... | collective-permute-start | bytes 3145736 | tf_op jit(solution)/shard_map/ppermute | solution.py:391
  110.4 11.6 %copy-start.7 = (f32[256,1024]{1,0:T(8,128)S(1)}, f32[256,1024]{1,0:T(8,128)}, u32[]{:S(2)}) copy-start(f32[256,1024]{1,0:T(8,128)} %get-tuple-element.30) | copy-start | bytes 3145732
  110.4 11.6 %copy-start.10 = (bf16[256,1024]{1,0:T(8,128)(2,1)S(1)}, bf16[256,1024]{1,0:T(8,128)(2,1)}, u32[]{:S(2)}) copy-start(bf16[256,1024]{1,0:T(8,128)(2,1)} %copy-done.9) | copy-start | bytes 1572868
  110.4 26.4 %collective-permute-start.16 = (bf16[256,3072]{1,0:T(8,128)(2,1)S(1)}, bf16[256,3072]{1,0:T(8,128)(2,1)S(1)}, u32[]{:S(2)}, u32[]{:S(2)}) collective-permute-start(bf16[256,3072]{1,0:T(8,128)(2,1)S(1)} %slice.64), channel_id=1, source_target_pairs={{8,16},{16,24},{20,12},{12,4},{9,17},{17,25},{21,13},{13,5},{10,18... | collective-permute-start | bytes 4718600 | tf_op jit(solution)/shard_map/ppermute | solution.py:302
  112.5 10.8 %copy-start.1 = (bf16[1,512,3072]{2,1,0:T(8,128)(2,1)S(1)}, bf16[1,512,3072]{2,1,0:T(8,128)(2,1)}, u32[]{:S(2)}) copy-start(bf16[1,512,3072]{2,1,0:T(8,128)(2,1)} %param.11) | copy-start | bytes 9437188
  112.5 10.8 %copy-start.6 = (bf16[2,256,1024]{2,1,0:T(8,128)(2,1)S(1)}, bf16[2,256,1024]{2,1,0:T(8,128)(2,1)}, u32[]{:S(2)}) copy-start(bf16[2,256,1024]{2,1,0:T(8,128)(2,1)} %get-tuple-element.38.refs_1_) | copy-start | bytes 3145732
  121.2 27.9 %collective-permute-start.19 = (bf16[256,3072]{1,0:T(8,128)(2,1)S(1)}, bf16[256,3072]{1,0:T(8,128)(2,1)S(1)}, u32[]{:S(2)}, u32[]{:S(2)}) collective-permute-start(bf16[256,3072]{1,0:T(8,128)(2,1)S(1)} %pad_maximum_fusion), channel_id=1, source_target_pairs={{8,16},{16,24},{20,12},{12,4},{9,17},{17,25},{21,13},{13,5},{10,18... | collective-permute-start | bytes 4718600 | tf_op jit(solution)/shard_map/ppermute | solution.py:302
  131.0 19.8 %collective-permute-start.13 = (bf16[256,1536]{1,0:T(8,128)(2,1)S(1)}, bf16[256,1536]{1,0:T(8,128)(2,1)S(1)}, u32[]{:S(2)}, u32[]{:S(2)}) collective-permute-start(bf16[256,1536]{1,0:T(8,128)(2,1)S(1)} %project.3), channel_id=1, source_target_pairs={{0,3},{1,0},{2,1},{3,2},{8,11},{9,8},{10,9},{11,10},{16,19},{17,16... | collective-permute-start | bytes 2359304 | tf_op jit(solution)/shard_map/ppermute | solution.py:401
  133.5 15.6 %collective-permute-start.14 = (bf16[256,1024]{1,0:T(8,128)(2,1)S(1)}, bf16[256,1024]{1,0:T(8,128)(2,1)S(1)}, u32[]{:S(2)}, u32[]{:S(2)}) collective-permute-start(bf16[256,1024]{1,0:T(8,128)(2,1)S(1)} %add_convert_fusion.refs_0_), channel_id=1, source_target_pairs={{0,8},{24,16},{1,9},{25,17},{2,10},{26,18},{3,11},{27,19},{4,12},{... | collective-permute-start | bytes 1572872 | tf_op jit(solution)/shard_map/ppermute | solution.py:392
  136.9 17.6 %collective-permute-start.17 = (bf16[256,3072]{1,0:T(8,128)(2,1)S(1)}, bf16[256,3072]{1,0:T(8,128)(2,1)S(1)}, u32[]{:S(2)}, u32[]{:S(2)}) collective-permute-start(bf16[256,3072]{1,0:T(8,128)(2,1)S(1)} %collective-permute-done.16.refs_4_), channel_id=1, source_target_pairs={{0,4},{4,0},{1,5},{5,1},{2,6},{6,2},{3,7},{7,3},{8,12},{12,8},{9,1... | collective-permute-start | bytes 4718600 | tf_op jit(solution)/shard_map/ppermute | solution.py:298
  150.8 4.7 %copy-start.8 = (bf16[256,1536]{1,0:T(8,128)(2,1)}, bf16[256,1536]{1,0:T(8,128)(2,1)S(1)}, u32[]{:S(2)}) copy-start(bf16[256,1536]{1,0:T(8,128)(2,1)S(1)} %collective-permute-done.13.first_ref) | copy-start | bytes 2359300
  150.8 8.5 %collective-permute-start.20 = (bf16[256,3072]{1,0:T(8,128)(2,1)S(1)}, bf16[256,3072]{1,0:T(8,128)(2,1)S(1)}, u32[]{:S(2)}, u32[]{:S(2)}) collective-permute-start(bf16[256,3072]{1,0:T(8,128)(2,1)S(1)} %collective-permute-done.19.refs_4_), channel_id=1, source_target_pairs={{0,4},{4,0},{1,5},{5,1},{2,6},{6,2},{3,7},{7,3},{8,12},{12,8},{9,1... | collective-permute-start | bytes 4718600 | tf_op jit(solution)/shard_map/ppermute | solution.py:298
  155.5 6.8 %collective-permute-start.18 = (bf16[256,256]{1,0:T(8,128)(2,1)S(1)}, bf16[256,256]{1,0:T(8,128)(2,1)S(1)}, u32[]{:S(2)}, u32[]{:S(2)}) collective-permute-start(bf16[256,256]{1,0:T(8,128)(2,1)S(1)} %get-tuple-element.41), channel_id=1, source_target_pairs={{0,3},{1,0},{2,1},{3,2},{8,11},{9,8},{10,9},{11,10},{16,19},{17,16... | collective-permute-start | bytes 393224 | tf_op jit(solution)/shard_map/ppermute | solution.py:401
  158.0 8.0 %collective-permute-start.22 = (bf16[256,256]{1,0:T(8,128)(2,1)S(1)}, bf16[256,256]{1,0:T(8,128)(2,1)S(1)}, u32[]{:S(2)}, u32[]{:S(2)}) collective-permute-start(bf16[256,256]{1,0:T(8,128)(2,1)S(1)} %get-tuple-element.45), channel_id=1, source_target_pairs={{8,3},{9,0},{10,1},{11,2},{16,27},{17,24},{18,25},{19,26},{12,7},{... | collective-permute-start | bytes 393224 | tf_op jit(solution)/shard_map/ppermute | solution.py:401
  160.3 10.8 %collective-permute-start.21 = (bf16[256,256]{1,0:T(8,128)(2,1)S(1)}, bf16[256,256]{1,0:T(8,128)(2,1)S(1)}, u32[]{:S(2)}, u32[]{:S(2)}) collective-permute-start(bf16[256,256]{1,0:T(8,128)(2,1)S(1)} %get-tuple-element.44), channel_id=1, source_target_pairs={{0,3},{1,0},{2,1},{3,2},{8,11},{9,8},{10,9},{11,10},{16,19},{17,16... | collective-permute-start | bytes 393224 | tf_op jit(solution)/shard_map/ppermute | solution.py:401
  161.1 10.1 %collective-permute-start.23 = (bf16[256,256]{1,0:T(8,128)(2,1)S(1)}, bf16[256,256]{1,0:T(8,128)(2,1)S(1)}, u32[]{:S(2)}, u32[]{:S(2)}) collective-permute-start(bf16[256,256]{1,0:T(8,128)(2,1)S(1)} %get-tuple-element.46), channel_id=1, source_target_pairs={{8,3},{9,0},{10,1},{11,2},{16,27},{17,24},{18,25},{19,26},{12,7},{... | collective-permute-start | bytes 393224 | tf_op jit(solution)/shard_map/ppermute | solution.py:401
  162.4 8.8 %copy-start.11 = (bf16[256,256]{1,0:T(8,128)(2,1)}, bf16[256,256]{1,0:T(8,128)(2,1)S(1)}, u32[]{:S(2)}) copy-start(bf16[256,256]{1,0:T(8,128)(2,1)S(1)} %collective-permute-done.18.refs_0_) | copy-start | bytes 393220
  166.0 5.1 %copy-start.12 = (bf16[256,256]{1,0:T(8,128)(2,1)}, bf16[256,256]{1,0:T(8,128)(2,1)S(1)}, u32[]{:S(2)}) copy-start(bf16[256,256]{1,0:T(8,128)(2,1)S(1)} %collective-permute-done.22.refs_2_) | copy-start | bytes 393220
  171.1 0.7 copy-start.13
  171.8 0.7 copy-start.14

commit v5 on v4

--- a/solution.py
+++ b/solution.py
@@ -343,7 +343,7 @@
     returned = [
         passed_along(part, "var", o) for o, part in zip(offsets[1:], grads[1:-1])
     ]
-    sends[2](returned[-1])
+    sends[2](grads[-1])
     query_grad = grads[0]
     for part in returned:
         query_grad = query_grad + part.astype(f32)

time: 175 us -> 175 us (level)
  waiting for transfers between devices: 84.3 us -> 88.4 us
  starting transfers between devices: 43.4 us -> 39.9 us
    ppermute x4, waiting for transfers between devices: 0.01 us -> 11 us  [on_line(): lax.ppermute(block, ('var', 'dp'), [(a * 2 + c, b * 2 + d) for (a, c), (b...]
    ppermute x9, waiting for transfers between devices: 62.6 us -> 53 us  [passed_along(): return lax.ppermute(block, axis, route)]
    ppermute x1, starting transfers between devices: 6.66 us -> 1.34 us  [shards(): outer_pair = lax.ppermute(after(pair, returned[1]), 'var', inward)]
    ppermute x9, starting transfers between devices: 13 us -> 17.5 us  [passed_along(): return lax.ppermute(block, axis, route)]
    ppermute x1, waiting for transfers between devices: 11.2 us -> 15.6 us  [shards(): outer_query = lax.ppermute(query_grad, 'var', inward)]
    ppermute x4, starting transfers between devices: 4.7 us -> 0.89 us  [swapped(): return lax.ppermute(block, 'dp', [(0, 1), (1, 0)])]
where the time goes in v5:
time: 175 us
  waiting for transfers between devices  88.4 us (51%)
  starting transfers between devices  39.9 us (23%)
  Pallas kernels  33.3 us (19%)
  local copies, waits for them, and re-layouts  9.27 us (5%)
  other arithmetic  3.67 us (2%)
    ppermute x9, waiting for transfers between devices, passed_along(): return lax.ppermute(block, axis, route)  53 us
    ppermute x9, starting transfers between devices, passed_along(): return lax.ppermute(block, axis, route)  17.5 us
    ppermute x1, waiting for transfers between devices, shards(): outer_query = lax.ppermute(query_grad, 'var', inward)  15.6 us
    pallas_call x1, Pallas kernels, block_grads(): pl.pallas_call(functools.partial(grads_kernel, n, window, head_size, scal...  14.2 us
    ppermute x4, waiting for transfers between devices, on_line(): lax.ppermute(block, ('var', 'dp'), [(a * 2 + c, b * 2 + d) for (a, c), (b...  11 us
    pallas_call x3, Pallas kernels, project(): pl.pallas_call(functools.partial(project_kernel, uses, len(token_sets), l...  9.73 us
    ppermute x5, waiting for transfers between devices, handed_on(): return lax.ppermute(block, ('var', 'segment'), route)  8.79 us
    ppermute x5, starting transfers between devices, handed_on(): return lax.ppermute(block, ('var', 'segment'), route)  8.27 us
  transfers between devices with their start and end apart: 24, of which 9 were waited for; matrix products, arithmetic and copies ran while one was open for 7% of the time, Pallas kernels for 18%

profile of v5, /device:TPU:0, one launch (start us, length us, event | category | flops | bytes accessed | tf_op | source)
XLA Modules:
  0.0 174.9 jit_solution(10799895254459921784)
XLA Ops:
  0.0 5.0 %collective-permute-start.1 = (bf16[256,1024]{1,0:T(8,128)(2,1)}, bf16[256,1024]{1,0:T(8,128)(2,1)S(1)}, u32[]{:S(2)}, u32[]{:S(2)}) collective-permute-start(bf16[256,1024]{1,0:T(8,128)(2,1)} %bitcast.34), channel_id=1, source_target_pairs={{8,0},{16,8},{24,16},{0,24},{9,1},{17,9},{25,17},{1,25},{10,2},{18... | collective-permute-start | bytes 1572872 | tf_op jit(solution)/shard_map/ppermute | solution.py:23
  5.1 3.8 %collective-permute-start.2 = (bf16[256,1024]{1,0:T(8,128)(2,1)}, bf16[256,1024]{1,0:T(8,128)(2,1)S(1)}, u32[]{:S(2)}, u32[]{:S(2)}) collective-permute-start(bf16[256,1024]{1,0:T(8,128)(2,1)} %bitcast.38), channel_id=1, source_target_pairs={{8,0},{16,8},{24,16},{0,24},{9,1},{17,9},{25,17},{1,25},{10,2},{18... | collective-permute-start | bytes 1572872 | tf_op jit(solution)/shard_map/ppermute | solution.py:23
  8.9 0.7 compare_select_fusion
  9.6 0.6 gather_fusion
  10.1 0.1 compare_reduce_fusion
  10.3 3.4 %slice_bitcast_fusion = bf16[384,3072]{1,0:T(8,128)(2,1)} fusion(bf16[1,512,3072]{2,1,0:T(8,128)(2,1)} %param.11), kind=kLoop, calls=%fused_computation.1 | loop fusion | bytes 4718592 | tf_op jit(solution)/shard_map/slice | solution.py:373
  13.7 2.5 %row_stats.2.refs_6_ = f32[4,8,256]{2,1,0:T(8,128)S(1)} custom-call(s32[1]{0:T(128)S(1)} %bitcast.45, bf16[256,1024]{1,0:T(8,128)(2,1)S(1)} %bitcast.28, bf16[256,1024]{1,0:T(8,128)(2,1)S(1)} %bitcast.31, bf16[256,1024]{1,0:T(8,128)(2,1)S(1)} %bitcast.36, bf16[256,1024]{1,0:T(8,128)(2,1)S(1)} %bitcast.40), custom_call_target="tpu_custom_call" | custom-call | flops 28750000 | bytes 1024 | tf_op jit(solution)/shard_map/row_stats/pallas_call | solution.py:175
  16.2 1.2 slice_bitcast_fusion.1
  17.4 2.2 %collective-permute-start = (bf16[128,3072]{1,0:T(8,128)(2,1)S(1)}, bf16[128,3072]{1,0:T(8,128)(2,1)}, u32[]{:S(2)}, u32[]{:S(2)}) collective-permute-start(bf16[128,3072]{1,0:T(8,128)(2,1)S(1)} %slice_bitcast_fusion.1), channel_id=1, source_target_pairs={{0,8},{8,16},{16,24},{12,4},{20,12},{28,20},{1,9},{9,17},{17,25},{... | collective-permute-start | bytes 2359304 | tf_op jit(solution)/shard_map/ppermute | solution.py:302
  19.6 0.1 slice.47.linked_ref
  19.7 20.5 %collective-permute-done.2.refs_1_.refs_3_ = bf16[256,1024]{1,0:T(8,128)(2,1)S(1)} collective-permute-done((bf16[256,1024]{1,0:T(8,128)(2,1)}, bf16[256,1024]{1,0:T(8,128)(2,1)S(1)}, u32[]{:S(2)}, u32[]{:S(2)}) %collective-permute-start.2) | collective-permute-done | bytes 524320 | tf_op jit(solution)/shard_map/ppermute | solution.py:23
  40.2 12.1 %collective-permute-done.4.refs_3_.refs_5_ = bf16[256,1024]{1,0:T(8,128)(2,1)S(1)} collective-permute-done((bf16[256,1024]{1,0:T(8,128)(2,1)}, bf16[256,1024]{1,0:T(8,128)(2,1)S(1)}, u32[]{:S(2)}, u32[]{:S(2)}) %collective-permute-start.4) | collective-permute-done | bytes 524320 | tf_op jit(solution)/shard_map/ppermute | solution.py:23
  52.3 4.4 %row_stats.3 = (f32[4,8,256]{2,1,0:T(8,128)S(1)}, f32[4,8,256]{2,1,0:T(8,128)S(1)}) custom-call(s32[2]{0:T(128)S(1)} %slice.47.linked_ref, bf16[256,1024]{1,0:T(8,128)(2,1)S(1)} %bitcast.29, bf16[256,1024]{1,0:T(8,128)(2,1)S(1)} %bitcast.32, bf16[256,1024]{1,0:T(8,128)(2,1)S(1)} %collective-permute-done.1.refs_0_.refs_2_, ...), custom_call_target="tpu_custom_call" | custom-call | flops 57500000 | bytes 1024 | tf_op jit(solution)/shard_map/row_stats/pallas_call | solution.py:175
  56.8 0.6 collective-permute-start.5
  57.3 1.5 collective-permute-start.6
  58.8 2.6 %collective-permute-done.5 = f32[2,4,8,256]{3,2,1,0:T(8,128)S(1)} collective-permute-done((f32[2,4,8,256]{3,2,1,0:T(8,128)S(1)}, f32[2,4,8,256]{3,2,1,0:T(8,128)S(1)}, u32[]{:S(2)}, u32[]{:S(2)}) %collective-permute-start.5) | collective-permute-done | bytes 65568 | tf_op jit(solution)/shard_map/ppermute | solution.py:23
  61.5 3.5 %collective-permute-start.10 = (bf16[384,3072]{1,0:T(8,128)(2,1)}, bf16[384,3072]{1,0:T(8,128)(2,1)}, u32[]{:S(2)}, u32[]{:S(2)}) collective-permute-start(bf16[384,3072]{1,0:T(8,128)(2,1)} %slice_bitcast_fusion), channel_id=1, source_target_pairs={{0,8},{8,16},{16,24},{12,4},{20,12},{28,20},{1,9},{9,17},{17,25},{... | collective-permute-start | bytes 7077896 | tf_op jit(solution)/shard_map/ppermute | solution.py:302
  65.1 0.0 collective-permute-done.7
  65.1 14.2 %block_grads.1 = (f32[256,1024]{1,0:T(8,128)}, bf16[256,1024]{1,0:T(8,128)(2,1)}, bf16[256,1024]{1,0:T(8,128)(2,1)}, bf16[2,256,1024]{2,1,0:T(8,128)(2,1)}) custom-call(s32[3]{0:T(128)S(1)} %convert_element_type.13.linked_ref, bf16[256,1024]{1,0:T(8,128)(2,1)S(1)} %bitcast.30, bf16[256,1024]{1,0:T(8,128)(2,1)S(1)} %bitcast.33, ...), custom_call_target="tpu_custom_call" | custom-call | flops 165600002048 | bytes 1024 | tf_op jit(solution)/shard_map/block_grads/pallas_call | solution.py:195
  79.3 11.0 %collective-permute-done.10.refs_4_ = bf16[384,3072]{1,0:T(8,128)(2,1)} collective-permute-done((bf16[384,3072]{1,0:T(8,128)(2,1)}, bf16[384,3072]{1,0:T(8,128)(2,1)}, u32[]{:S(2)}, u32[]{:S(2)}) %collective-permute-start.10) | collective-permute-done | bytes 2359328 | tf_op jit(solution)/shard_map/ppermute | solution.py:302
  90.3 6.5 %collective-permute-start.9 = (bf16[256,1024]{1,0:T(8,128)(2,1)}, bf16[256,1024]{1,0:T(8,128)(2,1)}, u32[]{:S(2)}, u32[]{:S(2)}) collective-permute-start(bf16[256,1024]{1,0:T(8,128)(2,1)} %get-tuple-element.32), channel_id=1, source_target_pairs={{8,0},{16,8},{24,16},{0,24},{9,1},{17,9},{25,17},{1,25},{10,2},{18... | collective-permute-start | bytes 1572872 | tf_op jit(solution)/shard_map/ppermute | solution.py:23
  96.8 0.2 collective-permute-start.11
  97.0 12.4 %collective-permute-done.9 = bf16[256,1024]{1,0:T(8,128)(2,1)} collective-permute-done((bf16[256,1024]{1,0:T(8,128)(2,1)}, bf16[256,1024]{1,0:T(8,128)(2,1)}, u32[]{:S(2)}, u32[]{:S(2)}) %collective-permute-start.9) | collective-permute-done | bytes 524320 | tf_op jit(solution)/shard_map/ppermute | solution.py:23
  109.4 1.3 collective-permute-start.15
  110.8 1.5 slice.64
  112.3 0.9 collective-permute-start.16
  113.2 1.2 slice.65
  114.4 1.4 pad_maximum_fusion
  115.8 5.4 %collective-permute-done.8 = bf16[256,1024]{1,0:T(8,128)(2,1)} collective-permute-done((bf16[256,1024]{1,0:T(8,128)(2,1)}, bf16[256,1024]{1,0:T(8,128)(2,1)}, u32[]{:S(2)}, u32[]{:S(2)}) %collective-permute-start.8) | collective-permute-done | bytes 524320 | tf_op jit(solution)/shard_map/ppermute | solution.py:23
  121.2 0.8 collective-permute-start.19
  122.0 1.5 add_convert_fusion.refs_0_
  123.5 7.7 %project.3 = bf16[256,1536]{1,0:T(8,128)(2,1)S(1)} custom-call(s32[1]{0:T(128)} %bitcast.flag_ref, bf16[256,1024]{1,0:T(8,128)(2,1)S(1)} %add_convert_fusion.refs_0_, bf16[2,256,1024]{2,1,0:T(8,128)(2,1)S(1)} %copy-done.6, bf16[512,3072]{1,0:T(8,128)(2,1)S(1)} %bitcast.27, bf16[128,3072]{1,0:T(8,128)(2,1)} %collective-permute-done.refs_3_, ...), custom_call_target="tpu_custom_call" | custom-call | flops 8215600128 | bytes 1024 | tf_op jit(solution)/shard_map/project/pallas_call | solution.py:280
  131.2 2.5 %collective-permute-start.13 = (bf16[256,1536]{1,0:T(8,128)(2,1)S(1)}, bf16[256,1536]{1,0:T(8,128)(2,1)S(1)}, u32[]{:S(2)}, u32[]{:S(2)}) collective-permute-start(bf16[256,1536]{1,0:T(8,128)(2,1)S(1)} %project.3), channel_id=1, source_target_pairs={{0,3},{1,0},{2,1},{3,2},{8,11},{9,8},{10,9},{11,10},{16,19},{17,16... | collective-permute-start | bytes 2359304 | tf_op jit(solution)/shard_map/ppermute | solution.py:401
  133.7 4.5 %collective-permute-start.14 = (bf16[256,1024]{1,0:T(8,128)(2,1)S(1)}, bf16[256,1024]{1,0:T(8,128)(2,1)S(1)}, u32[]{:S(2)}, u32[]{:S(2)}) collective-permute-start(bf16[256,1024]{1,0:T(8,128)(2,1)S(1)} %add_convert_fusion.refs_0_), channel_id=1, source_target_pairs={{0,8},{24,16},{1,9},{25,17},{2,10},{26,18},{3,11},{27,19},{4,12},{... | collective-permute-start | bytes 1572872 | tf_op jit(solution)/shard_map/ppermute | solution.py:392
  138.2 0.1 collective-permute-start.17
  138.3 15.6 %collective-permute-done.14.refs_2_ = bf16[256,1024]{1,0:T(8,128)(2,1)S(1)} collective-permute-done((bf16[256,1024]{1,0:T(8,128)(2,1)S(1)}, bf16[256,1024]{1,0:T(8,128)(2,1)S(1)}, u32[]{:S(2)}, u32[]{:S(2)}) %collective-permute-start.14) | collective-permute-done | bytes 524320 | tf_op jit(solution)/shard_map/ppermute | solution.py:392
  153.9 0.6 collective-permute-start.20
  154.5 1.0 project.4
  155.5 2.5 %collective-permute-start.18 = (bf16[256,256]{1,0:T(8,128)(2,1)S(1)}, bf16[256,256]{1,0:T(8,128)(2,1)S(1)}, u32[]{:S(2)}, u32[]{:S(2)}) collective-permute-start(bf16[256,256]{1,0:T(8,128)(2,1)S(1)} %get-tuple-element.41), channel_id=1, source_target_pairs={{0,3},{1,0},{2,1},{3,2},{8,11},{9,8},{10,9},{11,10},{16,19},{17,16... | collective-permute-start | bytes 393224 | tf_op jit(solution)/shard_map/ppermute | solution.py:401
  158.0 1.3 collective-permute-start.22
  159.3 1.0 project.5
  160.4 0.7 collective-permute-start.21
  161.1 1.3 collective-permute-start.23
  162.4 3.7 %collective-permute-done.22.refs_2_ = bf16[256,256]{1,0:T(8,128)(2,1)S(1)} collective-permute-done((bf16[256,256]{1,0:T(8,128)(2,1)S(1)}, bf16[256,256]{1,0:T(8,128)(2,1)S(1)}, u32[]{:S(2)}, u32[]{:S(2)}) %collective-permute-start.22) | collective-permute-done | bytes 131104 | tf_op jit(solution)/shard_map/ppermute | solution.py:401
  166.0 5.1 %collective-permute-done.21.refs_1_ = bf16[256,256]{1,0:T(8,128)(2,1)S(1)} collective-permute-done((bf16[256,256]{1,0:T(8,128)(2,1)S(1)}, bf16[256,256]{1,0:T(8,128)(2,1)S(1)}, u32[]{:S(2)}, u32[]{:S(2)}) %collective-permute-start.21) | collective-permute-done | bytes 131104 | tf_op jit(solution)/shard_map/ppermute | solution.py:401
  171.2 0.6 copy-done.11
  171.8 0.7 copy-done.12
  172.5 2.4 %placed.1 = bf16[256,2048]{1,0:T(8,128)(2,1)} custom-call(bf16[256,1536]{1,0:T(8,128)(2,1)} %copy-done.8, bf16[256,256]{1,0:T(8,128)(2,1)} %copy-done.9, bf16[256,256]{1,0:T(8,128)(2,1)} %copy-done.11, bf16[256,256]{1,0:T(8,128)(2,1)} %copy-done.10, bf16[256,256]{1,0:T(8,128)(2,1)} %copy-done.12), custom_call_target="tpu_custom_call" | custom-call | tf_op jit(solution)/shard_map/placed/pallas_call | solution.py:422
  (49 shorter events, 0.2 us)
Async XLA Ops:
  0.0 9.6 %copy-start = (s32[4,3]{1,0:T(4,128)S(1)}, s32[4,3]{1,0:T(4,128)}, u32[]{:S(2)}) copy-start(s32[4,3]{1,0:T(4,128)} %param.12) | copy-start | bytes 148
  0.0 19.7 %collective-permute-start.1 = (bf16[256,1024]{1,0:T(8,128)(2,1)}, bf16[256,1024]{1,0:T(8,128)(2,1)S(1)}, u32[]{:S(2)}, u32[]{:S(2)}) collective-permute-start(bf16[256,1024]{1,0:T(8,128)(2,1)} %bitcast.34), channel_id=1, source_target_pairs={{8,0},{16,8},{24,16},{0,24},{9,1},{17,9},{25,17},{1,25},{10,2},{18... | collective-permute-start | bytes 1572872 | tf_op jit(solution)/shard_map/ppermute | solution.py:23
  5.1 35.2 %collective-permute-start.3 = (bf16[256,1024]{1,0:T(8,128)(2,1)}, bf16[256,1024]{1,0:T(8,128)(2,1)S(1)}, u32[]{:S(2)}, u32[]{:S(2)}) collective-permute-start(bf16[256,1024]{1,0:T(8,128)(2,1)} %bitcast.35), channel_id=1, source_target_pairs={{24,0},{0,8},{8,16},{16,24},{25,1},{1,9},{9,17},{17,25},{26,2},{2,... | collective-permute-start | bytes 1572872 | tf_op jit(solution)/shard_map/ppermute | solution.py:23
  5.1 35.2 %collective-permute-start.2 = (bf16[256,1024]{1,0:T(8,128)(2,1)}, bf16[256,1024]{1,0:T(8,128)(2,1)S(1)}, u32[]{:S(2)}, u32[]{:S(2)}) collective-permute-start(bf16[256,1024]{1,0:T(8,128)(2,1)} %bitcast.38), channel_id=1, source_target_pairs={{8,0},{16,8},{24,16},{0,24},{9,1},{17,9},{25,17},{1,25},{10,2},{18... | collective-permute-start | bytes 1572872 | tf_op jit(solution)/shard_map/ppermute | solution.py:23
  8.9 43.4 %collective-permute-start.4 = (bf16[256,1024]{1,0:T(8,128)(2,1)}, bf16[256,1024]{1,0:T(8,128)(2,1)S(1)}, u32[]{:S(2)}, u32[]{:S(2)}) collective-permute-start(bf16[256,1024]{1,0:T(8,128)(2,1)} %bitcast.39), channel_id=1, source_target_pairs={{24,0},{0,8},{8,16},{16,24},{25,1},{1,9},{9,17},{17,25},{26,2},{2,... | collective-permute-start | bytes 1572872 | tf_op jit(solution)/shard_map/ppermute | solution.py:23
  10.3 3.4 %copy-start.2 = (bf16[1,1,1,256,1024]{4,3,2,1,0:T(8,128)(2,1)S(1)}, bf16[1,1,1,256,1024]{4,3,2,1,0:T(8,128)(2,1)}, u32[]{:S(2)}) copy-start(bf16[1,1,1,256,1024]{4,3,2,1,0:T(8,128)(2,1)} %param.8) | copy-start | bytes 1572868
  10.3 3.4 %copy-start.3 = (bf16[1,1,1,256,1024]{4,3,2,1,0:T(8,128)(2,1)S(1)}, bf16[1,1,1,256,1024]{4,3,2,1,0:T(8,128)(2,1)}, u32[]{:S(2)}) copy-start(bf16[1,1,1,256,1024]{4,3,2,1,0:T(8,128)(2,1)} %param.9) | copy-start | bytes 1572868
  10.3 3.4 %copy-start.4 = (bf16[1,1,1,256,1024]{4,3,2,1,0:T(8,128)(2,1)S(1)}, bf16[1,1,1,256,1024]{4,3,2,1,0:T(8,128)(2,1)}, u32[]{:S(2)}) copy-start(bf16[1,1,1,256,1024]{4,3,2,1,0:T(8,128)(2,1)} %param.7) | copy-start | bytes 1572868
  10.3 3.4 %copy-start.5 = (bf16[1,1,1,256,1024]{4,3,2,1,0:T(8,128)(2,1)S(1)}, bf16[1,1,1,256,1024]{4,3,2,1,0:T(8,128)(2,1)}, u32[]{:S(2)}) copy-start(bf16[1,1,1,256,1024]{4,3,2,1,0:T(8,128)(2,1)} %param.10) | copy-start | bytes 1572868
  17.4 47.6 %collective-permute-start = (bf16[128,3072]{1,0:T(8,128)(2,1)S(1)}, bf16[128,3072]{1,0:T(8,128)(2,1)}, u32[]{:S(2)}, u32[]{:S(2)}) collective-permute-start(bf16[128,3072]{1,0:T(8,128)(2,1)S(1)} %slice_bitcast_fusion.1), channel_id=1, source_target_pairs={{0,8},{8,16},{16,24},{12,4},{20,12},{28,20},{1,9},{9,17},{17,25},{... | collective-permute-start | bytes 2359304 | tf_op jit(solution)/shard_map/ppermute | solution.py:302
  56.8 4.7 %collective-permute-start.5 = (f32[2,4,8,256]{3,2,1,0:T(8,128)S(1)}, f32[2,4,8,256]{3,2,1,0:T(8,128)S(1)}, u32[]{:S(2)}, u32[]{:S(2)}) collective-permute-start(f32[2,4,8,256]{3,2,1,0:T(8,128)S(1)} %get-tuple-element.55), channel_id=1, source_target_pairs={{8,0},{16,8},{24,16},{0,24},{9,1},{17,9},{25,17},{1,25},{10,2},{18... | collective-permute-start | bytes 196616 | tf_op jit(solution)/shard_map/ppermute | solution.py:23
  57.3 7.7 %collective-permute-start.6 = (f32[2,4,8,256]{3,2,1,0:T(8,128)S(1)}, f32[2,4,8,256]{3,2,1,0:T(8,128)S(1)}, u32[]{:S(2)}, u32[]{:S(2)}) collective-permute-start(f32[2,4,8,256]{3,2,1,0:T(8,128)S(1)} %get-tuple-element.54), channel_id=1, source_target_pairs={{24,0},{0,8},{8,16},{16,24},{25,1},{1,9},{9,17},{17,25},{26,2},{2,... | collective-permute-start | bytes 196616 | tf_op jit(solution)/shard_map/ppermute | solution.py:23
  58.8 6.2 %collective-permute-start.7 = (f32[2,4,8,256]{3,2,1,0:T(8,128)S(1)}, f32[2,4,8,256]{3,2,1,0:T(8,128)S(1)}, u32[]{:S(2)}, u32[]{:S(2)}) collective-permute-start(f32[2,4,8,256]{3,2,1,0:T(8,128)S(1)} %get-tuple-element.53), channel_id=1, source_target_pairs={{16,0},{24,8},{0,16},{8,24},{17,1},{25,9},{1,17},{9,25},{18,2},{26... | collective-permute-start | bytes 196616 | tf_op jit(solution)/shard_map/ppermute | solution.py:23
  61.5 28.8 %collective-permute-start.10 = (bf16[384,3072]{1,0:T(8,128)(2,1)}, bf16[384,3072]{1,0:T(8,128)(2,1)}, u32[]{:S(2)}, u32[]{:S(2)}) collective-permute-start(bf16[384,3072]{1,0:T(8,128)(2,1)} %slice_bitcast_fusion), channel_id=1, source_target_pairs={{0,8},{8,16},{16,24},{12,4},{20,12},{28,20},{1,9},{9,17},{17,25},{... | collective-permute-start | bytes 7077896 | tf_op jit(solution)/shard_map/ppermute | solution.py:302
  90.3 33.2 %collective-permute-start.12 = (bf16[384,3072]{1,0:T(8,128)(2,1)}, bf16[384,3072]{1,0:T(8,128)(2,1)S(1)}, u32[]{:S(2)}, u32[]{:S(2)}) collective-permute-start(bf16[384,3072]{1,0:T(8,128)(2,1)} %collective-permute-done.10.refs_4_), channel_id=1, source_target_pairs={{0,4},{4,0},{1,5},{5,1},{2,6},{6,2},{3,7},{7,3},{8,12},{12,8},{9,1... | collective-permute-start | bytes 7077896 | tf_op jit(solution)/shard_map/ppermute | solution.py:298
  90.3 19.1 %collective-permute-start.9 = (bf16[256,1024]{1,0:T(8,128)(2,1)}, bf16[256,1024]{1,0:T(8,128)(2,1)}, u32[]{:S(2)}, u32[]{:S(2)}) collective-permute-start(bf16[256,1024]{1,0:T(8,128)(2,1)} %get-tuple-element.32), channel_id=1, source_target_pairs={{8,0},{16,8},{24,16},{0,24},{9,1},{17,9},{25,17},{1,25},{10,2},{18... | collective-permute-start | bytes 1572872 | tf_op jit(solution)/shard_map/ppermute | solution.py:23
  96.8 24.4 %collective-permute-start.8 = (bf16[256,1024]{1,0:T(8,128)(2,1)}, bf16[256,1024]{1,0:T(8,128)(2,1)}, u32[]{:S(2)}, u32[]{:S(2)}) collective-permute-start(bf16[256,1024]{1,0:T(8,128)(2,1)} %get-tuple-element.31), channel_id=1, source_target_pairs={{24,0},{0,8},{8,16},{16,24},{25,1},{1,9},{9,17},{17,25},{26,2},{2,... | collective-permute-start | bytes 1572872 | tf_op jit(solution)/shard_map/ppermute | solution.py:23
  96.8 26.6 %collective-permute-start.11 = (bf16[128,3072]{1,0:T(8,128)(2,1)}, bf16[128,3072]{1,0:T(8,128)(2,1)S(1)}, u32[]{:S(2)}, u32[]{:S(2)}) collective-permute-start(bf16[128,3072]{1,0:T(8,128)(2,1)} %collective-permute-done.refs_3_), channel_id=1, source_target_pairs={{0,4},{4,0},{1,5},{5,1},{2,6},{6,2},{3,7},{7,3},{8,12},{12,8},{9,1... | collective-permute-start | bytes 2359304 | tf_op jit(solution)/shard_map/ppermute | solution.py:298
  109.4 44.5 %collective-permute-start.15 = (bf16[2,256,1024]{2,1,0:T(8,128)(2,1)}, bf16[2,256,1024]{2,1,0:T(8,128)(2,1)S(1)}, u32[]{:S(2)}, u32[]{:S(2)}) collective-permute-start(bf16[2,256,1024]{2,1,0:T(8,128)(2,1)} %get-tuple-element.38.refs_1_), channel_id=1, source_target_pairs={{0,8},{24,16},{1,9},{25,17},{2,10},{26,18},{3,11},{27,19},{4,12},{... | collective-permute-start | bytes 3145736 | tf_op jit(solution)/shard_map/ppermute | solution.py:391
  112.3 9.7 %copy-start.7 = (f32[256,1024]{1,0:T(8,128)S(1)}, f32[256,1024]{1,0:T(8,128)}, u32[]{:S(2)}) copy-start(f32[256,1024]{1,0:T(8,128)} %get-tuple-element.30) | copy-start | bytes 3145732
  112.3 25.9 %collective-permute-start.16 = (bf16[256,3072]{1,0:T(8,128)(2,1)S(1)}, bf16[256,3072]{1,0:T(8,128)(2,1)S(1)}, u32[]{:S(2)}, u32[]{:S(2)}) collective-permute-start(bf16[256,3072]{1,0:T(8,128)(2,1)S(1)} %slice.64), channel_id=1, source_target_pairs={{8,16},{16,24},{20,12},{12,4},{9,17},{17,25},{21,13},{13,5},{10,18... | collective-permute-start | bytes 4718600 | tf_op jit(solution)/shard_map/ppermute | solution.py:302
  114.4 9.1 %copy-start.1 = (bf16[1,512,3072]{2,1,0:T(8,128)(2,1)S(1)}, bf16[1,512,3072]{2,1,0:T(8,128)(2,1)}, u32[]{:S(2)}) copy-start(bf16[1,512,3072]{2,1,0:T(8,128)(2,1)} %param.11) | copy-start | bytes 9437188
  114.4 9.1 %copy-start.6 = (bf16[2,256,1024]{2,1,0:T(8,128)(2,1)S(1)}, bf16[2,256,1024]{2,1,0:T(8,128)(2,1)}, u32[]{:S(2)}) copy-start(bf16[2,256,1024]{2,1,0:T(8,128)(2,1)} %get-tuple-element.38.refs_1_) | copy-start | bytes 3145732
  121.2 32.6 %collective-permute-start.19 = (bf16[256,3072]{1,0:T(8,128)(2,1)S(1)}, bf16[256,3072]{1,0:T(8,128)(2,1)S(1)}, u32[]{:S(2)}, u32[]{:S(2)}) collective-permute-start(bf16[256,3072]{1,0:T(8,128)(2,1)S(1)} %pad_maximum_fusion), channel_id=1, source_target_pairs={{8,16},{16,24},{20,12},{12,4},{9,17},{17,25},{21,13},{13,5},{10,18... | collective-permute-start | bytes 4718600 | tf_op jit(solution)/shard_map/ppermute | solution.py:302
  131.2 22.7 %collective-permute-start.13 = (bf16[256,1536]{1,0:T(8,128)(2,1)S(1)}, bf16[256,1536]{1,0:T(8,128)(2,1)S(1)}, u32[]{:S(2)}, u32[]{:S(2)}) collective-permute-start(bf16[256,1536]{1,0:T(8,128)(2,1)S(1)} %project.3), channel_id=1, source_target_pairs={{0,3},{1,0},{2,1},{3,2},{8,11},{9,8},{10,9},{11,10},{16,19},{17,16... | collective-permute-start | bytes 2359304 | tf_op jit(solution)/shard_map/ppermute | solution.py:401
  133.7 20.2 %collective-permute-start.14 = (bf16[256,1024]{1,0:T(8,128)(2,1)S(1)}, bf16[256,1024]{1,0:T(8,128)(2,1)S(1)}, u32[]{:S(2)}, u32[]{:S(2)}) collective-permute-start(bf16[256,1024]{1,0:T(8,128)(2,1)S(1)} %add_convert_fusion.refs_0_), channel_id=1, source_target_pairs={{0,8},{24,16},{1,9},{25,17},{2,10},{26,18},{3,11},{27,19},{4,12},{... | collective-permute-start | bytes 1572872 | tf_op jit(solution)/shard_map/ppermute | solution.py:392
  138.2 16.3 %collective-permute-start.17 = (bf16[256,3072]{1,0:T(8,128)(2,1)S(1)}, bf16[256,3072]{1,0:T(8,128)(2,1)S(1)}, u32[]{:S(2)}, u32[]{:S(2)}) collective-permute-start(bf16[256,3072]{1,0:T(8,128)(2,1)S(1)} %collective-permute-done.16.refs_4_), channel_id=1, source_target_pairs={{0,4},{4,0},{1,5},{5,1},{2,6},{6,2},{3,7},{7,3},{8,12},{12,8},{9,1... | collective-permute-start | bytes 4718600 | tf_op jit(solution)/shard_map/ppermute | solution.py:298
  153.9 1.6 copy-start.8
  153.9 5.4 %collective-permute-start.20 = (bf16[256,3072]{1,0:T(8,128)(2,1)S(1)}, bf16[256,3072]{1,0:T(8,128)(2,1)S(1)}, u32[]{:S(2)}, u32[]{:S(2)}) collective-permute-start(bf16[256,3072]{1,0:T(8,128)(2,1)S(1)} %collective-permute-done.19.refs_4_), channel_id=1, source_target_pairs={{0,4},{4,0},{1,5},{5,1},{2,6},{6,2},{3,7},{7,3},{8,12},{12,8},{9,1... | collective-permute-start | bytes 4718600 | tf_op jit(solution)/shard_map/ppermute | solution.py:298
  155.5 6.8 %collective-permute-start.18 = (bf16[256,256]{1,0:T(8,128)(2,1)S(1)}, bf16[256,256]{1,0:T(8,128)(2,1)S(1)}, u32[]{:S(2)}, u32[]{:S(2)}) collective-permute-start(bf16[256,256]{1,0:T(8,128)(2,1)S(1)} %get-tuple-element.41), channel_id=1, source_target_pairs={{0,3},{1,0},{2,1},{3,2},{8,11},{9,8},{10,9},{11,10},{16,19},{17,16... | collective-permute-start | bytes 393224 | tf_op jit(solution)/shard_map/ppermute | solution.py:401
  158.0 8.0 %collective-permute-start.22 = (bf16[256,256]{1,0:T(8,128)(2,1)S(1)}, bf16[256,256]{1,0:T(8,128)(2,1)S(1)}, u32[]{:S(2)}, u32[]{:S(2)}) collective-permute-start(bf16[256,256]{1,0:T(8,128)(2,1)S(1)} %get-tuple-element.45), channel_id=1, source_target_pairs={{8,3},{9,0},{10,1},{11,2},{16,27},{17,24},{18,25},{19,26},{12,7},{... | collective-permute-start | bytes 393224 | tf_op jit(solution)/shard_map/ppermute | solution.py:401
  160.4 10.8 %collective-permute-start.21 = (bf16[256,256]{1,0:T(8,128)(2,1)S(1)}, bf16[256,256]{1,0:T(8,128)(2,1)S(1)}, u32[]{:S(2)}, u32[]{:S(2)}) collective-permute-start(bf16[256,256]{1,0:T(8,128)(2,1)S(1)} %get-tuple-element.44), channel_id=1, source_target_pairs={{0,3},{1,0},{2,1},{3,2},{8,11},{9,8},{10,9},{11,10},{16,19},{17,16... | collective-permute-start | bytes 393224 | tf_op jit(solution)/shard_map/ppermute | solution.py:401
  161.1 10.1 %collective-permute-start.23 = (bf16[256,256]{1,0:T(8,128)(2,1)S(1)}, bf16[256,256]{1,0:T(8,128)(2,1)S(1)}, u32[]{:S(2)}, u32[]{:S(2)}) collective-permute-start(bf16[256,256]{1,0:T(8,128)(2,1)S(1)} %get-tuple-element.46), channel_id=1, source_target_pairs={{8,3},{9,0},{10,1},{11,2},{16,27},{17,24},{18,25},{19,26},{12,7},{... | collective-permute-start | bytes 393224 | tf_op jit(solution)/shard_map/ppermute | solution.py:401
  162.4 8.8 %copy-start.9 = (bf16[256,256]{1,0:T(8,128)(2,1)}, bf16[256,256]{1,0:T(8,128)(2,1)S(1)}, u32[]{:S(2)}) copy-start(bf16[256,256]{1,0:T(8,128)(2,1)S(1)} %collective-permute-done.18.refs_0_) | copy-start | bytes 393220
  166.0 5.1 %copy-start.10 = (bf16[256,256]{1,0:T(8,128)(2,1)}, bf16[256,256]{1,0:T(8,128)(2,1)S(1)}, u32[]{:S(2)}) copy-start(bf16[256,256]{1,0:T(8,128)(2,1)S(1)} %collective-permute-done.22.refs_2_) | copy-start | bytes 393220
  171.2 0.7 copy-start.11
  171.8 0.7 copy-start.12
